TPU v7x, 32 devices: a whole 2x2x4 slice. The times are simulated.
32 devices in a mesh: dp: 8 (over z, x), fsdp: 4 (over y, core).
Axes of the slice: x: 2, y: 2, z: 4, core: 2. Of those that a mesh axis runs over, the one named last changes fastest.
Arguments:
- tokens: bfloat16 [32, 128, 2048], P(('dp', 'fsdp')), may hold values from -6 to 6
- patches: bfloat16 [32, 256, 1664], P(('dp', 'fsdp')), may hold values from -6 to 6
- cotangent: bfloat16 [32, 128, 2048], P(('dp', 'fsdp')), may hold values from -6 to 6
- lengths: int32 [32], P(('dp', 'fsdp')), may hold values from 8 to 128, as said below
- episode_flags: int32 [32], P(('dp', 'fsdp')), may hold values 0 or 1
- norm_gains: float32 [3, 2048], replicated, may hold values from 0.1 to 1.9
- w_query: bfloat16 [2048, 2048], P('fsdp'), may hold values from -0.125 to 0.125
- w_key: bfloat16 [2048, 2048], P('fsdp'), may hold values from -0.125 to 0.125
- w_value: bfloat16 [2048, 2048], P('fsdp'), may hold values from -0.125 to 0.125
- w_out: bfloat16 [2048, 2048], P('fsdp'), may hold values from -0.375 to 0.375
- c_query: bfloat16 [2048, 2048], P('fsdp'), may hold values from -0.125 to 0.125
- c_key: bfloat16 [2048, 2048], P('fsdp'), may hold values from -0.125 to 0.125
- c_value: bfloat16 [2048, 2048], P('fsdp'), may hold values from -0.125 to 0.125
- c_out: bfloat16 [2048, 2048], P('fsdp'), may hold values from -0.5 to 0.5
- patch_proj: bfloat16 [1664, 2048], P('fsdp'), may hold values from -0.15625 to 0.15625
- w_gate: bfloat16 [5120, 2048], P('fsdp'), may hold values from -0.125 to 0.125
- w_up: bfloat16 [5120, 2048], P('fsdp'), may hold values from -0.125 to 0.125
- w_down: bfloat16 [5120, 2048], P('fsdp'), may hold values from -0.078125 to 0.078125
Outputs:
- out_tokens: bfloat16 [32, 128, 2048], P(('dp', 'fsdp'))
- tokens_grad: float32 [32, 128, 2048], P(('dp', 'fsdp'))
- patches_grad: float32 [32, 256, 1664], P(('dp', 'fsdp'))
- gains_grad: float32 [3, 2048], replicated
- w_query_grad: float32 [2048, 2048], P('fsdp', 'dp')
- w_key_grad: float32 [2048, 2048], P('fsdp', 'dp')
- w_value_grad: float32 [2048, 2048], P('fsdp', 'dp')
- w_out_grad: float32 [2048, 2048], P('fsdp', 'dp')
- c_query_grad: float32 [2048, 2048], P('fsdp', 'dp')
- c_key_grad: float32 [2048, 2048], P('fsdp', 'dp')
- c_value_grad: float32 [2048, 2048], P('fsdp', 'dp')
- c_out_grad: float32 [2048, 2048], P('fsdp', 'dp')
- patch_proj_grad: float32 [1664, 2048], P('fsdp', 'dp')
- w_gate_grad: float32 [5120, 2048], P('fsdp', 'dp')
- w_up_grad: float32 [5120, 2048], P('fsdp', 'dp')
- w_down_grad: float32 [5120, 2048], P('fsdp', 'dp')
Inputs may be any that keep to these rules, and one draw needn't show every extreme that they name: `lengths`: text length of each sequence; some sequence has length 128 and some 128 // 16. `episode_flags`: 1 marks a robot episode (causal attention), 0 a caption pair (its first half of tokens attends both ways).
All inputs are finite; a program needn't handle non-finite values. No bound on the sum of `episode_flags` on one device may be relied on, other than what follows from the above.
Results may differ from a plain program's by a relative error of at most 0.028.
Values may be sent and summed in bfloat16 or wider, within the bound.
No kernel may reach another device: no remote copies, remote signals or barrier semaphores. Data moves between devices by JAX's collectives and lax.ppermute only.
A program may use at most 640 MiB of HBM per device.

v0:
```python
import jax
import jax.numpy as jnp
from jax import lax
from jax.sharding import PartitionSpec as P

H = 16
HD = 128


def shortened(x):
    return jax.tree.map(lambda a: a.astype(jnp.bfloat16) if a.dtype == jnp.float32 else a, x)


def normed(values, gain):
    return values * lax.rsqrt(jnp.mean(values * values, axis=-1, keepdims=True) + 1e-06) * gain


def norm_back(values, gain, grad_normed):
    result, pull = jax.vjp(normed, values, gain)
    return pull(grad_normed)


def gated(gate_value, up_value):
    return jax.nn.gelu(gate_value, approximate=True) * up_value


def mask_tables(lengths, episode_flags, slot_len):
    positions = jnp.arange(slot_len, dtype=jnp.int32)
    bucket_len = jnp.where(
        lengths <= slot_len // 4,
        slot_len // 4,
        jnp.where(lengths <= slot_len // 2, slot_len // 2, slot_len),
    )
    prefix_len = jnp.where(episode_flags == 0, lengths // 2, 0)
    query_pos = positions[None, :, None]
    key_pos = positions[None, None, :]
    allowed = (key_pos < lengths[:, None, None]) & (
        (key_pos <= query_pos) | (key_pos < prefix_len[:, None, None])
    )
    live_rows = (positions[None, :] < bucket_len[:, None]).astype(jnp.float32)[:, :, None]
    return (allowed, live_rows)


def project(rows, matrix):
    return jnp.dot(rows, matrix, preferred_element_type=jnp.float32)


def project_back(rows, matrix):
    return lax.dot_general(
        rows, matrix, (((rows.ndim - 1,), (1,)), ((), ())), preferred_element_type=jnp.float32
    )


def outer_sum(left, right):
    flat_left = left.reshape(-1, left.shape[-1])
    flat_right = right.reshape(-1, right.shape[-1])
    return lax.dot_general(
        flat_left, flat_right, (((0,), (0,)), ((), ())), preferred_element_type=jnp.float32
    )


def by_heads(values):
    return values.reshape(values.shape[0], values.shape[1], H, HD)


def attend_forward(queries, keys, values, allowed):
    scores = jnp.einsum(
        "gqhd,gkhd->ghqk", by_heads(queries), by_heads(keys), preferred_element_type=jnp.float32
    ) * HD ** (-0.5)
    if allowed is not None:
        scores = jnp.where(allowed[:, None], scores, -1e30)
    row_max = jnp.max(scores, axis=-1, keepdims=True)
    weights = jnp.exp(scores - row_max)
    probs = weights / jnp.sum(weights, axis=-1, keepdims=True)
    mixed = jnp.einsum(
        "ghqk,gkhd->gqhd",
        probs.astype(jnp.bfloat16),
        by_heads(values),
        preferred_element_type=jnp.float32,
    )
    return (mixed.reshape(queries.shape).astype(jnp.bfloat16), probs)


def attend_backward(queries, keys, values, probs, grad_mixed):
    grad_heads = by_heads(grad_mixed)
    grad_probs = jnp.einsum(
        "gqhd,gkhd->ghqk", grad_heads, by_heads(values), preferred_element_type=jnp.float32
    )
    grad_values = jnp.einsum(
        "ghqk,gqhd->gkhd",
        probs.astype(jnp.bfloat16),
        grad_heads,
        preferred_element_type=jnp.float32,
    )
    grad_scores = (
        probs * (grad_probs - jnp.sum(probs * grad_probs, axis=-1, keepdims=True))
    ).astype(jnp.bfloat16)
    grad_queries = jnp.einsum(
        "ghqk,gkhd->gqhd", grad_scores, by_heads(keys), preferred_element_type=jnp.float32
    ) * HD ** (-0.5)
    grad_keys = jnp.einsum(
        "ghqk,gqhd->gkhd", grad_scores, by_heads(queries), preferred_element_type=jnp.float32
    ) * HD ** (-0.5)
    return (
        grad_queries.reshape(queries.shape).astype(jnp.bfloat16),
        grad_keys.reshape(keys.shape).astype(jnp.bfloat16),
        grad_values.reshape(values.shape).astype(jnp.bfloat16),
    )


def hidden_backward(rows, grad_rows, gate_mat, up_mat, down_mat):
    gate_value = project_back(rows, gate_mat)
    up_value = project_back(rows, up_mat)
    hidden_value, pull = jax.vjp(gated, gate_value, up_value)
    hidden = hidden_value.astype(jnp.bfloat16)
    grad_gate, grad_up = pull(project_back(grad_rows, down_mat))
    grad_gate = grad_gate.astype(jnp.bfloat16)
    grad_up = grad_up.astype(jnp.bfloat16)
    grad_input = project(grad_gate, gate_mat) + project(grad_up, up_mat)
    return (grad_input, (grad_gate, grad_up, hidden))


def reduce_grads(terms):
    partial_sums = jax.tree.map(
        lambda part: part.astype(jnp.float32),
        lax.psum_scatter(shortened(terms), "fsdp", scatter_dimension=0, tiled=True),
    )
    return jax.tree.map(
        lambda part: part.astype(jnp.float32),
        lax.psum_scatter(shortened(partial_sums), "dp", scatter_dimension=1, tiled=True),
    )


def block_grads(arrays, pairs):
    return reduce_grads(
        tuple((outer_sum(arrays[left_at], arrays[right_at]) for left_at, right_at in pairs))
    )


def on_device(
    tokens,
    patches,
    cotangent,
    lengths,
    episode_flags,
    norm_gains,
    w_query,
    w_key,
    w_value,
    w_out,
    c_query,
    c_key,
    c_value,
    c_out,
    patch_proj,
    w_gate,
    w_up,
    w_down,
):
    allowed, live_rows = mask_tables(lengths, episode_flags, tokens.shape[1])
    inputs = tokens.astype(jnp.float32)
    flat_shape = (-1, tokens.shape[2])

    def gather_self():
        return (
            lax.all_gather(w_query, "fsdp", axis=0, tiled=True),
            lax.all_gather(w_key, "fsdp", axis=0, tiled=True),
            lax.all_gather(w_value, "fsdp", axis=0, tiled=True),
            lax.all_gather(w_out, "fsdp", axis=0, tiled=True),
        )

    def gather_cross():
        return (
            lax.all_gather(c_query, "fsdp", axis=0, tiled=True),
            lax.all_gather(c_key, "fsdp", axis=0, tiled=True),
            lax.all_gather(c_value, "fsdp", axis=0, tiled=True),
            lax.all_gather(c_out, "fsdp", axis=0, tiled=True),
            lax.all_gather(patch_proj, "fsdp", axis=0, tiled=True),
        )

    def gather_hidden():
        return (
            lax.all_gather(w_gate, "fsdp", axis=0, tiled=True),
            lax.all_gather(w_up, "fsdp", axis=0, tiled=True),
            lax.all_gather(w_down, "fsdp", axis=0, tiled=True),
        )

    def attention_part(self_full, cross_full):
        first = normed(inputs, norm_gains[0]).astype(jnp.bfloat16)
        queries = project(first, self_full[0]).astype(jnp.bfloat16)
        keys = project(first, self_full[1]).astype(jnp.bfloat16)
        values = project(first, self_full[2]).astype(jnp.bfloat16)
        self_mixed, self_probs = attend_forward(queries, keys, values, allowed)
        after_self = inputs + project(self_mixed, self_full[3])
        second = normed(after_self, norm_gains[1]).astype(jnp.bfloat16)
        cross_queries = project(second, cross_full[0]).astype(jnp.bfloat16)
        context = project(patches, cross_full[4]).astype(jnp.bfloat16)
        cross_keys = project(context, cross_full[1]).astype(jnp.bfloat16)
        cross_values = project(context, cross_full[2]).astype(jnp.bfloat16)
        cross_mixed, cross_probs = attend_forward(cross_queries, cross_keys, cross_values, None)
        after_cross = after_self + project(cross_mixed, cross_full[3])
        third = normed(after_cross, norm_gains[2]).astype(jnp.bfloat16)
        return (
            first,
            queries,
            keys,
            values,
            self_mixed,
            self_probs,
            after_self,
            second,
            cross_queries,
            context,
            cross_keys,
            cross_values,
            cross_mixed,
            cross_probs,
            after_cross,
            third,
        )

    forward_state = attention_part(gather_self(), gather_cross())
    third_rows = forward_state[15].reshape(flat_shape)
    mlp_full = gather_hidden()
    hidden = gated(
        project_back(third_rows, mlp_full[0]), project_back(third_rows, mlp_full[1])
    ).astype(jnp.bfloat16)
    branch_out = project(hidden, mlp_full[2])
    out_tokens = ((forward_state[14] + branch_out.reshape(tokens.shape)) * live_rows).astype(
        jnp.bfloat16
    )
    self_full = gather_self()
    cross_full = gather_cross()
    (
        first,
        queries,
        keys,
        values,
        self_mixed,
        self_probs,
        after_self,
        second,
        cross_queries,
        context,
        cross_keys,
        cross_values,
        cross_mixed,
        cross_probs,
        after_cross,
        third,
    ) = attention_part(self_full, cross_full)
    grad_out = (cotangent.astype(jnp.float32) * live_rows).astype(jnp.bfloat16)
    third_rows = third.reshape(flat_shape)
    grad_rows = grad_out.reshape(flat_shape)
    mlp_full = gather_hidden()
    grad_third, parts = hidden_backward(
        third_rows, grad_rows, mlp_full[0], mlp_full[1], mlp_full[2]
    )
    grads = block_grads(
        (parts[0], parts[1], parts[2], third_rows, grad_rows), ((0, 3), (1, 3), (2, 4))
    )
    grad_cross_norm, gain_third = norm_back(
        after_cross, norm_gains[2], grad_third.reshape(tokens.shape)
    )
    grad_after_cross = grad_out.astype(jnp.float32) + grad_cross_norm
    grad_cross_out = grad_after_cross.astype(jnp.bfloat16)
    grad_cross_mixed = project_back(grad_cross_out, cross_full[3]).astype(jnp.bfloat16)
    grad_cq, grad_ck, grad_cv = attend_backward(
        cross_queries, cross_keys, cross_values, cross_probs, grad_cross_mixed
    )
    grad_context = (
        project_back(grad_ck, cross_full[1]) + project_back(grad_cv, cross_full[2])
    ).astype(jnp.bfloat16)
    patches_grad = project_back(grad_context, cross_full[4])
    cross_grads = block_grads(
        (
            second,
            grad_cq,
            context,
            grad_ck,
            grad_cv,
            cross_mixed,
            grad_cross_out,
            patches,
            grad_context,
        ),
        ((0, 1), (2, 3), (2, 4), (5, 6), (7, 8)),
    )
    grad_self_norm, gain_second = norm_back(
        after_self, norm_gains[1], project_back(grad_cq, cross_full[0])
    )
    grad_after_self = grad_after_cross + grad_self_norm
    grad_self_out = grad_after_self.astype(jnp.bfloat16)
    grad_self_mixed = project_back(grad_self_out, self_full[3]).astype(jnp.bfloat16)
    grad_queries, grad_keys, grad_values = attend_backward(
        queries, keys, values, self_probs, grad_self_mixed
    )
    grad_first = (
        project_back(grad_queries, self_full[0])
        + project_back(grad_keys, self_full[1])
        + project_back(grad_values, self_full[2])
    )
    self_grads = block_grads(
        (first, grad_queries, grad_keys, grad_values, self_mixed, grad_self_out),
        ((0, 1), (0, 2), (0, 3), (4, 5)),
    )
    grad_input_norm, gain_first = norm_back(inputs, norm_gains[0], grad_first)
    tokens_grad = grad_after_self + grad_input_norm
    gains_grad = lax.psum(jnp.stack([gain_first, gain_second, gain_third]), ("dp", "fsdp"))
    return (
        (out_tokens, tokens_grad, patches_grad, gains_grad)
        + tuple(self_grads)
        + tuple(cross_grads)
        + tuple(grads)
    )


def solution(mesh):
    in_specs = (
        P(("dp", "fsdp"), None, None),
        P(("dp", "fsdp"), None, None),
        P(("dp", "fsdp"), None, None),
        P(("dp", "fsdp")),
        P(("dp", "fsdp")),
        P(),
        P("fsdp", None),
        P("fsdp", None),
        P("fsdp", None),
        P("fsdp", None),
        P("fsdp", None),
        P("fsdp", None),
        P("fsdp", None),
        P("fsdp", None),
        P("fsdp", None),
        P("fsdp", None),
        P("fsdp", None),
        P("fsdp", None),
    )
    out_specs = (
        P(("dp", "fsdp"), None, None),
        P(("dp", "fsdp"), None, None),
        P(("dp", "fsdp"), None, None),
        P(),
        P("fsdp", "dp"),
        P("fsdp", "dp"),
        P("fsdp", "dp"),
        P("fsdp", "dp"),
        P("fsdp", "dp"),
        P("fsdp", "dp"),
        P("fsdp", "dp"),
        P("fsdp", "dp"),
        P("fsdp", "dp"),
        P("fsdp", "dp"),
        P("fsdp", "dp"),
        P("fsdp", "dp"),
    )
    return jax.shard_map(
        on_device, mesh=mesh, in_specs=in_specs, out_specs=out_specs, check_vma=False
    )
```

profile of v0, /device:TPU:4, one launch (start us, length us, event | category | flops | bytes accessed | tf_op | source)
XLA Modules:
  0.0 3092.1 jit_solution(12355770528214428879)
XLA Ops:
  64.0 54.9 %all-gather.15.cloned.1.call-done = bf16[2048,2048]{1,0:T(8,128)(2,1)} async-done(((bf16[512,2048]{1,0:T(8,128)(2,1)}), bf16[2048,2048]{1,0:T(8,128)(2,1)}) %all-gather.15.cloned.1.call-update) | async-done | bytes 8388624 | tf_op jit(solution)/shard_map/all_gather | solution.py:166
  124.6 54.2 %all-gather.17.cloned.1.call-done = bf16[2048,2048]{1,0:T(8,128)(2,1)} async-done(((bf16[512,2048]{1,0:T(8,128)(2,1)}), bf16[2048,2048]{1,0:T(8,128)(2,1)}) %all-gather.17.cloned.1.call-update) | async-done | bytes 8388624 | tf_op jit(solution)/shard_map/all_gather | solution.py:167
  184.5 54.0 %all-gather.27.cloned.1.call-done = bf16[2048,2048]{1,0:T(8,128)(2,1)} async-done(((bf16[512,2048]{1,0:T(8,128)(2,1)}), bf16[2048,2048]{1,0:T(8,128)(2,1)}) %all-gather.27.cloned.1.call-update) | async-done | bytes 8388624 | tf_op jit(solution)/shard_map/all_gather | solution.py:175
  250.3 48.0 %all-gather.13.cloned.1.call-done = bf16[2048,2048]{1,0:T(8,128)(2,1)} async-done(((bf16[512,2048]{1,0:T(8,128)(2,1)}), bf16[2048,2048]{1,0:T(8,128)(2,1)}) %all-gather.13.cloned.1.call-update) | async-done | bytes 8388624 | tf_op jit(solution)/shard_map/all_gather | solution.py:168
  306.1 51.9 %all-gather.19.cloned.1.call-done = bf16[2048,2048]{1,0:T(8,128)(2,1)} async-done(((bf16[512,2048]{1,0:T(8,128)(2,1)}), bf16[2048,2048]{1,0:T(8,128)(2,1)}) %all-gather.19.cloned.1.call-update) | async-done | bytes 8388624 | tf_op jit(solution)/shard_map/all_gather | solution.py:169
  362.9 54.9 %all-gather.25.cloned.1.call-done = bf16[2048,2048]{1,0:T(8,128)(2,1)} async-done(((bf16[512,2048]{1,0:T(8,128)(2,1)}), bf16[2048,2048]{1,0:T(8,128)(2,1)}) %all-gather.25.cloned.1.call-update) | async-done | bytes 8388624 | tf_op jit(solution)/shard_map/all_gather | solution.py:174
  428.5 49.2 %all-gather.23.cloned.1.call-done = bf16[2048,2048]{1,0:T(8,128)(2,1)} async-done(((bf16[512,2048]{1,0:T(8,128)(2,1)}), bf16[2048,2048]{1,0:T(8,128)(2,1)}) %all-gather.23.cloned.1.call-update) | async-done | bytes 8388624 | tf_op jit(solution)/shard_map/all_gather | solution.py:176
  485.6 52.1 %all-gather.29.cloned.1.call-done = bf16[2048,2048]{1,0:T(8,128)(2,1)} async-done(((bf16[512,2048]{1,0:T(8,128)(2,1)}), bf16[2048,2048]{1,0:T(8,128)(2,1)}) %all-gather.29.cloned.1.call-update) | async-done | bytes 8388624 | tf_op jit(solution)/shard_map/all_gather | solution.py:177
  543.7 127.0 %all-gather.33.cloned.1.call-done = bf16[5120,2048]{1,0:T(8,128)(2,1)} async-done(((bf16[1280,2048]{1,0:T(8,128)(2,1)}), bf16[5120,2048]{1,0:T(8,128)(2,1)}) %all-gather.33.cloned.1.call-update) | async-done | bytes 20971536 | tf_op jit(solution)/shard_map/all_gather | solution.py:184
  683.4 120.5 %all-gather.31.cloned.1.call-done = bf16[5120,2048]{1,0:T(8,128)(2,1)} async-done(((bf16[1280,2048]{1,0:T(8,128)(2,1)}), bf16[5120,2048]{1,0:T(8,128)(2,1)}) %all-gather.31.cloned.1.call-update) | async-done | bytes 20971536 | tf_op jit(solution)/shard_map/all_gather | solution.py:183
  816.2 120.8 %all-gather.35.cloned.1.call-done = bf16[5120,2048]{1,0:T(8,128)(2,1)} async-done(((bf16[1280,2048]{1,0:T(8,128)(2,1)}), bf16[5120,2048]{1,0:T(8,128)(2,1)}) %all-gather.35.cloned.1.call-update) | async-done | bytes 20971536 | tf_op jit(solution)/shard_map/all_gather | solution.py:185
  1138.3 74.1 %reduce-scatter.39.cloned.1.call-done = bf16[512,2048]{1,0:T(8,128)(2,1)} async-done(((bf16[2048,2048]{1,0:T(8,128)(2,1)}), bf16[512,2048]{1,0:T(8,128)(2,1)}) %reduce-scatter.39.cloned.1.call-update) | async-done | bytes 2097168 | tf_op jit(solution)/shard_map/reduce_scatter | solution.py:126
  1212.5 74.3 %reduce-scatter.55.cloned.1.call-done = bf16[512,2048]{1,0:T(8,128)(2,1)} async-done(((bf16[2048,2048]{1,0:T(8,128)(2,1)}), bf16[512,2048]{1,0:T(8,128)(2,1)}) %reduce-scatter.55.cloned.1.call-update) | async-done | bytes 2097168 | tf_op jit(solution)/shard_map/reduce_scatter | solution.py:126
  1286.9 74.1 %reduce-scatter.51.cloned.1.call-done = bf16[512,2048]{1,0:T(8,128)(2,1)} async-done(((bf16[2048,2048]{1,0:T(8,128)(2,1)}), bf16[512,2048]{1,0:T(8,128)(2,1)}) %reduce-scatter.51.cloned.1.call-update) | async-done | bytes 2097168 | tf_op jit(solution)/shard_map/reduce_scatter | solution.py:126
  1361.1 74.3 %reduce-scatter.47.cloned.1.call-done = bf16[512,2048]{1,0:T(8,128)(2,1)} async-done(((bf16[2048,2048]{1,0:T(8,128)(2,1)}), bf16[512,2048]{1,0:T(8,128)(2,1)}) %reduce-scatter.47.cloned.1.call-update) | async-done | bytes 2097168 | tf_op jit(solution)/shard_map/reduce_scatter | solution.py:126
  1435.4 74.3 %reduce-scatter.35.cloned.1.call-done = bf16[512,2048]{1,0:T(8,128)(2,1)} async-done(((bf16[2048,2048]{1,0:T(8,128)(2,1)}), bf16[512,2048]{1,0:T(8,128)(2,1)}) %reduce-scatter.35.cloned.1.call-update) | async-done | bytes 2097168 | tf_op jit(solution)/shard_map/reduce_scatter | solution.py:126
  1509.7 74.3 %reduce-scatter.31.cloned.1.call-done = bf16[512,2048]{1,0:T(8,128)(2,1)} async-done(((bf16[2048,2048]{1,0:T(8,128)(2,1)}), bf16[512,2048]{1,0:T(8,128)(2,1)}) %reduce-scatter.31.cloned.1.call-update) | async-done | bytes 2097168 | tf_op jit(solution)/shard_map/reduce_scatter | solution.py:126
  1584.1 74.3 %reduce-scatter.27.cloned.1.call-done = bf16[512,2048]{1,0:T(8,128)(2,1)} async-done(((bf16[2048,2048]{1,0:T(8,128)(2,1)}), bf16[512,2048]{1,0:T(8,128)(2,1)}) %reduce-scatter.27.cloned.1.call-update) | async-done | bytes 2097168 | tf_op jit(solution)/shard_map/reduce_scatter | solution.py:126
  1658.4 155.9 %reduce-scatter.69.cloned.1.call-done = bf16[1280,2048]{1,0:T(8,128)(2,1)} async-done(((bf16[5120,2048]{1,0:T(8,128)(2,1)}), bf16[1280,2048]{1,0:T(8,128)(2,1)}) %reduce-scatter.69.cloned.1.call-update) | async-done | bytes 5242896 | tf_op jit(solution)/shard_map/reduce_scatter | solution.py:126
  1814.4 155.7 %reduce-scatter.65.cloned.1.call-done = bf16[1280,2048]{1,0:T(8,128)(2,1)} async-done(((bf16[5120,2048]{1,0:T(8,128)(2,1)}), bf16[1280,2048]{1,0:T(8,128)(2,1)}) %reduce-scatter.65.cloned.1.call-update) | async-done | bytes 5242896 | tf_op jit(solution)/shard_map/reduce_scatter | solution.py:126
  1970.4 155.5 %reduce-scatter.61.cloned.1.call-done = bf16[1280,2048]{1,0:T(8,128)(2,1)} async-done(((bf16[5120,2048]{1,0:T(8,128)(2,1)}), bf16[1280,2048]{1,0:T(8,128)(2,1)}) %reduce-scatter.61.cloned.1.call-update) | async-done | bytes 5242896 | tf_op jit(solution)/shard_map/reduce_scatter | solution.py:126
  2205.0 63.9 %reduce-scatter.45.cloned.1.call-done = bf16[512,256]{1,0:T(8,128)(2,1)} async-done(((bf16[512,2048]{1,0:T(8,128)(2,1)}), bf16[512,256]{1,0:T(8,128)(2,1)}) %reduce-scatter.45.cloned.1.call-update) | async-done | bytes 262160 | tf_op jit(solution)/shard_map/reduce_scatter | solution.py:130
  2270.7 69.0 %reduce-scatter.41.cloned.1.call-done = bf16[512,256]{1,0:T(8,128)(2,1)} async-done(((bf16[512,2048]{1,0:T(8,128)(2,1)}), bf16[512,256]{1,0:T(8,128)(2,1)}) %reduce-scatter.41.cloned.1.call-update) | async-done | bytes 262160 | tf_op jit(solution)/shard_map/reduce_scatter | solution.py:130
  2341.5 69.0 %reduce-scatter.57.cloned.1.call-done = bf16[512,256]{1,0:T(8,128)(2,1)} async-done(((bf16[512,2048]{1,0:T(8,128)(2,1)}), bf16[512,256]{1,0:T(8,128)(2,1)}) %reduce-scatter.57.cloned.1.call-update) | async-done | bytes 262160 | tf_op jit(solution)/shard_map/reduce_scatter | solution.py:130
  2412.3 69.1 %reduce-scatter.53.cloned.1.call-done = bf16[512,256]{1,0:T(8,128)(2,1)} async-done(((bf16[512,2048]{1,0:T(8,128)(2,1)}), bf16[512,256]{1,0:T(8,128)(2,1)}) %reduce-scatter.53.cloned.1.call-update) | async-done | bytes 262160 | tf_op jit(solution)/shard_map/reduce_scatter | solution.py:130
  2483.2 68.9 %reduce-scatter.49.cloned.1.call-done = bf16[512,256]{1,0:T(8,128)(2,1)} async-done(((bf16[512,2048]{1,0:T(8,128)(2,1)}), bf16[512,256]{1,0:T(8,128)(2,1)}) %reduce-scatter.49.cloned.1.call-update) | async-done | bytes 262160 | tf_op jit(solution)/shard_map/reduce_scatter | solution.py:130
  2553.9 69.2 %reduce-scatter.37.cloned.1.call-done = bf16[512,256]{1,0:T(8,128)(2,1)} async-done(((bf16[512,2048]{1,0:T(8,128)(2,1)}), bf16[512,256]{1,0:T(8,128)(2,1)}) %reduce-scatter.37.cloned.1.call-update) | async-done | bytes 262160 | tf_op jit(solution)/shard_map/reduce_scatter | solution.py:130
  2624.9 68.8 %reduce-scatter.33.cloned.1.call-done = bf16[512,256]{1,0:T(8,128)(2,1)} async-done(((bf16[512,2048]{1,0:T(8,128)(2,1)}), bf16[512,256]{1,0:T(8,128)(2,1)}) %reduce-scatter.33.cloned.1.call-update) | async-done | bytes 262160 | tf_op jit(solution)/shard_map/reduce_scatter | solution.py:130
  2695.5 68.7 %reduce-scatter.29.cloned.1.call-done = bf16[512,256]{1,0:T(8,128)(2,1)} async-done(((bf16[512,2048]{1,0:T(8,128)(2,1)}), bf16[512,256]{1,0:T(8,128)(2,1)}) %reduce-scatter.29.cloned.1.call-update) | async-done | bytes 262160 | tf_op jit(solution)/shard_map/reduce_scatter | solution.py:130
  2766.0 103.9 %reduce-scatter.71.cloned.1.call-done = bf16[1280,256]{1,0:T(8,128)(2,1)} async-done(((bf16[1280,2048]{1,0:T(8,128)(2,1)}), bf16[1280,256]{1,0:T(8,128)(2,1)}) %reduce-scatter.71.cloned.1.call-update) | async-done | bytes 655376 | tf_op jit(solution)/shard_map/reduce_scatter | solution.py:130
  2872.1 104.3 %reduce-scatter.67.cloned.1.call-done = bf16[1280,256]{1,0:T(8,128)(2,1)} async-done(((bf16[1280,2048]{1,0:T(8,128)(2,1)}), bf16[1280,256]{1,0:T(8,128)(2,1)}) %reduce-scatter.67.cloned.1.call-update) | async-done | bytes 655376 | tf_op jit(solution)/shard_map/reduce_scatter | solution.py:130
  2978.7 104.2 %reduce-scatter.63.cloned.1.call-done = bf16[1280,256]{1,0:T(8,128)(2,1)} async-done(((bf16[1280,2048]{1,0:T(8,128)(2,1)}), bf16[1280,256]{1,0:T(8,128)(2,1)}) %reduce-scatter.63.cloned.1.call-update) | async-done | bytes 655376 | tf_op jit(solution)/shard_map/reduce_scatter | solution.py:130
  (275 shorter events, 442.0 us)
Async XLA Ops:
  9.4 229.1 %all-gather.27.cloned.1.call-start = ((), (), s32[]{:S(2)}) async-start(), calls=%async_computation.31 | async-start | bytes 10485760 | tf_op jit(solution)/shard_map/all_gather | solution.py:175
  10.0 288.3 %all-gather.13.cloned.1.call-start = ((), (), s32[]{:S(2)}) async-start(), calls=%async_computation.24 | async-start | bytes 10485760 | tf_op jit(solution)/shard_map/all_gather | solution.py:168
  10.6 347.4 %all-gather.19.cloned.1.call-start = ((), (), s32[]{:S(2)}) async-start(), calls=%async_computation.27 | async-start | bytes 10485760 | tf_op jit(solution)/shard_map/all_gather | solution.py:169
  11.2 406.7 %all-gather.25.cloned.1.call-start = ((), (), s32[]{:S(2)}) async-start(), calls=%async_computation.30 | async-start | bytes 10485760 | tf_op jit(solution)/shard_map/all_gather | solution.py:174
  11.9 465.9 %all-gather.23.cloned.1.call-start = ((), (), s32[]{:S(2)}) async-start(), calls=%async_computation.29 | async-start | bytes 10485760 | tf_op jit(solution)/shard_map/all_gather | solution.py:176
  12.7 525.0 %all-gather.29.cloned.1.call-start = ((), (), s32[]{:S(2)}) async-start(), calls=%async_computation.32 | async-start | bytes 10485760 | tf_op jit(solution)/shard_map/all_gather | solution.py:177
  13.4 657.3 %all-gather.33.cloned.1.call-start = ((), (), s32[]{:S(2)}) async-start(), calls=%async_computation.34 | async-start | bytes 26214400 | tf_op jit(solution)/shard_map/all_gather | solution.py:184
  14.0 790.0 %all-gather.31.cloned.1.call-start = ((), (), s32[]{:S(2)}) async-start(), calls=%async_computation.33 | async-start | bytes 26214400 | tf_op jit(solution)/shard_map/all_gather | solution.py:183
  14.7 922.3 %all-gather.35.cloned.1.call-start = ((), (), s32[]{:S(2)}) async-start(), calls=%async_computation.35 | async-start | bytes 26214400 | tf_op jit(solution)/shard_map/all_gather | solution.py:185
  15.3 1109.7 %reduce-scatter.73.cloned.1.call-start = ((), (), s32[]{:S(2)}) async-start(), calls=%async_computation.59 | async-start | bytes 8519680
  1013.5 198.9 %reduce-scatter.39.cloned.1.call-start = ((), (), s32[]{:S(2)}) async-start(), calls=%async_computation.42 | async-start | bytes 10485760 | tf_op jit(solution)/shard_map/reduce_scatter | solution.py:126
  1028.3 258.5 %reduce-scatter.55.cloned.1.call-start = ((), (), s32[]{:S(2)}) async-start(), calls=%async_computation.50 | async-start | bytes 10485760 | tf_op jit(solution)/shard_map/reduce_scatter | solution.py:126
  1034.9 326.1 %reduce-scatter.51.cloned.1.call-start = ((), (), s32[]{:S(2)}) async-start(), calls=%async_computation.48 | async-start | bytes 10485760 | tf_op jit(solution)/shard_map/reduce_scatter | solution.py:126
  1042.1 393.2 %reduce-scatter.47.cloned.1.call-start = ((), (), s32[]{:S(2)}) async-start(), calls=%async_computation.46 | async-start | bytes 10485760 | tf_op jit(solution)/shard_map/reduce_scatter | solution.py:126
  1049.0 460.6 %reduce-scatter.35.cloned.1.call-start = ((), (), s32[]{:S(2)}) async-start(), calls=%async_computation.40 | async-start | bytes 10485760 | tf_op jit(solution)/shard_map/reduce_scatter | solution.py:126
  1064.8 519.2 %reduce-scatter.31.cloned.1.call-start = ((), (), s32[]{:S(2)}) async-start(), calls=%async_computation.38 | async-start | bytes 10485760 | tf_op jit(solution)/shard_map/reduce_scatter | solution.py:126
  1078.4 579.9 %reduce-scatter.27.cloned.1.call-start = ((), (), s32[]{:S(2)}) async-start(), calls=%async_computation.36 | async-start | bytes 10485760 | tf_op jit(solution)/shard_map/reduce_scatter | solution.py:126
  1088.0 726.3 %reduce-scatter.69.cloned.1.call-start = ((), (), s32[]{:S(2)}) async-start(), calls=%async_computation.57 | async-start | bytes 26214400 | tf_op jit(solution)/shard_map/reduce_scatter | solution.py:126
  1100.7 869.4 %reduce-scatter.65.cloned.1.call-start = ((), (), s32[]{:S(2)}) async-start(), calls=%async_computation.55 | async-start | bytes 26214400 | tf_op jit(solution)/shard_map/reduce_scatter | solution.py:126
  1113.3 1012.5 %reduce-scatter.61.cloned.1.call-start = ((), (), s32[]{:S(2)}) async-start(), calls=%async_computation.53 | async-start | bytes 26214400 | tf_op jit(solution)/shard_map/reduce_scatter | solution.py:126
  1124.9 1078.3 %reduce-scatter.59.cloned.1.call-start = ((), (), s32[]{:S(2)}) async-start(), calls=%async_computation.52 | async-start | bytes 2359296 | tf_op jit(solution)/shard_map/reduce_scatter | solution.py:130
  1128.8 1140.1 %reduce-scatter.45.cloned.1.call-start = ((), (), s32[]{:S(2)}) async-start(), calls=%async_computation.45 | async-start | bytes 2359296 | tf_op jit(solution)/shard_map/reduce_scatter | solution.py:130
  1138.3 1201.4 %reduce-scatter.41.cloned.1.call-start = ((), (), s32[]{:S(2)}) async-start(), calls=%async_computation.43 | async-start | bytes 2359296 | tf_op jit(solution)/shard_map/reduce_scatter | solution.py:130
  1212.5 1198.1 %reduce-scatter.57.cloned.1.call-start = ((), (), s32[]{:S(2)}) async-start(), calls=%async_computation.51 | async-start | bytes 2359296 | tf_op jit(solution)/shard_map/reduce_scatter | solution.py:130
  1286.8 1194.6 %reduce-scatter.53.cloned.1.call-start = ((), (), s32[]{:S(2)}) async-start(), calls=%async_computation.49 | async-start | bytes 2359296 | tf_op jit(solution)/shard_map/reduce_scatter | solution.py:130
  1361.0 1191.1 %reduce-scatter.49.cloned.1.call-start = ((), (), s32[]{:S(2)}) async-start(), calls=%async_computation.47 | async-start | bytes 2359296 | tf_op jit(solution)/shard_map/reduce_scatter | solution.py:130
  1435.4 1187.7 %reduce-scatter.37.cloned.1.call-start = ((), (), s32[]{:S(2)}) async-start(), calls=%async_computation.41 | async-start | bytes 2359296 | tf_op jit(solution)/shard_map/reduce_scatter | solution.py:130
  1509.7 1184.0 %reduce-scatter.33.cloned.1.call-start = ((), (), s32[]{:S(2)}) async-start(), calls=%async_computation.39 | async-start | bytes 2359296 | tf_op jit(solution)/shard_map/reduce_scatter | solution.py:130
  1584.0 1180.1 %reduce-scatter.29.cloned.1.call-start = ((), (), s32[]{:S(2)}) async-start(), calls=%async_computation.37 | async-start | bytes 2359296 | tf_op jit(solution)/shard_map/reduce_scatter | solution.py:130
  1658.4 1211.5 %reduce-scatter.71.cloned.1.call-start = ((), (), s32[]{:S(2)}) async-start(), calls=%async_computation.58 | async-start | bytes 5898240 | tf_op jit(solution)/shard_map/reduce_scatter | solution.py:130
  1814.3 1162.1 %reduce-scatter.67.cloned.1.call-start = ((), (), s32[]{:S(2)}) async-start(), calls=%async_computation.56 | async-start | bytes 5898240 | tf_op jit(solution)/shard_map/reduce_scatter | solution.py:130
  1970.1 1112.8 %reduce-scatter.63.cloned.1.call-start = ((), (), s32[]{:S(2)}) async-start(), calls=%async_computation.54 | async-start | bytes 5898240 | tf_op jit(solution)/shard_map/reduce_scatter | solution.py:130
  (56 other events, 2402.1 us)
Sparse Core Ops, SparseCore 0:
  60.6 58.2 all-gather.14
  120.5 58.2 all-gather.16
  180.2 58.2 all-gather.26
  239.9 58.2 all-gather.12
  299.7 58.2 all-gather.18
  539.1 131.6 all-gather.32
  672.3 131.6 all-gather.30
  805.4 131.6 all-gather.34
  1001.9 61.9 reduce-scatter.72
  1066.5 71.6 reduce-scatter.42
  1140.7 71.7 reduce-scatter.38
  1215.0 71.7 reduce-scatter.54
  1289.2 71.7 reduce-scatter.50
  1363.6 71.6 reduce-scatter.46
  1437.9 71.7 reduce-scatter.34
  1512.3 71.6 reduce-scatter.30
  1586.6 71.7 reduce-scatter.26
  1661.1 153.1 reduce-scatter.68
  1816.9 153.1 reduce-scatter.64
  1972.7 153.1 reduce-scatter.60
  2129.4 68.9 reduce-scatter.58
  2201.8 67.1 reduce-scatter.44
  2272.3 67.3 reduce-scatter.40
  2343.2 67.2 reduce-scatter.56
  2414.1 67.3 reduce-scatter.52
  2484.8 67.2 reduce-scatter.48
  2555.7 67.3 reduce-scatter.36
  2626.6 67.0 reduce-scatter.32
  2697.1 67.0 reduce-scatter.28
  2767.8 102.0 reduce-scatter.70
  2873.5 102.9 reduce-scatter.66
  2979.9 102.9 reduce-scatter.62
  (4 shorter events, 224.0 us)
where the time goes:
time: 3100 us; the launch traced here: 3090 us
  waiting for transfers between devices  2690 us (87%)
  matrix products  271 us (9%)
  blocking collectives  42.4 us (1%)
  local copies, waits for them, and re-layouts  39.6 us (1%)
    reduce_scatter x11, waiting for transfers between devices, reduce_grads(): lax.psum_scatter(shortened(terms), 'fsdp', scatter_dimension=0, tiled=True)  996 us
    reduce_scatter x12, waiting for transfers between devices, reduce_grads(): lax.psum_scatter(shortened(partial_sums), 'dp', scatter_dimension=1, tile...  859 us
    all_gather x1, waiting for transfers between devices, gather_hidden(): lax.all_gather(w_up, 'fsdp', axis=0, tiled=True)  127 us
    all_gather x1, waiting for transfers between devices, gather_hidden(): lax.all_gather(w_down, 'fsdp', axis=0, tiled=True)  121 us
    all_gather x1, waiting for transfers between devices, gather_hidden(): lax.all_gather(w_gate, 'fsdp', axis=0, tiled=True)  121 us
    dot_general x12, matrix products, outer_sum(): lax.dot_general(flat_left, flat_right, (((0,), (0,)), ((), ())), preferre...  87.7 us
    dot_general x12, matrix products, project_back(): lax.dot_general(rows, matrix, (((rows.ndim - 1,), (1,)), ((), ())), prefe...  84 us
    dot_general x12, matrix products, project(): return jnp.dot(rows, matrix, preferred_element_type=jnp.float32)  77.5 us
  transfers between devices with their start and end apart: 36, of which 34 were waited for; matrix products, arithmetic and copies ran while one was open for 8% of the time, Pallas kernels for 0%

commit v1 on v0

v1 whole, which is shorter than its diff:
```python
import functools

import jax
import jax.numpy as jnp
from jax import lax
from jax.experimental import pallas as pl
from jax.experimental.pallas import tpu as pltpu
from jax.sharding import PartitionSpec as P

HD = 128
SCALE = HD ** (-0.5)
EPS = 1e-06
BF = jnp.bfloat16
F32 = jnp.float32
GROUP = 4


def cost(us):
    return pl.CostEstimate(
        flops=int(us * 8e8), bytes_accessed=int(us * 2e6), transcendentals=0
    )


def low(v):
    return v.astype(BF)


def dot(left, right, left_dim, right_dim):
    return lax.dot_general(
        left, right, (((left_dim,), (right_dim,)), ((), ())), preferred_element_type=F32
    )


def nn(left, right):
    return dot(left, right, 1, 0)


def nt(left, right):
    return dot(left, right, 1, 1)


def tn(left, right):
    return dot(left, right, 0, 0)


def normed(values, gain):
    return low(values * lax.rsqrt(jnp.mean(values * values, axis=-1, keepdims=True) + EPS) * gain)


def norm_back(values, gain, grad):
    scale = lax.rsqrt(jnp.mean(values * values, axis=-1, keepdims=True) + EPS)
    unit = values * scale
    weighted = grad * gain
    grad_values = scale * (weighted - unit * jnp.mean(weighted * unit, axis=-1, keepdims=True))
    return grad_values, jnp.sum(grad * unit, axis=0)


def gelu_parts(v):
    c = 0.7978845608028654
    t = jnp.tanh(c * (v + 0.044715 * (v * v * v)))
    value = 0.5 * v * (1.0 + t)
    slope = 0.5 * (1.0 + t) + 0.5 * v * (1.0 - t * t) * (c * (1.0 + 3 * 0.044715 * v * v))
    return value, slope


def allowed_at(info, rows, columns):
    length = info[pl.program_id(0), 0]
    flag = info[pl.program_id(0), 1]
    prefix = jnp.where(flag == 0, length // 2, 0)
    query = lax.broadcasted_iota(jnp.int32, (rows, columns), 0)
    key = lax.broadcasted_iota(jnp.int32, (rows, columns), 1)
    return (key < length) & ((key <= query) | (key < prefix))


def probabilities(q, k, allowed):
    scores = nt(q, k) * SCALE
    if allowed is not None:
        scores = jnp.where(allowed, scores, -1e30)
    weights = jnp.exp(scores - jnp.max(scores, axis=-1, keepdims=True))
    return weights / jnp.sum(weights, axis=-1, keepdims=True)


def attend_kernel(masked, info, q_ref, k_ref, v_ref, out_ref):
    allowed = allowed_at(info, q_ref.shape[0], k_ref.shape[0]) if masked else None
    for head in range(q_ref.shape[1] // HD):
        at = pl.ds(head * HD, HD)
        probs = probabilities(q_ref[:, at], k_ref[:, at], allowed)
        out_ref[:, at] = low(nn(low(probs), v_ref[:, at]))


def attend_back_kernel(masked, info, q_ref, k_ref, v_ref, g_ref, gq_ref, gk_ref, gv_ref):
    allowed = allowed_at(info, q_ref.shape[0], k_ref.shape[0]) if masked else None
    for head in range(q_ref.shape[1] // HD):
        at = pl.ds(head * HD, HD)
        q, k, v, g = q_ref[:, at], k_ref[:, at], v_ref[:, at], g_ref[:, at]
        probs = probabilities(q, k, allowed)
        grad_probs = nt(g, v)
        gv_ref[:, at] = low(tn(low(probs), g))
        total = jnp.sum(probs * grad_probs, axis=-1, keepdims=True)
        grad_scores = low(probs * (grad_probs - total))
        gq_ref[:, at] = low(nn(grad_scores, k) * SCALE)
        gk_ref[:, at] = low(tn(grad_scores, q) * SCALE)


def head_block(rows, width):
    return pl.BlockSpec((rows, width), lambda s, info: (s, 0))


def attend(info, q, k, v, rows, keys, width, masked):
    return pl.pallas_call(
        functools.partial(attend_kernel, masked),
        out_shape=jax.ShapeDtypeStruct((GROUP * rows, width), BF),
        grid_spec=pltpu.PrefetchScalarGridSpec(
            num_scalar_prefetch=1,
            grid=(GROUP,),
            in_specs=[
                head_block(rows, width),
                head_block(keys, width),
                head_block(keys, width),
            ],
            out_specs=head_block(rows, width),
        ),
        compiler_params=pltpu.CompilerParams(vmem_limit_bytes=24 << 20),
        cost_estimate=cost(6 if masked else 4),
    )(info, q, k, v)


def attend_back(info, q, k, v, grad, rows, keys, width, masked):
    return pl.pallas_call(
        functools.partial(attend_back_kernel, masked),
        out_shape=(
            jax.ShapeDtypeStruct((GROUP * rows, width), BF),
            jax.ShapeDtypeStruct((GROUP * keys, width), BF),
            jax.ShapeDtypeStruct((GROUP * keys, width), BF),
        ),
        grid_spec=pltpu.PrefetchScalarGridSpec(
            num_scalar_prefetch=1,
            grid=(GROUP,),
            in_specs=[
                head_block(rows, width),
                head_block(keys, width),
                head_block(keys, width),
                head_block(rows, width),
            ],
            out_specs=(
                head_block(rows, width),
                head_block(keys, width),
                head_block(keys, width),
            ),
        ),
        compiler_params=pltpu.CompilerParams(vmem_limit_bytes=24 << 20),
        cost_estimate=cost(8),
    )(info, q, k, v, grad)


def placed(place, pieces):
    rows = pieces[0].shape[0]
    half = rows // 2
    f, x = place[0], place[1] % 2

    def at(block, part):
        return pl.multiple_of((f ^ block) * rows + part * half, half)

    spots = (
        pl.ds(at(0, 0), rows),
        pl.ds(at(1, 0), rows),
        pl.ds(at(2, x), half),
        pl.ds(at(2, 1 - x), half),
        pl.ds(at(3, x), half),
        pl.ds(at(3, 1 - x), half),
    )
    return tuple(zip(pieces, spots))


def row_tiles(rows, body):
    size = next((size for size in (512, 640) if rows % size == 0), rows)
    if size == rows:
        body(pl.ds(0, rows))
    else:
        pl.loop(0, rows // size)(lambda i: body(pl.ds(pl.multiple_of(i * size, size), size)))


def to_heads_kernel(count, place, *refs):
    pieces, out_ref = placed(place, refs[count : count + 6]), refs[count + 6]
    start = 0
    for rows_ref in refs[:count]:
        total = None
        for piece, features in pieces:
            term = nn(rows_ref[:, features], piece[...])
            total = term if total is None else total + term
        out_ref[pl.ds(start, rows_ref.shape[0]), :] = low(total)
        start += rows_ref.shape[0]


def from_heads_kernel(count, place, *refs):
    grads, pieces, out_ref = refs[:count], refs[count:-1], refs[-1]

    def tile(at):
        for part in range(6):
            total = None
            for i in range(count):
                piece, features = placed(place, pieces[6 * i : 6 * i + 6])[part]
                term = nt(grads[i][at, :], piece[...])
                total = term if total is None else total + term
            out_ref[at, features] = low(total)

    row_tiles(out_ref.shape[0], tile)


def piece_specs(pieces):
    rows, width = pieces[0].shape[0], pieces[1][0].shape[-1]
    specs = [pl.BlockSpec((rows, width), lambda i, place: (0, place[0]))]
    for array, at in pieces[1:]:
        block = (None,) * len(at) + array.shape[len(at) :]
        specs.append(pl.BlockSpec(block, lambda i, place, at=at: (*at, 0, 0)))
    return specs


def piece_arrays(pieces):
    return [pieces[0]] + [array for array, at in pieces[1:]]


def fixed(array):
    return pl.BlockSpec(array.shape, lambda i, place: (0, 0))


def to_heads(place, blocks, pieces):
    out = (sum(block.shape[0] for block in blocks), pieces[1][0].shape[-1])
    return pl.pallas_call(
        functools.partial(to_heads_kernel, len(blocks)),
        out_shape=jax.ShapeDtypeStruct(out, BF),
        grid_spec=pltpu.PrefetchScalarGridSpec(
            num_scalar_prefetch=1,
            grid=(1,),
            in_specs=[fixed(block) for block in blocks] + piece_specs(pieces),
            out_specs=pl.BlockSpec(out, lambda i, place: (0, 0)),
        ),
        compiler_params=pltpu.CompilerParams(vmem_limit_bytes=48 << 20),
        cost_estimate=cost(out[0] / 190),
    )(place, *blocks, *piece_arrays(pieces))


def from_heads(place, grads, weights):
    count = len(weights)
    out = (grads[0].shape[0], weights[0][0].shape[1])
    specs = [spec for pieces in weights for spec in piece_specs(pieces)]
    return pl.pallas_call(
        functools.partial(from_heads_kernel, count),
        out_shape=jax.ShapeDtypeStruct(out, BF),
        grid_spec=pltpu.PrefetchScalarGridSpec(
            num_scalar_prefetch=1,
            grid=(1,),
            in_specs=[fixed(g) for g in grads] + specs,
            out_specs=pl.BlockSpec(out, lambda i, place: (0, 0)),
        ),
        compiler_params=pltpu.CompilerParams(vmem_limit_bytes=56 << 20),
        cost_estimate=cost(3 + out[0] * count / 230),
    )(place, *grads, *[array for pieces in weights for array in piece_arrays(pieces)])


def half_kernel(place, *refs):
    lefts, rights, out_ref = refs[0:-1:2], refs[1:-1:2], refs[-1]
    start = 0
    for left, right in zip(lefts, rights):

        def product(at, start=start, left=left, right=right):
            out_ref[0, pl.ds(pl.multiple_of(start + at.start, 16), at.size), :] = low(
                nn(left[at, :], right[...])
            )

        row_tiles(left.shape[0], product)
        start += left.shape[0]


def half_grads(place, terms, order, side):
    def target(k, place):
        rel = (side << order[0]) + ((k // 2) << order[1]) + ((k % 2) << order[2])
        return place[1] ^ rel

    def source(k, place):
        return (target(k, place) // 2) ^ place[0]

    specs, arrays = [], []
    rows = 0
    for kind, left, right in terms:
        tall, tokens = left.shape[-2:]
        if kind == "columns":
            tall, wide = tall // GROUP, right.shape[1] // 2
            specs.append(pl.BlockSpec((tall, tokens), lambda k, place: (target(k, place) // 2, 0)))
            specs.append(pl.BlockSpec((tokens, wide), lambda k, place: (0, target(k, place) % 2)))
        elif kind == "owners":
            right, column = right
            wide = left.shape[-2] // 2
            specs.append(
                pl.BlockSpec((None, tall, tokens), lambda k, place: (source(k, place), 0, 0))
            )
            specs.append(
                pl.BlockSpec(
                    (None, tokens, wide),
                    lambda k, place, column=column: (
                        source(k, place),
                        0,
                        2 * column + target(k, place) % 2,
                    ),
                )
            )
        else:
            wide = right.shape[1] // 8
            specs.append(pl.BlockSpec((tall, tokens), lambda k, place: (0, 0)))
            specs.append(pl.BlockSpec((tokens, wide), lambda k, place: (0, target(k, place))))
        arrays += [left, right]
        rows += tall
    return pl.pallas_call(
        half_kernel,
        out_shape=jax.ShapeDtypeStruct((4, rows, wide), BF),
        grid_spec=pltpu.PrefetchScalarGridSpec(
            num_scalar_prefetch=1,
            grid=(4,),
            in_specs=specs,
            out_specs=pl.BlockSpec((1, rows, wide), lambda k, place: (k, 0, 0)),
        ),
        compiler_params=pltpu.CompilerParams(vmem_limit_bytes=48 << 20),
        cost_estimate=cost(rows / 210),
    )(place, *arrays)


def turn_kernel(*refs):
    start = 0
    for block in refs[:-1]:
        rows = block.shape[0]
        refs[-1][:, pl.ds(start, rows)] = block[...].T
        start += rows


def turn(*blocks):
    width = blocks[0].shape[1]
    step = 512 if width % 512 == 0 else width
    rows = sum(block.shape[0] for block in blocks)
    return pl.pallas_call(
        turn_kernel,
        out_shape=jax.ShapeDtypeStruct((width, rows), BF),
        grid=(width // step,),
        in_specs=[pl.BlockSpec((block.shape[0], step), lambda i: (0, i)) for block in blocks],
        out_specs=pl.BlockSpec((step, rows), lambda i: (i, 0)),
        compiler_params=pltpu.CompilerParams(vmem_limit_bytes=32 << 20),
        cost_estimate=cost(3),
    )(*blocks)


def turn_own_kernel(place, *refs):
    blocks, out_ref = refs[:-1], refs[-1]
    rows = blocks[0].shape[0]
    for k, block in enumerate(blocks):
        turned = block[...].T
        for r in range(GROUP):
            out_ref[r, :, pl.ds((k ^ r) * rows, rows)] = turned


def turn_own(place, blocks, width):
    rows = blocks[0].shape[0]
    out = (GROUP, width, GROUP * rows)
    return pl.pallas_call(
        turn_own_kernel,
        out_shape=jax.ShapeDtypeStruct(out, BF),
        grid_spec=pltpu.PrefetchScalarGridSpec(
            num_scalar_prefetch=1,
            grid=(1,),
            in_specs=[pl.BlockSpec((rows, width), lambda i, place: (0, place[0]))] * GROUP,
            out_specs=pl.BlockSpec(out, lambda i, place: (0, 0, 0)),
        ),
        compiler_params=pltpu.CompilerParams(vmem_limit_bytes=32 << 20),
        cost_estimate=cost(3),
    )(place, *blocks)


def join_kernel(place, *refs):
    for r, block in enumerate(refs[:-1]):

        @pl.when(pl.program_id(0) == r)
        def _():
            refs[-1][...] = block[...]


def join(place, blocks):
    rows, width = blocks[0].shape
    return pl.pallas_call(
        join_kernel,
        out_shape=jax.ShapeDtypeStruct((GROUP * rows, width), BF),
        grid_spec=pltpu.PrefetchScalarGridSpec(
            num_scalar_prefetch=1,
            grid=(GROUP,),
            in_specs=[fixed(block) for block in blocks],
            out_specs=pl.BlockSpec((rows, width), lambda i, place: (place[0] ^ i, 0)),
        ),
        compiler_params=pltpu.CompilerParams(vmem_limit_bytes=40 << 20),
        cost_estimate=cost(5),
    )(place, *blocks)


def all_grads(parts, terms):
    rows = sum(left.shape[0] for left, right in terms)
    wide = terms[0][1].shape[1] // parts
    specs = []
    for left, right in terms:
        specs.append(pl.BlockSpec(left.shape, lambda p, place: (0, 0)))
        specs.append(pl.BlockSpec((right.shape[0], wide), lambda p, place: (0, p)))
    return pl.pallas_call(
        half_kernel,
        out_shape=jax.ShapeDtypeStruct((parts, rows, wide), BF),
        grid_spec=pltpu.PrefetchScalarGridSpec(
            num_scalar_prefetch=1,
            grid=(parts,),
            in_specs=specs,
            out_specs=pl.BlockSpec((1, rows, wide), lambda p, place: (p, 0, 0)),
        ),
        compiler_params=pltpu.CompilerParams(vmem_limit_bytes=48 << 20),
        cost_estimate=cost(18),
    )(jnp.zeros((2,), jnp.int32), *[array for term in terms for array in term])


def after(values, *earlier):
    return lax.optimization_barrier((values, *earlier))[0]


def wide_sum(*terms):
    total = terms[0].astype(F32)
    for term in terms[1:]:
        total = total + term.astype(F32)
    return total


def solution(mesh):
    dp, fsdp = mesh.shape["dp"], mesh.shape["fsdp"]
    assert fsdp == GROUP and dp % GROUP == 0
    inner = dp // GROUP

    def swap(values, r):
        return lax.ppermute(values, "fsdp", [(i, i ^ r) for i in range(fsdp)])

    def across(values):
        return lax.ppermute(values, "dp", [(i, i ^ 1) for i in range(dp)])

    def gather_blocks(values, chip=None):
        chip = swap(values, 2) if chip is None else chip
        return values, swap(values, 1), chip, swap(chip, 1)

    def gather_rows(values, chip=None):
        return jnp.concatenate(gather_blocks(values, chip), axis=0)

    def core_sum(terms):
        blocks = terms.reshape((GROUP, -1) + terms.shape[1:])
        got = swap(low(blocks[1::2]), 1)
        return wide_sum(blocks[0], got[0]), low(wide_sum(blocks[2], got[1]))

    def scatter_sum(terms):
        own, other = core_sum(terms)
        return own + swap(other, 2).astype(F32)

    def gather_plane(values, near=None):
        half = values.shape[0] // 2
        chip, side = near or (swap(values, 2), across(values))
        far = jnp.concatenate([across(chip[:half]), swap(side[half:], 2)], axis=0)
        blocks = [values, chip, side, far]
        mates = [swap(block, 1) for block in blocks]
        return jnp.concatenate([b for pair in zip(blocks, mates) for b in pair], axis=0)

    def plane_core(terms):
        blocks = terms.reshape((2 * GROUP, -1) + terms.shape[1:])
        got = swap(low(blocks[1::2]), 1)
        return [wide_sum(blocks[2 * i], got[i]) for i in range(GROUP)]

    def plane_far(sums):
        own, chip, side, far = sums
        half = far.shape[0] // 2
        top, bottom = across(low(far[:half])), swap(low(far[half:]), 2)
        chip = jnp.concatenate([wide_sum(chip[:half], top), chip[half:]], axis=0)
        side = jnp.concatenate([side[:half], wide_sum(side[half:], bottom)], axis=0)
        return own, low(chip), low(side)

    def plane_near(sums):
        own, chip, side = sums
        return own, swap(chip, 2), across(side)

    def pick(bit, low_part, high_part, axis):
        return jnp.where(
            bit == 0,
            jnp.concatenate([low_part, high_part], axis=axis),
            jnp.concatenate([high_part, low_part], axis=axis),
        )

    def sent_parts(weights, f, place, parts):
        rows, width = weights[0].shape[0], weights[0].shape[1] // GROUP
        size = rows // parts

        def part(weight, r):
            return lax.dynamic_slice(weight, (place * size, (f ^ r) * width), (size, width))

        return jnp.stack([jnp.stack([part(weight, 2), part(weight, 3)]) for weight in weights])

    def mate_parts(weights, f):
        rows, width = weights[0].shape[0], weights[0].shape[1] // GROUP
        sent = [lax.dynamic_slice(w, (0, (f ^ 1) * width), (rows, width)) for w in weights]
        return swap(jnp.stack(sent), 1)

    def head_pieces(weights, near, far, mate, mate_at=0):
        near_mate, far_mate = swap(near[:, 1], 1), swap(far[:, 1], 1)
        return [
            (
                weight,
                (mate, (i + mate_at,)),
                (near, (i, 0)),
                (far, (i, 0)),
                (near_mate, (i,)),
                (far_mate, (i,)),
            )
            for i, weight in enumerate(weights)
        ]

    def plain_sum(terms):
        parts = []
        for kind, left, right in terms:
            if kind == "owners":
                f = lax.axis_index("fsdp")
                size = left.shape[-2]
                right = right[0][:, :, right[1] * size : (right[1] + 1) * size]
                part = jnp.einsum("srt,stc->src", left, right, preferred_element_type=F32)
                part = jnp.take(part, f ^ jnp.arange(GROUP), axis=0)
                part = part.reshape(GROUP, size, inner, -1).transpose(0, 2, 1, 3)
                parts.append(low(part).reshape((dp, size, -1)))
            elif kind == "columns":
                tall = left.reshape(GROUP, -1, left.shape[1])
                wide = right.reshape(right.shape[0], inner, -1)
                part = jnp.einsum("zrt,txc->zxrc", tall, wide, preferred_element_type=F32)
                parts.append(low(part).reshape((dp,) + part.shape[2:]))
            else:
                wide = right.reshape(right.shape[0], dp, -1)
                parts.append(low(jnp.einsum("rt,tpc->prc", left, wide, preferred_element_type=F32)))
        grads = jnp.concatenate(parts, axis=1)
        return lax.psum_scatter(grads, "dp", scatter_dimension=0).astype(F32)

    def hop(values, bit):
        return lax.ppermute(values, "dp", [(i, i ^ (1 << bit)) for i in range(dp)])

    class Sum:
        def __init__(self, place, terms, order):
            self.place, self.terms, self.order = place, terms, order

        def send(self):
            if dp == 8:
                self.sent = half_grads(self.place, self.terms, self.order, 1)
            else:
                self.sent = self.total = plain_sum(self.terms)
            return self.sent

        def keep(self, *earlier):
            if dp == 8:
                first = after(self.terms[0][1], *earlier)
                terms = ((self.terms[0][0], first, self.terms[0][2]),) + self.terms[1:]
                self.kept = half_grads(self.place, terms, self.order, 0)
                return self.kept
            return self.sent

        def add(self, stage, *earlier):
            if dp != 8:
                return self.sent
            if stage == 1:
                self.one = after(hop(self.sent, self.order[0]), *earlier)
                self.sent = low(wide_sum(self.kept[2:], self.one[2:]))
                return self.sent
            if stage == 2:
                self.two = after(hop(self.sent, self.order[1]), *earlier)
                self.sent = low(wide_sum(self.kept[1], self.one[1], self.two[1]))
                return self.sent
            three = after(hop(self.sent, self.order[2]), *earlier)
            self.total = wide_sum(self.kept[0], self.one[0], self.two[0], three)
            return self.total

        def parts(self):
            out, at = [], 0
            for kind, left, right in self.terms:
                rows = left.shape[0] // GROUP if kind == "columns" else left.shape[-2]
                out.append(self.total[at : at + rows])
                at += rows
            return out

    def place_columns(values):
        pairs = []
        for z in range(GROUP):
            for x in range(inner):
                for f in range(GROUP):
                    pairs.append(((z * inner + x) * GROUP + f, (f * inner + x) * GROUP + z))
        return lax.ppermute(values, ("dp", "fsdp"), pairs)

    def on_device(
        tokens,
        patches,
        cotangent,
        lengths,
        episode_flags,
        norm_gains,
        w_query,
        w_key,
        w_value,
        w_out,
        c_query,
        c_key,
        c_value,
        c_out,
        patch_proj,
        w_gate,
        w_up,
        w_down,
    ):
        f = lax.axis_index("fsdp")
        x = lax.axis_index("dp") % 2
        z = (lax.axis_index("dp") // 2) % 2
        place = jnp.stack([f, lax.axis_index("dp")]).astype(jnp.int32)
        slot = tokens.shape[1]
        keys = patches.shape[1]
        width = tokens.shape[2] // GROUP
        inputs = tokens[0].astype(F32)
        bucket = jnp.where(
            lengths[0] <= slot // 4,
            slot // 4,
            jnp.where(lengths[0] <= slot // 2, slot // 2, slot),
        )
        live = (jnp.arange(slot, dtype=jnp.int32) < bucket).astype(F32)[:, None]
        grad_out = low(cotangent[0].astype(F32) * live)
        info = jnp.stack([lengths, episode_flags], axis=1)
        chip_info = swap(info, 2)
        w_query, w_key, w_value, inputs, chip_info = lax.optimization_barrier(
            (w_query, w_key, w_value, inputs, chip_info)
        )
        pair_near = swap(sent_parts((w_query, w_key), f, x, 2), 2)
        value_near = swap(sent_parts((w_value,), f, x, 2), 2)
        first = normed(inputs, norm_gains[0])
        first_chip = swap(first, 2)
        pair_far = across(pair_near)
        value_far = across(after(value_near, pair_far))

        rows = patch_proj.shape[0] // 4
        patch_in = after(patch_proj, pair_near, value_near)
        patch_mate = swap(patch_in, 1)
        patch_part = swap(lax.dynamic_slice_in_dim(patch_in, (2 * x + z) * rows, rows, 0), 2)
        patch_half = pick(z, patch_part, hop(patch_part, 1), 0)
        patch_chip = pick(x, patch_half, across(patch_half), 0)
        patch_far = swap(patch_chip, 1)
        cross_own = (c_key, c_value, c_query)
        cross_part = swap(sent_parts(after(cross_own, patch_part), f, 2 * x + z, 4), 2)
        cross_near = pick(z, cross_part, hop(cross_part, 1), 2)
        cross_far = across(cross_near)
        self_mate = mate_parts((w_query, w_key, w_value), f)
        first_blocks = gather_blocks(first, after(first_chip, pair_far))
        info = jnp.concatenate([info, swap(info, 1), chip_info, swap(chip_info, 1)], axis=0)
        query_w, key_w = head_pieces((w_query, w_key), pair_near, pair_far, self_mate)
        (value_w,) = head_pieces((w_value,), value_near, value_far, self_mate, 2)
        queries = to_heads(place, first_blocks, query_w)
        keys_all = to_heads(place, first_blocks, key_w)
        values_all = to_heads(place, first_blocks, value_w)
        mixed = attend(info, queries, keys_all, values_all, slot, slot, width, True)
        own, other = core_sum(low(nn(after(mixed, cross_near, patch_half), w_out)))
        cross_mate = mate_parts(after(cross_own, other), f)
        sent_out = other
        other = swap(other, 2)
        after_self = inputs + own + other.astype(F32)
        second = normed(after_self, norm_gains[1])
        second_chip = swap(second, 2)
        patch_blocks = (patch_proj, patch_mate, patch_chip, patch_far)
        patch_mat = join(place, after(patch_blocks, sent_out))
        context = low(nn(after(patches[0], second), patch_mat))
        context_chip = swap(context, 2)
        second_chip, cross_far = lax.optimization_barrier((second_chip, cross_far))
        second_blocks = gather_blocks(second, second_chip)
        cross_key_w, cross_value_w, cross_query_w = head_pieces(
            cross_own, cross_near, cross_far, cross_mate
        )
        cross_q = to_heads(place, second_blocks, cross_query_w)
        context_blocks = gather_blocks(context, after(context_chip, cross_q))
        cross_k = to_heads(place, context_blocks, cross_key_w)
        cross_v = to_heads(place, context_blocks, cross_value_w)
        grad_early = after(grad_out, context)
        cross_v, *grad_near = lax.optimization_barrier(
            (cross_v, swap(grad_early, 2), across(grad_early))
        )
        cross_mixed = attend(info, cross_q, cross_k, cross_v, slot, keys, width, False)
        own, other = core_sum(low(nn(cross_mixed, c_out)))
        grad_all = gather_plane(grad_out, after(tuple(grad_near), other))
        other = after(swap(other, 2), grad_all)
        after_cross = after_self + own + other.astype(F32)
        third = normed(after_cross, norm_gains[2])
        third_all = gather_plane(third)
        patch_width = patch_proj.shape[0]
        patch_rows = after(patches[0], third_all)

        def patch_piece(r):
            return lax.dynamic_slice(patch_rows, (0, (f ^ r) * patch_width), (keys, patch_width))

        patch_pieces = [patch_piece(0)] + [swap(patch_piece(r), r) for r in range(1, GROUP)]

        units = w_gate.shape[0] // 2
        gate_half, up_half, down_half = (
            lax.dynamic_slice_in_dim(w, x * units, units, 0) for w in (w_gate, w_up, w_down)
        )
        gate = nt(third_all, gate_half)
        up = nt(third_all, up_half)
        value, slope = gelu_parts(gate)
        hidden = low(value * up)
        grad_hidden = nt(grad_all, down_half)
        grad_gate = low(grad_hidden * up * slope)
        grad_up = low(grad_hidden * value)
        grad_gate, *patch_pieces = lax.optimization_barrier((grad_gate, *patch_pieces))
        third_part = low(nn(grad_gate, gate_half) + nn(grad_up, up_half))
        sums = plane_far(plane_core(third_part))
        hidden_terms = tuple(
            (turn(after(left, third_part)), right)
            for left, right in ((grad_gate, third_all), (grad_up, third_all), (hidden, grad_all))
        )
        first_left = after(hidden_terms[0][0], sums[1], sums[2])
        hidden_terms = ((first_left, third_all),) + hidden_terms[1:]
        hidden_bundle = all_grads(dp // 2, hidden_terms)
        hidden_grads = lax.psum_scatter(
            hidden_bundle,
            "dp",
            scatter_dimension=0,
            axis_index_groups=[list(range(i, dp, 2)) for i in range(2)],
        )
        own, chip, side = plane_near(sums)
        grad_third = wide_sum(own, after(chip, hidden_bundle), side)

        grad_norm, gain_third = norm_back(after_cross, norm_gains[2], grad_third)
        grad_after_cross = grad_out.astype(F32) + grad_norm
        grad_cross_out = low(grad_after_cross)
        cross_turned = turn(after(cross_mixed, grad_third))
        second_turned = turn(*after(second_blocks, grad_third))
        grad_cross_all = gather_rows(
            grad_cross_out, after(swap(grad_cross_out, 2), cross_turned, second_turned)
        )
        grad_cross_mixed = low(nt(grad_cross_all, c_out))
        grad_cq, grad_ck, grad_cv = attend_back(
            info, cross_q, cross_k, cross_v, grad_cross_mixed, slot, keys, width, False
        )
        own, other = core_sum(from_heads(place, (grad_cq,), (cross_query_w,)))
        context_turned = turn(*after(context_blocks, grad_cq))
        sum_cross = Sum(
            place,
            (("rows", cross_turned, grad_cross_all), ("columns", second_turned, grad_cq)),
            (0, 1, 2),
        )
        grad_second = own + after(swap(other, 2), sum_cross.send(), context_turned).astype(F32)

        grad_norm, gain_second = norm_back(after_self, norm_gains[1], grad_second)
        grad_after_self = grad_after_cross + grad_norm
        grad_self_out = low(grad_after_self)
        self_chip = swap(grad_self_out, 2)
        mixed_turned = turn(after(mixed, grad_self_out))
        first_turned = turn_own(place, after(first_blocks, grad_self_out), width)
        grad_self_all = gather_rows(
            grad_self_out,
            after(self_chip, mixed_turned, first_turned, sum_cross.keep(grad_self_out)),
        )
        grad_mixed = low(nt(grad_self_all, w_out))
        grad_q, grad_k, grad_v = attend_back(
            info, queries, keys_all, values_all, grad_mixed, slot, slot, width, True
        )
        heads = jnp.concatenate([grad_q, grad_k, grad_v], axis=1)
        heads_chip = swap(heads, 2)
        cross_one = sum_cross.add(1, grad_q)
        own, other = core_sum(
            from_heads(place, (after(grad_q, cross_one), grad_k, grad_v), (query_w, key_w, value_w))
        )
        other = swap(other, 2)
        sum_context = Sum(
            place,
            (
                ("columns", context_turned, grad_ck),
                ("columns", context_turned, grad_cv),
                ("rows", mixed_turned, grad_self_all),
            ),
            (0, 1, 2),
        )
        context_part = from_heads(
            place, (after(grad_ck, heads_chip), grad_cv), (cross_key_w, cross_value_w)
        )
        grad_first = own + after(
            other, sum_context.send(), context_part, hidden_grads, heads_chip
        ).astype(F32)
        grad_norm, gain_first = norm_back(inputs, norm_gains[0], grad_first)
        tokens_grad = (grad_after_self + grad_norm)[None]
        context_own, context_other = core_sum(context_part)
        context_other = swap(context_other, 2)
        gains = jnp.stack([gain_first, gain_second, gain_third])
        heads_all = jnp.stack([heads, swap(heads, 1), heads_chip, swap(heads_chip, 1)])
        sum_self = Sum(
            place,
            (("owners", first_turned, (heads_all, 0)), ("owners", first_turned, (heads_all, 1))),
            (0, 1, 2),
        )
        sum_value = Sum(place, (("owners", first_turned, (heads_all, 2)),), (1, 0, 2))
        kept = sum_context.keep(sum_self.send(), sum_value.send())
        step = sum_cross.add(2, kept)
        patch_turned = turn(*after(tuple(patch_pieces), kept))
        grad_context = low(context_own + after(context_other, kept, patch_turned).astype(F32))
        context_chip = swap(grad_context, 2)
        for bit in reversed(range(2, dp.bit_length() - 1)):
            gains = gains + after(hop(gains, bit), patch_turned)
        gains = gains + after(hop(gains, 1), grad_context)
        kept = sum_self.keep(grad_context, gains), sum_value.keep(grad_context)
        value_one = sum_value.add(1, *kept)
        cross_all = sum_cross.add(3, value_one)
        context_one = sum_context.add(1, cross_all)
        context_chip = after(context_chip, context_one)
        grad_context_all = gather_rows(grad_context, context_chip)
        sum_patch = Sum(place, (("rows", patch_turned, grad_context_all),), (1, 0, 2))
        sum_patch.send()
        step = sum_context.add(2, sum_patch.keep(sum_patch.sent))
        step = sum_self.add(1, step)
        out_part = low(nn(after(hidden, step), down_half))
        sums = plane_core(out_part)
        patches_grad = nt(after(grad_context, step), patch_mat)[None]
        own, chip, side = plane_far(after(tuple(sums), step))
        step = sum_patch.add(1, step, patches_grad, chip, side)
        columns = tokens.shape[2] // dp
        hidden_grads = after(hidden_grads, chip, side)
        hidden_other = across(
            lax.dynamic_slice_in_dim(hidden_grads, (1 - x) * columns, columns, 1)
        )
        step = sum_value.add(2, step)
        step = sum_self.add(2, step)
        own, chip, side = plane_near((own, chip, side))
        step = sum_patch.add(2, step)
        out_tokens = low((after_cross + wide_sum(own, after(chip, step), side)) * live)[None]
        gains = gains + after(hop(after(gains, step), 0), out_tokens)
        gains = gains + after(swap(gains, 2), out_tokens)
        gains_grad = gains + after(swap(gains, 1), out_tokens)
        step = sum_context.add(3, step, gains_grad)
        c_out_grad, c_query_grad = sum_cross.parts()
        c_key_grad, c_value_grad, w_out_grad = sum_context.parts()
        moved = place_columns(low(jnp.stack([c_query_grad, c_key_grad, c_value_grad])))
        hidden_mine = lax.dynamic_slice_in_dim(hidden_grads, x * columns, columns, 1)
        hidden_mine, hidden_other = after((hidden_mine, hidden_other), step)

        def both_halves(i):
            mine, other = (
                half[i * units : (i + 1) * units] for half in (hidden_mine, hidden_other)
            )
            return jnp.where(
                x == 0,
                jnp.concatenate([mine, other], axis=0),
                jnp.concatenate([other, mine], axis=0),
            ).astype(F32)

        gate_grad, up_grad, down_grad = (both_halves(i) for i in range(3))
        step = sum_value.add(3, step, gate_grad)
        step = sum_patch.add(3, step)
        step = sum_self.add(3, step)
        c_query_grad, c_key_grad, c_value_grad = after(moved, step).astype(F32)

        w_query_grad, w_key_grad = sum_self.parts()
        (w_value_grad,), (patch_proj_grad,) = sum_value.parts(), sum_patch.parts()

        return (
            out_tokens,
            tokens_grad,
            patches_grad,
            gains_grad,
            w_query_grad,
            w_key_grad,
            w_value_grad,
            w_out_grad,
            c_query_grad,
            c_key_grad,
            c_value_grad,
            c_out_grad,
            patch_proj_grad,
            gate_grad,
            up_grad,
            down_grad,
        )

    both, rows, block = ("dp", "fsdp"), P("fsdp", None), P("fsdp", "dp")
    whole = P(both, None, None)
    return jax.shard_map(
        on_device,
        mesh=mesh,
        in_specs=(whole, whole, whole, P(both), P(both), P()) + (rows,) * 12,
        out_specs=(whole, whole, whole, P()) + (block,) * 12,
        check_vma=False,
    )
```

time: 3100 us -> 781 us (0.25)
  waiting for transfers between devices: 2690 us -> 328 us
  matrix products: 271 us -> 49.5 us
  Pallas kernels: 0 us -> 140 us
  starting transfers between devices: 2.67 us -> 83.3 us
  other arithmetic: 27.8 us -> 83.8 us
  blocking collectives: 42.4 us -> 0 us
    reduce_scatter x23 -> x1, waiting for transfers between devices: 1860 us -> 0.01 us  [on_device(): lax.psum_scatter(hidden_bundle, 'dp', scatter_dimension=0, axis_index_gro...]
    all_gather x12 -> x0, waiting for transfers between devices: 829 us -> none  [the longest x1 127 us: gather_hidden(): lax.all_gather(w_up, 'fsdp', axis=0, tiled=True)]
    ppermute x0 -> x105, waiting for transfers between devices: none -> 328 us  [the longest x71 128 us: swap(): return lax.ppermute(values, 'fsdp', [(i, i ^ r) for i in range(fsdp)])]
    dot_general x47 -> x12, matrix products: 268 us -> 49.5 us  [dot(): lax.dot_general(left, right, (((left_dim,), (right_dim,)), ((), ())), pre...]
    pallas_call x0 -> x34, Pallas kernels: none -> 140 us  [the longest x10 46.9 us: half_grads(): pl.pallas_call(half_kernel, out_shape=jax.ShapeDtypeStruct((4, rows, wide...]
    ppermute x0 -> x105, starting transfers between devices: none -> 83.3 us  [the longest x71 38.3 us: swap(): return lax.ppermute(values, 'fsdp', [(i, i ^ r) for i in range(fsdp)])]
    psum x1 -> x0, blocking collectives: 42.4 us -> none  [on_device(): lax.psum(jnp.stack([gain_first, gain_second, gain_third]), ('dp', 'fsdp'))]
  transfers between devices with their start and end apart: 36 -> 106, of which waited for: 34 -> 45; matrix products, arithmetic and copies ran while one was open for 8% -> 21% of each run, Pallas kernels for 0% -> 17%
where the time goes in v1:
time: 781 us; the launch traced here: 773 us
  waiting for transfers between devices  328 us (42%)
  Pallas kernels  140 us (18%)
  other arithmetic  83.8 us (11%)
  starting transfers between devices  83.3 us (11%)
  local copies, waits for them, and re-layouts  70.5 us (9%)
  matrix products  49.5 us (6%)
  between operations  18.5 us (2%)
    ppermute x71, waiting for transfers between devices, swap(): return lax.ppermute(values, 'fsdp', [(i, i ^ r) for i in range(fsdp)])  128 us
    ppermute x20, waiting for transfers between devices, hop(): return lax.ppermute(values, 'dp', [(i, i ^ 1 << bit) for i in range(dp)])  127 us
    dot_general x12, matrix products, dot(): lax.dot_general(left, right, (((left_dim,), (right_dim,)), ((), ())), pre...  49.5 us
    pallas_call x10, Pallas kernels, half_grads(): pl.pallas_call(half_kernel, out_shape=jax.ShapeDtypeStruct((4, rows, wide...  46.9 us
    ppermute x13, waiting for transfers between devices, across(): return lax.ppermute(values, 'dp', [(i, i ^ 1) for i in range(dp)])  43.3 us
    ppermute x71, starting transfers between devices, swap(): return lax.ppermute(values, 'fsdp', [(i, i ^ r) for i in range(fsdp)])  38.3 us
    unnamed x312, local copies, waits for them, and re-layouts  31.2 us
    ppermute x1, waiting for transfers between devices, place_columns(): return lax.ppermute(values, ('dp', 'fsdp'), pairs)  29.7 us
  transfers between devices with their start and end apart: 106, of which 45 were waited for; matrix products, arithmetic and copies ran while one was open for 21% of the time, Pallas kernels for 17%

profile of v1, /device:TPU:4, one launch (start us, length us, event | category | flops | bytes accessed | tf_op | source)
XLA Modules:
  0.0 773.4 jit_solution(13119506441754098918)
XLA Ops:
  22.3 30.0 %collective-permute-done.11.refs_6_.refs_17_ = bf16[1,2,256,512]{3,2,1,0:T(8,128)(2,1)S(1)} collective-permute-done((bf16[1,2,256,512]{3,2,1,0:T(8,128)(2,1)S(1)}, bf16[1,2,256,512]{3,2,1,0:T(8,128)(2,1)S(1)}, u32[]{:S(2)}, u32[]{:S(2)}) %collective-permute-start.11) | collective-permute-done | bytes 524320 | tf_op jit(solution)/shard_map/ppermute | solution.py:438
  58.0 13.6 %collective-permute-done.15 = bf16[104,2048]{1,0:T(8,128)(2,1)S(1)} collective-permute-done((bf16[104,2048]{1,0:T(8,128)(2,1)S(1)}, bf16[104,2048]{1,0:T(8,128)(2,1)S(1)}, u32[]{:S(2)}, u32[]{:S(2)}) %collective-permute-start.15) | collective-permute-done | bytes 426016 | tf_op jit(solution)/shard_map/ppermute | solution.py:438
  80.8 6.2 collective-permute-done.18
  106.9 6.4 shard_map.300.refs_0_
  133.7 6.5 collective-permute-done.20
  149.4 10.2 %collective-permute-done.23 = bf16[3,2,256,512]{3,2,0,1:T(8,128)(2,1)} collective-permute-done((bf16[3,2,256,512]{3,2,0,1:T(8,128)(2,1)S(1)}, bf16[3,2,256,512]{3,2,0,1:T(8,128)(2,1)}, u32[]{:S(2)}, u32[]{:S(2)}) %collective-permute-start.23) | collective-permute-done | bytes 1572896 | tf_op jit(solution)/shard_map/ppermute | solution.py:441
  169.8 8.5 %collective-permute-done.32.refs_2_ = bf16[256,2048]{1,0:T(8,128)(2,1)S(1)} collective-permute-done((bf16[256,2048]{1,0:T(8,128)(2,1)S(1)}, bf16[256,2048]{1,0:T(8,128)(2,1)S(1)}, u32[]{:S(2)}, u32[]{:S(2)}) %collective-permute-start.32) | collective-permute-done | bytes 1048608 | tf_op jit(solution)/shard_map/ppermute | solution.py:438
  188.5 5.5 collective-permute-done.35
  240.3 6.7 fusion.11
  269.0 7.1 fusion.9
  293.8 5.9 collective-permute-done.58
  303.4 13.0 %shard_map.309 = bf16[4,1920,512]{2,1,0:T(8,128)(2,1)} custom-call(s32[2]{0:T(128)S(1)} %broadcast_6_place.2.place, bf16[640,1024]{1,0:T(8,128)(2,1)S(1)} %shard_map.306.refs_0_, bf16[1024,2048]{1,0:T(8,128)(2,1)} %copy-done.136, bf16[640,1024]{1,0:T(8,128)(2,1)S(1)} %shard_map.307.refs_2_, bf16[1024,2048]{1,0:T(8,128)(2,1)} %copy-done.136, ...), custom_call_target="tpu_custom_call" | custom-call | flops 14400000000 | bytes 36000000 | tf_op jit(solution)/shard_map/pallas_call | solution.py:407
  323.3 10.1 %collective-permute-done.61 = bf16[128,2048]{1,0:T(8,128)(2,1)S(1)} collective-permute-done((bf16[128,2048]{1,0:T(8,128)(2,1)S(1)}, bf16[128,2048]{1,0:T(8,128)(2,1)S(1)}, u32[]{:S(2)}, u32[]{:S(2)}) %collective-permute-start.61) | collective-permute-done | bytes 524320 | tf_op jit(solution)/shard_map/ppermute | solution.py:438
  336.7 8.1 %shard_map.312 = (bf16[512,512]{1,0:T(8,128)(2,1)S(1)}, bf16[1024,512]{1,0:T(8,128)(2,1)S(1)}, bf16[1024,512]{1,0:T(8,128)(2,1)S(1)}) custom-call(s32[4,2]{1,0:T(4,128)S(1)} %pad_add_fusion.info, bf16[512,512]{1,0:T(8,128)(2,1)S(1)} %copy-done.35, bf16[1024,512]{1,0:T(8,128)(2,1)S(1)} %copy-done.68, bf16[1024,512]{1,0:T(8,128)(2,1)S(1)} %copy-done.66, ...), custom_call_target="tpu_custom_call" | custom-call | flops 6400000000 | bytes 16000000 | tf_op jit(solution)/shard_map/pallas_call | solution.py:129
  382.3 5.6 collective-permute-done.66
  393.0 8.0 %shard_map.319 = (bf16[512,512]{1,0:T(8,128)(2,1)S(1)}, bf16[512,512]{1,0:T(8,128)(2,1)S(1)}, bf16[512,512]{1,0:T(8,128)(2,1)S(1)}) custom-call(s32[4,2]{1,0:T(4,128)S(1)} %pad_add_fusion.info, bf16[512,512]{1,0:T(8,128)(2,1)S(1)} %copy-done.27, bf16[512,512]{1,0:T(8,128)(2,1)S(1)} %copy-done.25, bf16[512,512]{1,0:T(8,128)(2,1)S(1)} %copy-done.62, ...), custom_call_target="tpu_custom_call" | custom-call | flops 6400000000 | bytes 16000000 | tf_op jit(solution)/shard_map/pallas_call | solution.py:129
  404.9 31.1 %collective-permute-done.73 = bf16[4,1024,256]{2,1,0:T(8,128)(2,1)S(1)} collective-permute-done((bf16[4,1024,256]{2,1,0:T(8,128)(2,1)S(1)}, bf16[4,1024,256]{2,1,0:T(8,128)(2,1)S(1)}, u32[]{:S(2)}, u32[]{:S(2)}) %collective-permute-start.73) | collective-permute-done | bytes 2097184 | tf_op jit(solution)/shard_map/ppermute | solution.py:542
  440.2 8.9 %shard_map.325 = bf16[512,2048]{1,0:T(8,128)(2,1)} custom-call(s32[2]{0:T(128)} %copy-done.42, bf16[512,512]{1,0:T(8,128)(2,1)} %copy-done.36, bf16[512,512]{1,0:T(8,128)(2,1)} %copy-done.37, bf16[512,512]{1,0:T(8,128)(2,1)} %copy-done.38, bf16[512,2048]{1,0:T(8,128)(2,1)} %refs_3_, bf16[3,512,512]{2,1,0:T(8,128)(2,1)} %copy-done.6, ...), custom_call_target="tpu_custom_call" | custom-call | flops 7742608896 | bytes 19356520 | tf_op jit(solution)/shard_map/pallas_call | solution.py:247
  452.4 10.3 %shard_map.320 = bf16[1024,2048]{1,0:T(8,128)(2,1)} custom-call(s32[2]{0:T(128)} %copy-done.42, bf16[1024,512]{1,0:T(8,128)(2,1)} %copy-done.74, bf16[1024,512]{1,0:T(8,128)(2,1)} %copy-done.76, bf16[512,2048]{1,0:T(8,128)(2,1)} %refs_2_.1, bf16[3,512,512]{2,1,0:T(8,128)(2,1)} %copy-done.21, bf16[3,2,256,512]{3,2,1,0:T(8,128)(2,1)} %copy.38.refs_6_.refs_3_.refs_4_.refs_10_, ...), custom_call_target="tpu_custom_call" | custom-call | flops 9523478528 | bytes 23808696 | tf_op jit(solution)/shard_map/pallas_call | solution.py:247
  466.1 8.4 %shard_map.326 = bf16[4,1536,256]{2,1,0:T(8,128)(2,1)} custom-call(s32[2]{0:T(128)S(1)} %copy-done.44, bf16[2048,1024]{1,0:T(8,128)(2,1)} %copy-done.63, bf16[1024,512]{1,0:T(8,128)(2,1)S(1)} %copy-done.75, bf16[2048,1024]{1,0:T(8,128)(2,1)} %copy-done.63, bf16[1024,512]{1,0:T(8,128)(2,1)S(1)} %copy-done.77, bf16[512,512]{1,0:T(8,128)(2,1)S(1)} %copy-done.83, ...), custom_call_target="tpu_custom_call" | custom-call | flops 5851428352 | bytes 14628571 | tf_op jit(solution)/shard_map/pallas_call | solution.py:313
  478.2 6.6 pad_maximum_fusion.refs_1_.refs_3_
  498.4 8.4 %shard_map.323 = bf16[4,1536,256]{2,1,0:T(8,128)(2,1)} custom-call(s32[2]{0:T(128)S(1)} %copy-done.44, bf16[2048,1024]{1,0:T(8,128)(2,1)} %copy-done.63, bf16[1024,512]{1,0:T(8,128)(2,1)S(1)} %copy-done.75, bf16[2048,1024]{1,0:T(8,128)(2,1)} %copy-done.63, bf16[1024,512]{1,0:T(8,128)(2,1)S(1)} %copy-done.77, bf16[512,512]{1,0:T(8,128)(2,1)S(1)} %copy-done.83, ...), custom_call_target="tpu_custom_call" | custom-call | flops 5851428352 | bytes 14628571 | tf_op jit(solution)/shard_map/pallas_call | solution.py:313
  512.9 9.4 %collective-permute-done.70 = bf16[256,2048]{1,0:T(8,128)(2,1)S(1)} collective-permute-done((bf16[256,2048]{1,0:T(8,128)(2,1)S(1)}, bf16[256,2048]{1,0:T(8,128)(2,1)S(1)}, u32[]{:S(2)}, u32[]{:S(2)}) %collective-permute-start.70) | collective-permute-done | bytes 1048608 | tf_op jit(solution)/shard_map/ppermute | solution.py:438
  564.3 26.6 %collective-permute-done.83 = bf16[2,1536,256]{2,1,0:T(8,128)(2,1)} collective-permute-done((bf16[2,1536,256]{2,1,0:T(8,128)(2,1)}, bf16[2,1536,256]{2,1,0:T(8,128)(2,1)}, u32[]{:S(2)}, u32[]{:S(2)}) %collective-permute-start.83) | collective-permute-done | bytes 1572896 | tf_op jit(solution)/shard_map/ppermute | solution.py:542
  593.7 9.5 %collective-permute-done.78 = bf16[4,1024,256]{2,1,0:T(8,128)(2,1)S(1)} collective-permute-done((bf16[4,1024,256]{2,1,0:T(8,128)(2,1)S(1)}, bf16[4,1024,256]{2,1,0:T(8,128)(2,1)S(1)}, u32[]{:S(2)}, u32[]{:S(2)}) %collective-permute-start.78) | collective-permute-done | bytes 2097184 | tf_op jit(solution)/shard_map/ppermute | solution.py:542
  626.6 6.2 convolution_bitcast_fusion
  634.2 6.1 collective-permute-done.88
  641.5 15.5 %collective-permute-done.90 = bf16[4,416,256]{2,1,0:T(8,128)(2,1)S(1)} collective-permute-done((bf16[4,416,256]{2,1,0:T(8,128)(2,1)S(1)}, bf16[4,416,256]{2,1,0:T(8,128)(2,1)S(1)}, u32[]{:S(2)}, u32[]{:S(2)}) %collective-permute-start.90) | collective-permute-done | bytes 852000 | tf_op jit(solution)/shard_map/ppermute | solution.py:542
  659.9 18.9 %collective-permute-done.93 = bf16[2,1024,256]{2,1,0:T(8,128)(2,1)S(1)} collective-permute-done((bf16[2,1024,256]{2,1,0:T(8,128)(2,1)}, bf16[2,1024,256]{2,1,0:T(8,128)(2,1)S(1)}, u32[]{:S(2)}, u32[]{:S(2)}) %collective-permute-start.93) | collective-permute-done | bytes 1048608 | tf_op jit(solution)/shard_map/ppermute | solution.py:542
  698.4 13.8 %collective-permute-done.103 = bf16[1920,256]{1,0:T(8,128)(2,1)S(1)} collective-permute-done((bf16[1920,256]{1,0:T(8,128)(2,1)S(1)}, bf16[1920,256]{1,0:T(8,128)(2,1)S(1)}, u32[]{:S(2)}, u32[]{:S(2)}) %collective-permute-start.103) | collective-permute-done | bytes 983072 | tf_op jit(solution)/shard_map/ppermute | solution.py:441
  716.3 13.2 %collective-permute-done.100 = bf16[416,256]{1,0:T(8,128)(2,1)S(1)} collective-permute-done((bf16[416,256]{1,0:T(8,128)(2,1)S(1)}, bf16[416,256]{1,0:T(8,128)(2,1)S(1)}, u32[]{:S(2)}, u32[]{:S(2)}) %collective-permute-start.100) | collective-permute-done | bytes 213024 | tf_op jit(solution)/shard_map/ppermute | solution.py:542
  734.2 29.7 %collective-permute-done.104 = bf16[3,512,256]{2,1,0:T(8,128)(2,1)S(1)} collective-permute-done((bf16[3,512,256]{2,1,0:T(8,128)(2,1)S(1)}, bf16[3,512,256]{2,1,0:T(8,128)(2,1)S(1)}, u32[]{:S(2)}, u32[]{:S(2)}) %collective-permute-start.104) | collective-permute-done | bytes 786464 | tf_op jit(solution)/shard_map/ppermute | solution.py:592
  (681 shorter events, 380.7 us)
Async XLA Ops:
  7.2 516.0 %reduce-scatter.2.cloned.1.call-start = ((), (), s32[]{:S(2)}) async-start(), calls=%async_computation.1 | async-start | bytes 9830400 | tf_op jit(solution)/shard_map/reduce_scatter | solution.py:721
  8.8 47.7 %collective-permute-start.1 = (s32[1,2]{1,0:T(1,128)S(1)}, s32[1,2]{1,0:T(1,128)S(1)}, u32[]{:S(2)}, u32[]{:S(2)}) collective-permute-start(s32[1,2]{1,0:T(1,128)S(1)} %pad_add_fusion.1), channel_id=1, source_target_pairs={{0,1},{1,0},{2,3},{3,2},{4,5},{5,4},{6,7},{7,6},{8,9},{9,8},{10,11... | collective-permute-start | bytes 32 | tf_op jit(solution)/shard_map/ppermute | solution.py:438
  15.0 37.4 %collective-permute-start.5 = (bf16[2,2,256,512]{3,2,0,1:T(8,128)(2,1)S(1)}, bf16[2,2,256,512]{3,2,0,1:T(8,128)(2,1)S(1)}, u32[]{:S(2)}, u32[]{:S(2)}) collective-permute-start(bf16[2,2,256,512]{3,2,0,1:T(8,128)(2,1)S(1)} %pad_maximum_fusion.6), channel_id=1, source_target_pairs={{0,2},{1,3},{2,0},{3,1},{4,6},{5,7},{6,4},{7,5},{8,10},{9,11},{10,... | collective-permute-start | bytes 3145736 | tf_op jit(solution)/shard_map/ppermute | solution.py:438
  16.5 35.8 %collective-permute-start.11 = (bf16[1,2,256,512]{3,2,1,0:T(8,128)(2,1)S(1)}, bf16[1,2,256,512]{3,2,1,0:T(8,128)(2,1)S(1)}, u32[]{:S(2)}, u32[]{:S(2)}) collective-permute-start(bf16[1,2,256,512]{3,2,1,0:T(8,128)(2,1)S(1)} %maximum_bitcast_fusion.2), channel_id=1, source_target_pairs={{0,2},{1,3},{2,0},{3,1},{4,6},{5,7},{6,4},{7,5},{8,10},{9,11},{10,... | collective-permute-start | bytes 1572872 | tf_op jit(solution)/shard_map/ppermute | solution.py:438
  18.6 60.3 %collective-permute-start.4 = (bf16[128,2048]{1,0:T(8,128)(2,1)S(1)}, bf16[128,2048]{1,0:T(8,128)(2,1)S(1)}, u32[]{:S(2)}, u32[]{:S(2)}) collective-permute-start(bf16[128,2048]{1,0:T(8,128)(2,1)S(1)} %multiply_convert_fusion.5.refs_0_), channel_id=1, source_target_pairs={{0,2},{1,3},{2,0},{3,1},{4,6},{5,7},{6,4},{7,5},{8,10},{9,11},{10,... | collective-permute-start | bytes 1572872 | tf_op jit(solution)/shard_map/ppermute | solution.py:438
  20.0 60.7 %collective-permute-start.3 = (bf16[128,2048]{1,0:T(8,128)(2,1)S(1)}, bf16[128,2048]{1,0:T(8,128)(2,1)S(1)}, u32[]{:S(2)}, u32[]{:S(2)}) collective-permute-start(bf16[128,2048]{1,0:T(8,128)(2,1)S(1)} %multiply_convert_fusion.5.refs_0_), channel_id=1, source_target_pairs={{0,1},{1,0},{2,3},{3,2},{4,5},{5,4},{6,7},{7,6},{8,9},{9,8},{10,11... | collective-permute-start | bytes 1572872 | tf_op jit(solution)/shard_map/ppermute | solution.py:438
  57.6 32.7 %collective-permute-start.8 = (bf16[3,512,512]{2,1,0:T(8,128)(2,1)S(1)}, bf16[3,512,512]{2,1,0:T(8,128)(2,1)S(1)}, u32[]{:S(2)}, u32[]{:S(2)}) collective-permute-start(bf16[3,512,512]{2,1,0:T(8,128)(2,1)S(1)} %pad_maximum_fusion.4), channel_id=1, source_target_pairs={{0,1},{1,0},{2,3},{3,2},{4,5},{5,4},{6,7},{7,6},{8,9},{9,8},{10,11... | collective-permute-start | bytes 4718600 | tf_op jit(solution)/shard_map/ppermute | solution.py:438
  90.4 29.4 %collective-permute-start.29 = (bf16[208,2048]{1,0:T(8,128)(2,1)}, bf16[208,2048]{1,0:T(8,128)(2,1)}, u32[]{:S(2)}, u32[]{:S(2)}) collective-permute-start(bf16[208,2048]{1,0:T(8,128)(2,1)} %maximum_select_fusion.2), channel_id=1, source_target_pairs={{0,4},{4,0},{8,12},{12,8},{16,20},{20,16},{24,28},{28,24},{1,5},{5... | collective-permute-start | bytes 2555912 | tf_op jit(solution)/shard_map/ppermute | solution.py:441
  123.1 36.5 %collective-permute-start.23 = (bf16[3,2,256,512]{3,2,0,1:T(8,128)(2,1)S(1)}, bf16[3,2,256,512]{3,2,0,1:T(8,128)(2,1)}, u32[]{:S(2)}, u32[]{:S(2)}) collective-permute-start(bf16[3,2,256,512]{3,2,0,1:T(8,128)(2,1)S(1)} %copy-done.92), channel_id=1, source_target_pairs={{0,4},{4,0},{8,12},{12,8},{16,20},{20,16},{24,28},{28,24},{1,5},{5... | collective-permute-start | bytes 4718600 | tf_op jit(solution)/shard_map/ppermute | solution.py:441
  124.5 37.1 %collective-permute-start.26 = (bf16[3,256,512]{2,1,0:T(8,128)(2,1)}, bf16[3,256,512]{2,1,0:T(8,128)(2,1)S(1)}, u32[]{:S(2)}, u32[]{:S(2)}) collective-permute-start(bf16[3,256,512]{2,1,0:T(8,128)(2,1)} %slice_bitcast_fusion.2), channel_id=1, source_target_pairs={{0,1},{1,0},{2,3},{3,2},{4,5},{5,4},{6,7},{7,6},{8,9},{9,8},{10,11... | collective-permute-start | bytes 2359304 | tf_op jit(solution)/shard_map/ppermute | solution.py:438
  132.3 33.9 %collective-permute-start.25 = (bf16[3,512,512]{2,1,0:T(8,128)(2,1)}, bf16[3,512,512]{2,1,0:T(8,128)(2,1)S(1)}, u32[]{:S(2)}, u32[]{:S(2)}) collective-permute-start(bf16[3,512,512]{2,1,0:T(8,128)(2,1)} %pad_maximum_fusion.5), channel_id=1, source_target_pairs={{0,1},{1,0},{2,3},{3,2},{4,5},{5,4},{6,7},{7,6},{8,9},{9,8},{10,11... | collective-permute-start | bytes 4718600 | tf_op jit(solution)/shard_map/ppermute | solution.py:438
  149.0 29.2 %collective-permute-start.32 = (bf16[256,2048]{1,0:T(8,128)(2,1)S(1)}, bf16[256,2048]{1,0:T(8,128)(2,1)S(1)}, u32[]{:S(2)}, u32[]{:S(2)}) collective-permute-start(bf16[256,2048]{1,0:T(8,128)(2,1)S(1)} %convolution_convert_fusion.3.refs_0_), channel_id=1, source_target_pairs={{0,2},{1,3},{2,0},{3,1},{4,6},{5,7},{6,4},{7,5},{8,10},{9,11},{10,... | collective-permute-start | bytes 3145736 | tf_op jit(solution)/shard_map/ppermute | solution.py:438
  387.9 48.0 %collective-permute-start.73 = (bf16[4,1024,256]{2,1,0:T(8,128)(2,1)S(1)}, bf16[4,1024,256]{2,1,0:T(8,128)(2,1)S(1)}, u32[]{:S(2)}, u32[]{:S(2)}) collective-permute-start(bf16[4,1024,256]{2,1,0:T(8,128)(2,1)S(1)} %shard_map.314), channel_id=1, source_target_pairs={{0,4},{4,0},{8,12},{12,8},{16,20},{20,16},{24,28},{28,24},{1,5},{5... | collective-permute-start | bytes 6291464 | tf_op jit(solution)/shard_map/ppermute | solution.py:542
  403.7 48.1 %collective-permute-start.68 = (bf16[512,1536]{1,0:T(8,128)(2,1)}, bf16[512,1536]{1,0:T(8,128)(2,1)}, u32[]{:S(2)}, u32[]{:S(2)}) collective-permute-start(bf16[512,1536]{1,0:T(8,128)(2,1)} %constant_dynamic-update-slice_fusion.18), channel_id=1, source_target_pairs={{0,2},{1,3},{2,0},{3,1},{4,6},{5,7},{6,4},{7,5},{8,10},{9,11},{10,... | collective-permute-start | bytes 4718600 | tf_op jit(solution)/shard_map/ppermute | solution.py:438
  404.9 72.0 %collective-permute-start.71 = (bf16[512,1536]{1,0:T(8,128)(2,1)}, bf16[512,1536]{1,0:T(8,128)(2,1)}, u32[]{:S(2)}, u32[]{:S(2)}) collective-permute-start(bf16[512,1536]{1,0:T(8,128)(2,1)} %constant_dynamic-update-slice_fusion.18), channel_id=1, source_target_pairs={{0,1},{1,0},{2,3},{3,2},{4,5},{5,4},{6,7},{7,6},{8,9},{9,8},{10,11... | collective-permute-start | bytes 4718600 | tf_op jit(solution)/shard_map/ppermute | solution.py:438
  438.6 68.1 %collective-permute-start.80 = (bf16[2,1024,256]{2,1,0:T(8,128)(2,1)}, bf16[2,1024,256]{2,1,0:T(8,128)(2,1)}, u32[]{:S(2)}, u32[]{:S(2)}) collective-permute-start(bf16[2,1024,256]{2,1,0:T(8,128)(2,1)} %add_convert_fusion.3), channel_id=1, source_target_pairs={{0,8},{4,12},{8,0},{12,4},{16,24},{20,28},{24,16},{28,20},{1,9},{5... | collective-permute-start | bytes 3145736 | tf_op jit(solution)/shard_map/ppermute | solution.py:542
  466.1 29.0 %collective-permute-start.69 = (bf16[2,256,2048]{2,1,0:T(8,128)(2,1)}, bf16[2,256,2048]{2,1,0:T(8,128)(2,1)S(1)}, u32[]{:S(2)}, u32[]{:S(2)}) collective-permute-start(bf16[2,256,2048]{2,1,0:T(8,128)(2,1)} %slice.439), channel_id=1, source_target_pairs={{0,1},{1,0},{2,3},{3,2},{4,5},{5,4},{6,7},{7,6},{8,9},{9,8},{10,11... | collective-permute-start | bytes 6291464 | tf_op jit(solution)/shard_map/ppermute | solution.py:438
  474.5 75.4 %collective-permute-start.79 = (bf16[4,1536,256]{2,1,0:T(8,128)(2,1)}, bf16[4,1536,256]{2,1,0:T(8,128)(2,1)}, u32[]{:S(2)}, u32[]{:S(2)}) collective-permute-start(bf16[4,1536,256]{2,1,0:T(8,128)(2,1)} %shard_map.326), channel_id=1, source_target_pairs={{0,4},{4,0},{8,12},{12,8},{16,20},{20,16},{24,28},{28,24},{1,5},{5... | collective-permute-start | bytes 9437192 | tf_op jit(solution)/shard_map/ppermute | solution.py:542
  476.9 46.3 %collective-permute-start.75 = (bf16[128,2048]{1,0:T(8,128)(2,1)S(1)}, bf16[128,2048]{1,0:T(8,128)(2,1)}, u32[]{:S(2)}, u32[]{:S(2)}) collective-permute-start(bf16[128,2048]{1,0:T(8,128)(2,1)S(1)} %fusion.23), channel_id=1, source_target_pairs={{0,2},{1,3},{2,0},{3,1},{4,6},{5,7},{6,4},{7,5},{8,10},{9,11},{10,... | collective-permute-start | bytes 1572872 | tf_op jit(solution)/shard_map/ppermute | solution.py:438
  489.3 55.3 %collective-permute-start.82 = (bf16[4,512,256]{2,1,0:T(8,128)(2,1)}, bf16[4,512,256]{2,1,0:T(8,128)(2,1)}, u32[]{:S(2)}, u32[]{:S(2)}) collective-permute-start(bf16[4,512,256]{2,1,0:T(8,128)(2,1)} %shard_map.322), channel_id=1, source_target_pairs={{0,8},{4,12},{8,0},{12,4},{16,24},{20,28},{24,16},{28,20},{1,9},{5... | collective-permute-start | bytes 3145736 | tf_op jit(solution)/shard_map/ppermute | solution.py:542
  509.0 38.1 %collective-permute-start.81 = (bf16[1024,256]{1,0:T(8,128)(2,1)}, bf16[1024,256]{1,0:T(8,128)(2,1)}, u32[]{:S(2)}, u32[]{:S(2)}) collective-permute-start(bf16[1024,256]{1,0:T(8,128)(2,1)} %fusion.41), channel_id=1, source_target_pairs={{0,16},{4,20},{8,24},{12,28},{16,0},{20,4},{24,8},{28,12},{1,17},{... | collective-permute-start | bytes 1572872 | tf_op jit(solution)/shard_map/ppermute | solution.py:542
  553.8 37.1 %collective-permute-start.83 = (bf16[2,1536,256]{2,1,0:T(8,128)(2,1)}, bf16[2,1536,256]{2,1,0:T(8,128)(2,1)}, u32[]{:S(2)}, u32[]{:S(2)}) collective-permute-start(bf16[2,1536,256]{2,1,0:T(8,128)(2,1)} %add_convert_fusion.1), channel_id=1, source_target_pairs={{0,8},{4,12},{8,0},{12,4},{16,24},{20,28},{24,16},{28,20},{1,9},{5... | collective-permute-start | bytes 4718600 | tf_op jit(solution)/shard_map/ppermute | solution.py:542
  555.5 47.8 %collective-permute-start.78 = (bf16[4,1024,256]{2,1,0:T(8,128)(2,1)S(1)}, bf16[4,1024,256]{2,1,0:T(8,128)(2,1)S(1)}, u32[]{:S(2)}, u32[]{:S(2)}) collective-permute-start(bf16[4,1024,256]{2,1,0:T(8,128)(2,1)S(1)} %copy-done.20), channel_id=1, source_target_pairs={{0,4},{4,0},{8,12},{12,8},{16,20},{20,16},{24,28},{28,24},{1,5},{5... | collective-permute-start | bytes 6291464 | tf_op jit(solution)/shard_map/ppermute | solution.py:542
  617.4 40.5 %collective-permute-start.94 = (bf16[2,512,256]{2,1,0:T(8,128)(2,1)S(1)}, bf16[2,512,256]{2,1,0:T(8,128)(2,1)S(1)}, u32[]{:S(2)}, u32[]{:S(2)}) collective-permute-start(bf16[2,512,256]{2,1,0:T(8,128)(2,1)S(1)} %copy-done.122), channel_id=1, source_target_pairs={{0,4},{4,0},{8,12},{12,8},{16,20},{20,16},{24,28},{28,24},{1,5},{5... | collective-permute-start | bytes 1572872 | tf_op jit(solution)/shard_map/ppermute | solution.py:542
  618.3 38.6 %collective-permute-start.90 = (bf16[4,416,256]{2,1,0:T(8,128)(2,1)S(1)}, bf16[4,416,256]{2,1,0:T(8,128)(2,1)S(1)}, u32[]{:S(2)}, u32[]{:S(2)}) collective-permute-start(bf16[4,416,256]{2,1,0:T(8,128)(2,1)S(1)} %shard_map.329), channel_id=1, source_target_pairs={{0,8},{4,12},{8,0},{12,4},{16,24},{20,28},{24,16},{28,20},{1,9},{5... | collective-permute-start | bytes 2555912 | tf_op jit(solution)/shard_map/ppermute | solution.py:542
  618.7 73.2 %collective-permute-start.102 = (bf16[1536,256]{1,0:T(8,128)(2,1)}, bf16[1536,256]{1,0:T(8,128)(2,1)S(1)}, u32[]{:S(2)}, u32[]{:S(2)}) collective-permute-start(bf16[1536,256]{1,0:T(8,128)(2,1)} %fusion.37), channel_id=1, source_target_pairs={{0,16},{4,20},{8,24},{12,28},{16,0},{20,4},{24,8},{28,12},{1,17},{... | collective-permute-start | bytes 2359304 | tf_op jit(solution)/shard_map/ppermute | solution.py:542
  621.7 57.0 %collective-permute-start.93 = (bf16[2,1024,256]{2,1,0:T(8,128)(2,1)}, bf16[2,1024,256]{2,1,0:T(8,128)(2,1)S(1)}, u32[]{:S(2)}, u32[]{:S(2)}) collective-permute-start(bf16[2,1024,256]{2,1,0:T(8,128)(2,1)} %add_convert_fusion.2), channel_id=1, source_target_pairs={{0,8},{4,12},{8,0},{12,4},{16,24},{20,28},{24,16},{28,20},{1,9},{5... | collective-permute-start | bytes 3145736 | tf_op jit(solution)/shard_map/ppermute | solution.py:542
  640.2 40.0 %collective-permute-start.95 = (bf16[128,2048]{1,0:T(8,128)(2,1)S(1)}, bf16[128,2048]{1,0:T(8,128)(2,1)S(1)}, u32[]{:S(2)}, u32[]{:S(2)}) collective-permute-start(bf16[128,2048]{1,0:T(8,128)(2,1)S(1)} %pad_maximum_fusion.14), channel_id=1, source_target_pairs={{0,4},{4,0},{8,12},{12,8},{16,20},{20,16},{24,28},{28,24},{1,5},{5... | collective-permute-start | bytes 1572872 | tf_op jit(solution)/shard_map/ppermute | solution.py:441
  684.8 29.6 %collective-permute-start.101 = (bf16[512,256]{1,0:T(8,128)(2,1)S(1)}, bf16[512,256]{1,0:T(8,128)(2,1)S(1)}, u32[]{:S(2)}, u32[]{:S(2)}) collective-permute-start(bf16[512,256]{1,0:T(8,128)(2,1)S(1)} %fusion.46), channel_id=1, source_target_pairs={{0,16},{4,20},{8,24},{12,28},{16,0},{20,4},{24,8},{28,12},{1,17},{... | collective-permute-start | bytes 786440 | tf_op jit(solution)/shard_map/ppermute | solution.py:542
  686.9 43.5 %collective-permute-start.99 = (bf16[1024,256]{1,0:T(8,128)(2,1)S(1)}, bf16[1024,256]{1,0:T(8,128)(2,1)S(1)}, u32[]{:S(2)}, u32[]{:S(2)}) collective-permute-start(bf16[1024,256]{1,0:T(8,128)(2,1)S(1)} %fusion.42), channel_id=1, source_target_pairs={{0,16},{4,20},{8,24},{12,28},{16,0},{20,4},{24,8},{28,12},{1,17},{... | collective-permute-start | bytes 1572872 | tf_op jit(solution)/shard_map/ppermute | solution.py:542
  689.1 40.5 %collective-permute-start.100 = (bf16[416,256]{1,0:T(8,128)(2,1)S(1)}, bf16[416,256]{1,0:T(8,128)(2,1)S(1)}, u32[]{:S(2)}, u32[]{:S(2)}) collective-permute-start(bf16[416,256]{1,0:T(8,128)(2,1)S(1)} %fusion.48), channel_id=1, source_target_pairs={{0,16},{4,20},{8,24},{12,28},{16,0},{20,4},{24,8},{28,12},{1,17},{... | collective-permute-start | bytes 638984 | tf_op jit(solution)/shard_map/ppermute | solution.py:542
  694.9 69.0 %collective-permute-start.104 = (bf16[3,512,256]{2,1,0:T(8,128)(2,1)S(1)}, bf16[3,512,256]{2,1,0:T(8,128)(2,1)S(1)}, u32[]{:S(2)}, u32[]{:S(2)}) collective-permute-start(bf16[3,512,256]{2,1,0:T(8,128)(2,1)S(1)} %pad_maximum_fusion.8), channel_id=1, source_target_pairs={{0,0},{1,8},{2,16},{3,24},{4,4},{5,12},{6,20},{7,28},{8,1},{9,9},{... | collective-permute-start | bytes 2359304 | tf_op jit(solution)/shard_map/ppermute | solution.py:592
  (222 other events, 2646.4 us)
Sparse Core Ops, SparseCore 0:
  316.6 145.1 reduce-scatter.1

commit v2 on v1

--- a/solution.py
+++ b/solution.py
@@ -639,14 +639,15 @@
         value_far = across(after(value_near, pair_far))
 
         rows = patch_proj.shape[0] // 4
-        patch_in = after(patch_proj, pair_near, value_near)
+        patch_in = after(patch_proj, pair_near)
         patch_mate = swap(patch_in, 1)
         patch_part = swap(lax.dynamic_slice_in_dim(patch_in, (2 * x + z) * rows, rows, 0), 2)
         patch_half = pick(z, patch_part, hop(patch_part, 1), 0)
         patch_chip = pick(x, patch_half, across(patch_half), 0)
         patch_far = swap(patch_chip, 1)
         cross_own = (c_key, c_value, c_query)
-        cross_part = swap(sent_parts(after(cross_own, patch_part), f, 2 * x + z, 4), 2)
+        cross_ready = after(cross_own, patch_part, value_near)
+        cross_part = swap(sent_parts(cross_ready, f, 2 * x + z, 4), 2)
         cross_near = pick(z, cross_part, hop(cross_part, 1), 2)
         cross_far = across(cross_near)
         self_mate = mate_parts((w_query, w_key, w_value), f)
@@ -678,13 +679,13 @@
         context_blocks = gather_blocks(context, after(context_chip, cross_q))
         cross_k = to_heads(place, context_blocks, cross_key_w)
         cross_v = to_heads(place, context_blocks, cross_value_w)
+        cross_mixed = attend(info, cross_q, cross_k, cross_v, slot, keys, width, False)
         grad_early = after(grad_out, context)
-        cross_v, *grad_near = lax.optimization_barrier(
-            (cross_v, swap(grad_early, 2), across(grad_early))
-        )
-        cross_mixed = attend(info, cross_q, cross_k, cross_v, slot, keys, width, False)
+        cross_mixed, *grad_near = lax.optimization_barrier(
+            (cross_mixed, swap(grad_early, 2), across(grad_early))
+        )
         own, other = core_sum(low(nn(cross_mixed, c_out)))
-        grad_all = gather_plane(grad_out, after(tuple(grad_near), other))
+        grad_all = gather_plane(grad_out, tuple(grad_near))
         other = after(swap(other, 2), grad_all)
         after_cross = after_self + own + other.astype(F32)
         third = normed(after_cross, norm_gains[2])
@@ -764,11 +765,10 @@
         )
         heads = jnp.concatenate([grad_q, grad_k, grad_v], axis=1)
         heads_chip = swap(heads, 2)
-        cross_one = sum_cross.add(1, grad_q)
-        own, other = core_sum(
-            from_heads(place, (after(grad_q, cross_one), grad_k, grad_v), (query_w, key_w, value_w))
-        )
+        self_part = from_heads(place, (grad_q, grad_k, grad_v), (query_w, key_w, value_w))
+        own, other = core_sum(self_part)
         other = swap(other, 2)
+        cross_one = sum_cross.add(1, self_part)
         sum_context = Sum(
             place,
             (
@@ -812,30 +812,33 @@
         grad_context_all = gather_rows(grad_context, context_chip)
         sum_patch = Sum(place, (("rows", patch_turned, grad_context_all),), (1, 0, 2))
         sum_patch.send()
-        step = sum_context.add(2, sum_patch.keep(sum_patch.sent))
+        kept = sum_patch.keep(sum_patch.sent)
+        out_part = low(nn(after(hidden, kept), down_half))
+        sums = plane_core(out_part)
+        patches_grad = nt(after(grad_context, kept), patch_mat)[None]
+        step = sum_context.add(2, kept, out_part, patches_grad)
         step = sum_self.add(1, step)
-        out_part = low(nn(after(hidden, step), down_half))
-        sums = plane_core(out_part)
-        patches_grad = nt(after(grad_context, step), patch_mat)[None]
         own, chip, side = plane_far(after(tuple(sums), step))
-        step = sum_patch.add(1, step, patches_grad, chip, side)
+        step = sum_patch.add(1, step)
+        step = sum_value.add(2, step)
+        gains = gains + after(hop(after(gains, step), 0), chip, side)
+        gains = gains + after(swap(gains, 2), chip)
+        gains_grad = gains + after(swap(gains, 1), chip)
+        step = sum_patch.add(2, step, chip, side, gains_grad)
+        step = sum_self.add(2, step)
         columns = tokens.shape[2] // dp
-        hidden_grads = after(hidden_grads, chip, side)
+        hidden_grads = after(hidden_grads, step)
         hidden_other = across(
             lax.dynamic_slice_in_dim(hidden_grads, (1 - x) * columns, columns, 1)
         )
-        step = sum_value.add(2, step)
-        step = sum_self.add(2, step)
         own, chip, side = plane_near((own, chip, side))
-        step = sum_patch.add(2, step)
-        out_tokens = low((after_cross + wide_sum(own, after(chip, step), side)) * live)[None]
-        gains = gains + after(hop(after(gains, step), 0), out_tokens)
-        gains = gains + after(swap(gains, 2), out_tokens)
-        gains_grad = gains + after(swap(gains, 1), out_tokens)
-        step = sum_context.add(3, step, gains_grad)
+        step = sum_context.add(3, step)
         c_out_grad, c_query_grad = sum_cross.parts()
         c_key_grad, c_value_grad, w_out_grad = sum_context.parts()
         moved = place_columns(low(jnp.stack([c_query_grad, c_key_grad, c_value_grad])))
+        step = sum_value.add(3, step, hidden_other)
+        step = sum_self.add(3, step)
+        out_tokens = low((after_cross + wide_sum(own, after(chip, step), side)) * live)[None]
         hidden_mine = lax.dynamic_slice_in_dim(hidden_grads, x * columns, columns, 1)
         hidden_mine, hidden_other = after((hidden_mine, hidden_other), step)
 
@@ -850,9 +853,7 @@
             ).astype(F32)
 
         gate_grad, up_grad, down_grad = (both_halves(i) for i in range(3))
-        step = sum_value.add(3, step, gate_grad)
-        step = sum_patch.add(3, step)
-        step = sum_self.add(3, step)
+        step = sum_patch.add(3, step, gate_grad)
         c_query_grad, c_key_grad, c_value_grad = after(moved, step).astype(F32)
 
         w_query_grad, w_key_grad = sum_self.parts()

time: 781 us -> 747 us (0.956)
  waiting for transfers between devices: 328 us -> 290 us
    ppermute x20, waiting for transfers between devices: 127 us -> 84.9 us  [hop(): return lax.ppermute(values, 'dp', [(i, i ^ 1 << bit) for i in range(dp)])]
    unnamed x312 -> x300, local copies, waits for them, and re-layouts: 31.2 us -> 31.8 us
  transfers between devices with their start and end apart: 106 -> 106, of which waited for: 45 -> 42; matrix products, arithmetic and copies ran while one was open for 21% -> 24% of each run, Pallas kernels for 17% -> 19%
where the time goes in v2:
time: 747 us; the launch traced here: 739 us
  waiting for transfers between devices  290 us (39%)
  Pallas kernels  142 us (19%)
  starting transfers between devices  84.6 us (11%)
  other arithmetic  82.5 us (11%)
  local copies, waits for them, and re-layouts  71.3 us (10%)
  matrix products  50.4 us (7%)
  between operations  18.4 us (2%)
    ppermute x71, waiting for transfers between devices, swap(): return lax.ppermute(values, 'fsdp', [(i, i ^ r) for i in range(fsdp)])  133 us
    ppermute x20, waiting for transfers between devices, hop(): return lax.ppermute(values, 'dp', [(i, i ^ 1 << bit) for i in range(dp)])  84.9 us
    dot_general x12, matrix products, dot(): lax.dot_general(left, right, (((left_dim,), (right_dim,)), ((), ())), pre...  50.4 us
    pallas_call x10, Pallas kernels, half_grads(): pl.pallas_call(half_kernel, out_shape=jax.ShapeDtypeStruct((4, rows, wide...  49.2 us
    ppermute x13, waiting for transfers between devices, across(): return lax.ppermute(values, 'dp', [(i, i ^ 1) for i in range(dp)])  39.3 us
    ppermute x71, starting transfers between devices, swap(): return lax.ppermute(values, 'fsdp', [(i, i ^ r) for i in range(fsdp)])  36.3 us
    ppermute x1, waiting for transfers between devices, place_columns(): return lax.ppermute(values, ('dp', 'fsdp'), pairs)  33.3 us
    unnamed x300, local copies, waits for them, and re-layouts  31.8 us
  transfers between devices with their start and end apart: 106, of which 42 were waited for; matrix products, arithmetic and copies ran while one was open for 24% of the time, Pallas kernels for 19%

profile of v2, /device:TPU:4, one launch (start us, length us, event | category | flops | bytes accessed | tf_op | source)
XLA Modules:
  0.0 739.4 jit_solution(11242581605144644056)
XLA Ops:
  20.8 21.1 %collective-permute-done.5 = bf16[2,2,256,512]{3,2,0,1:T(8,128)(2,1)S(1)} collective-permute-done((bf16[2,2,256,512]{3,2,0,1:T(8,128)(2,1)S(1)}, bf16[2,2,256,512]{3,2,0,1:T(8,128)(2,1)S(1)}, u32[]{:S(2)}, u32[]{:S(2)}) %collective-permute-start.5) | collective-permute-done | bytes 1048608 | tf_op jit(solution)/shard_map/ppermute | solution.py:438
  47.0 6.2 collective-permute-done.11.refs_6_.refs_17_
  53.2 9.1 %collective-permute-done.15 = bf16[104,2048]{1,0:T(8,128)(2,1)S(1)} collective-permute-done((bf16[104,2048]{1,0:T(8,128)(2,1)S(1)}, bf16[104,2048]{1,0:T(8,128)(2,1)S(1)}, u32[]{:S(2)}, u32[]{:S(2)}) %collective-permute-start.15) | collective-permute-done | bytes 426016 | tf_op jit(solution)/shard_map/ppermute | solution.py:438
  82.8 9.5 %collective-permute-done.16 = bf16[3,2,128,512]{3,2,0,1:T(8,128)(2,1)S(1)} collective-permute-done((bf16[3,2,128,512]{3,2,0,1:T(8,128)(2,1)S(1)}, bf16[3,2,128,512]{3,2,0,1:T(8,128)(2,1)S(1)}, u32[]{:S(2)}, u32[]{:S(2)}) %collective-permute-start.16) | collective-permute-done | bytes 786464 | tf_op jit(solution)/shard_map/ppermute | solution.py:438
  104.0 6.4 shard_map.300.refs_0_
  131.1 7.2 collective-permute-done.20
  147.4 9.2 %collective-permute-done.23 = bf16[3,2,256,512]{3,2,0,1:T(8,128)(2,1)} collective-permute-done((bf16[3,2,256,512]{3,2,0,1:T(8,128)(2,1)S(1)}, bf16[3,2,256,512]{3,2,0,1:T(8,128)(2,1)}, u32[]{:S(2)}, u32[]{:S(2)}) %collective-permute-start.23) | collective-permute-done | bytes 1572896 | tf_op jit(solution)/shard_map/ppermute | solution.py:441
  166.7 9.6 %collective-permute-done.32.refs_2_ = bf16[256,2048]{1,0:T(8,128)(2,1)S(1)} collective-permute-done((bf16[256,2048]{1,0:T(8,128)(2,1)S(1)}, bf16[256,2048]{1,0:T(8,128)(2,1)S(1)}, u32[]{:S(2)}, u32[]{:S(2)}) %collective-permute-start.32) | collective-permute-done | bytes 1048608 | tf_op jit(solution)/shard_map/ppermute | solution.py:438
  213.1 10.9 %collective-permute-done.37 = bf16[128,2048]{1,0:T(8,128)(2,1)S(1)} collective-permute-done((bf16[128,2048]{1,0:T(8,128)(2,1)S(1)}, bf16[128,2048]{1,0:T(8,128)(2,1)S(1)}, u32[]{:S(2)}, u32[]{:S(2)}) %collective-permute-start.37) | collective-permute-done | bytes 524320 | tf_op jit(solution)/shard_map/ppermute | solution.py:438
  230.3 11.3 %collective-permute-done.47 = bf16[128,2048]{1,0:T(8,128)(2,1)} collective-permute-done((bf16[128,2048]{1,0:T(8,128)(2,1)}, bf16[128,2048]{1,0:T(8,128)(2,1)}, u32[]{:S(2)}, u32[]{:S(2)}) %collective-permute-start.47) | collective-permute-done | bytes 524320 | tf_op jit(solution)/shard_map/ppermute | solution.py:441
  260.3 8.1 %fusion.15 = f32[1024,640]{1,0:T(8,128)} fusion(bf16[1024,2048]{1,0:T(8,128)(2,1)} %constant_dynamic-update-slice_fusion.9.refs_1_.refs_3_, bf16[1280,2048]{1,0:T(8,128)(2,1)} %param.34, s32[]{:T(128)S(6)} %select_n.149), kind=kOutput, calls=%fused_computation.29 | convolution fusion | flops 2684354560 | bytes 9437188 | tf_op jit(solution)/shard_map/dot_general | solution.py:29
  273.4 8.1 %multiply_convert_fusion = (bf16[1024,640]{1,0:T(8,128)(2,1)S(1)}, bf16[1024,640]{1,0:T(8,128)(2,1)S(1)}, bf16[1024,640]{1,0:T(8,128)(2,1)S(1)}) fusion(f32[1024,640]{1,0:T(8,128)} %fusion.18, f32[1024,640]{1,0:T(8,128)} %fusion.15, bf16[1024,2048]{1,0:T(8,128)(2,1)S(1)} %copy-done.131, bf16[1280,2048]{1,0:T(8,128)(2,1)} %param.35, s32[]{:T(128)S(6)} %select_n.149), kind=kOutput, calls=%fused_computation.20 | convolution fusion | flops 2700738560 | bytes 15990788 | tf_op jit(solution)/shard_map/dot_general | solution.py:29
  309.7 13.0 %shard_map.309 = bf16[4,1920,512]{2,1,0:T(8,128)(2,1)} custom-call(s32[2]{0:T(128)S(1)} %broadcast_6_place.2.place, bf16[640,1024]{1,0:T(8,128)(2,1)S(1)} %shard_map.306.refs_0_, bf16[1024,2048]{1,0:T(8,128)(2,1)} %constant_dynamic-update-slice_fusion.9.refs_1_.refs_3_, bf16[640,1024]{1,0:T(8,128)(2,1)S(1)} %shard_map.307.refs_2_, ...), custom_call_target="tpu_custom_call" | custom-call | flops 14400000000 | bytes 36000000 | tf_op jit(solution)/shard_map/pallas_call | solution.py:407
  330.1 10.1 %collective-permute-done.61 = bf16[128,2048]{1,0:T(8,128)(2,1)S(1)} collective-permute-done((bf16[128,2048]{1,0:T(8,128)(2,1)S(1)}, bf16[128,2048]{1,0:T(8,128)(2,1)S(1)}, u32[]{:S(2)}, u32[]{:S(2)}) %collective-permute-start.61) | collective-permute-done | bytes 524320 | tf_op jit(solution)/shard_map/ppermute | solution.py:438
  343.5 8.1 %shard_map.312 = (bf16[512,512]{1,0:T(8,128)(2,1)S(1)}, bf16[1024,512]{1,0:T(8,128)(2,1)S(1)}, bf16[1024,512]{1,0:T(8,128)(2,1)S(1)}) custom-call(s32[4,2]{1,0:T(4,128)S(1)} %pad_add_fusion.info, bf16[512,512]{1,0:T(8,128)(2,1)S(1)} %copy-done.33, bf16[1024,512]{1,0:T(8,128)(2,1)S(1)} %copy-done.66, bf16[1024,512]{1,0:T(8,128)(2,1)S(1)} %copy-done.64, ...), custom_call_target="tpu_custom_call" | custom-call | flops 6400000000 | bytes 16000000 | tf_op jit(solution)/shard_map/pallas_call | solution.py:129
  388.8 5.8 collective-permute-done.66
  397.8 8.0 %shard_map.319 = (bf16[512,512]{1,0:T(8,128)(2,1)S(1)}, bf16[512,512]{1,0:T(8,128)(2,1)S(1)}, bf16[512,512]{1,0:T(8,128)(2,1)S(1)}) custom-call(s32[4,2]{1,0:T(4,128)S(1)} %pad_add_fusion.info, bf16[512,512]{1,0:T(8,128)(2,1)S(1)} %copy-done.25, bf16[512,512]{1,0:T(8,128)(2,1)S(1)} %copy-done.23, bf16[512,512]{1,0:T(8,128)(2,1)S(1)} %copy-done.60, ...), custom_call_target="tpu_custom_call" | custom-call | flops 6400000000 | bytes 16000000 | tf_op jit(solution)/shard_map/pallas_call | solution.py:129
  409.6 8.7 %shard_map.326 = bf16[512,2048]{1,0:T(8,128)(2,1)} custom-call(s32[2]{0:T(128)} %copy-done.40, bf16[512,512]{1,0:T(8,128)(2,1)} %copy-done.34, bf16[512,512]{1,0:T(8,128)(2,1)} %copy-done.35, bf16[512,512]{1,0:T(8,128)(2,1)} %copy-done.36, bf16[512,2048]{1,0:T(8,128)(2,1)} %refs_3_, bf16[3,512,512]{2,1,0:T(8,128)(2,1)} %copy-done.6, ...), custom_call_target="tpu_custom_call" | custom-call | flops 7742608896 | bytes 19356520 | tf_op jit(solution)/shard_map/pallas_call | solution.py:247
  421.3 21.6 %collective-permute-done.76 = bf16[4,1024,256]{2,1,0:T(8,128)(2,1)} collective-permute-done((bf16[4,1024,256]{2,1,0:T(8,128)(2,1)}, bf16[4,1024,256]{2,1,0:T(8,128)(2,1)}, u32[]{:S(2)}, u32[]{:S(2)}) %collective-permute-start.76) | collective-permute-done | bytes 2097184 | tf_op jit(solution)/shard_map/ppermute | solution.py:542
  446.4 10.5 %shard_map.324 = bf16[1024,2048]{1,0:T(8,128)(2,1)} custom-call(s32[2]{0:T(128)} %copy-done.40, bf16[1024,512]{1,0:T(8,128)(2,1)} %copy-done.72, bf16[1024,512]{1,0:T(8,128)(2,1)} %copy-done.74, bf16[512,2048]{1,0:T(8,128)(2,1)} %refs_2_.1, bf16[3,512,512]{2,1,0:T(8,128)(2,1)} %copy-done.19, bf16[3,2,256,512]{3,2,1,0:T(8,128)(2,1)} %copy.38.refs_6_.refs_3_.refs_4_.refs_10_, ...), custom_call_target="tpu_custom_call" | custom-call | flops 9523478528 | bytes 23808696 | tf_op jit(solution)/shard_map/pallas_call | solution.py:247
  460.6 8.5 %shard_map.325 = bf16[4,1536,256]{2,1,0:T(8,128)(2,1)} custom-call(s32[2]{0:T(128)S(1)} %copy-done.42, bf16[2048,1024]{1,0:T(8,128)(2,1)} %copy-done.61, bf16[1024,512]{1,0:T(8,128)(2,1)S(1)} %copy-done.73, bf16[2048,1024]{1,0:T(8,128)(2,1)} %copy-done.61, bf16[1024,512]{1,0:T(8,128)(2,1)S(1)} %copy-done.75, bf16[512,512]{1,0:T(8,128)(2,1)S(1)} %copy-done.81, ...), custom_call_target="tpu_custom_call" | custom-call | flops 5851428352 | bytes 14628571 | tf_op jit(solution)/shard_map/pallas_call | solution.py:313
  472.5 6.6 pad_maximum_fusion.refs_1_.refs_3_
  493.4 8.5 %shard_map.322 = bf16[4,1536,256]{2,1,0:T(8,128)(2,1)} custom-call(s32[2]{0:T(128)S(1)} %copy-done.42, bf16[2048,1024]{1,0:T(8,128)(2,1)} %copy-done.61, bf16[1024,512]{1,0:T(8,128)(2,1)S(1)} %copy-done.73, bf16[2048,1024]{1,0:T(8,128)(2,1)} %copy-done.61, bf16[1024,512]{1,0:T(8,128)(2,1)S(1)} %copy-done.75, bf16[512,512]{1,0:T(8,128)(2,1)S(1)} %copy-done.81, ...), custom_call_target="tpu_custom_call" | custom-call | flops 5851428352 | bytes 14628571 | tf_op jit(solution)/shard_map/pallas_call | solution.py:313
  507.8 8.8 %collective-permute-done.72 = bf16[256,2048]{1,0:T(8,128)(2,1)S(1)} collective-permute-done((bf16[256,2048]{1,0:T(8,128)(2,1)S(1)}, bf16[256,2048]{1,0:T(8,128)(2,1)S(1)}, u32[]{:S(2)}, u32[]{:S(2)}) %collective-permute-start.72) | collective-permute-done | bytes 1048608 | tf_op jit(solution)/shard_map/ppermute | solution.py:438
  556.6 5.5 convolution_convert_fusion
  567.3 6.6 convolution_bitcast_fusion
  573.8 12.9 %collective-permute-done.87 = bf16[2,1536,256]{2,1,0:T(8,128)(2,1)} collective-permute-done((bf16[2,1536,256]{2,1,0:T(8,128)(2,1)}, bf16[2,1536,256]{2,1,0:T(8,128)(2,1)}, u32[]{:S(2)}, u32[]{:S(2)}) %collective-permute-start.87) | collective-permute-done | bytes 1572896 | tf_op jit(solution)/shard_map/ppermute | solution.py:542
  600.1 20.8 %collective-permute-done.91 = bf16[4,416,256]{2,1,0:T(8,128)(2,1)S(1)} collective-permute-done((bf16[4,416,256]{2,1,0:T(8,128)(2,1)S(1)}, bf16[4,416,256]{2,1,0:T(8,128)(2,1)S(1)}, u32[]{:S(2)}, u32[]{:S(2)}) %collective-permute-start.91) | collective-permute-done | bytes 852000 | tf_op jit(solution)/shard_map/ppermute | solution.py:542
  633.9 5.9 collective-permute-done.94
  656.0 14.4 %collective-permute-done.99 = bf16[512,256]{1,0:T(8,128)(2,1)S(1)} collective-permute-done((bf16[512,256]{1,0:T(8,128)(2,1)S(1)}, bf16[512,256]{1,0:T(8,128)(2,1)S(1)}, u32[]{:S(2)}, u32[]{:S(2)}) %collective-permute-start.99) | collective-permute-done | bytes 262176 | tf_op jit(solution)/shard_map/ppermute | solution.py:542
  670.4 9.9 %collective-permute-done.101 = bf16[1920,256]{1,0:T(8,128)(2,1)S(1)} collective-permute-done((bf16[1920,256]{1,0:T(8,128)(2,1)S(1)}, bf16[1920,256]{1,0:T(8,128)(2,1)S(1)}, u32[]{:S(2)}, u32[]{:S(2)}) %collective-permute-start.101) | collective-permute-done | bytes 983072 | tf_op jit(solution)/shard_map/ppermute | solution.py:441
  691.6 33.3 %collective-permute-done.103 = bf16[3,512,256]{2,1,0:T(8,128)(2,1)S(1)} collective-permute-done((bf16[3,512,256]{2,1,0:T(8,128)(2,1)S(1)}, bf16[3,512,256]{2,1,0:T(8,128)(2,1)S(1)}, u32[]{:S(2)}, u32[]{:S(2)}) %collective-permute-start.103) | collective-permute-done | bytes 786464 | tf_op jit(solution)/shard_map/ppermute | solution.py:592
  (669 shorter events, 377.0 us)
Async XLA Ops:
  7.2 510.4 %reduce-scatter.2.cloned.1.call-start = ((), (), s32[]{:S(2)}) async-start(), calls=%async_computation.1 | async-start | bytes 9830400 | tf_op jit(solution)/shard_map/reduce_scatter | solution.py:722
  8.7 37.4 %collective-permute-start.1 = (s32[1,2]{1,0:T(1,128)S(1)}, s32[1,2]{1,0:T(1,128)S(1)}, u32[]{:S(2)}, u32[]{:S(2)}) collective-permute-start(s32[1,2]{1,0:T(1,128)S(1)} %pad_add_fusion.1), channel_id=1, source_target_pairs={{0,1},{1,0},{2,3},{3,2},{4,5},{5,4},{6,7},{7,6},{8,9},{9,8},{10,11... | collective-permute-start | bytes 32 | tf_op jit(solution)/shard_map/ppermute | solution.py:438
  12.4 34.5 %collective-permute-start.2 = (s32[1,2]{1,0:T(1,128)S(1)}, s32[1,2]{1,0:T(1,128)S(1)}, u32[]{:S(2)}, u32[]{:S(2)}) collective-permute-start(s32[1,2]{1,0:T(1,128)S(1)} %collective-permute-done), channel_id=1, source_target_pairs={{0,1},{1,0},{2,3},{3,2},{4,5},{5,4},{6,7},{7,6},{8,9},{9,8},{10,11... | collective-permute-start | bytes 32 | tf_op jit(solution)/shard_map/ppermute | solution.py:438
  17.4 35.8 %collective-permute-start.11 = (bf16[1,2,256,512]{3,2,1,0:T(8,128)(2,1)S(1)}, bf16[1,2,256,512]{3,2,1,0:T(8,128)(2,1)S(1)}, u32[]{:S(2)}, u32[]{:S(2)}) collective-permute-start(bf16[1,2,256,512]{3,2,1,0:T(8,128)(2,1)S(1)} %maximum_bitcast_fusion.2), channel_id=1, source_target_pairs={{0,2},{1,3},{2,0},{3,1},{4,6},{5,7},{6,4},{7,5},{8,10},{9,11},{10,... | collective-permute-start | bytes 1572872 | tf_op jit(solution)/shard_map/ppermute | solution.py:438
  53.2 28.2 %collective-permute-start.8 = (bf16[3,512,512]{2,1,0:T(8,128)(2,1)S(1)}, bf16[3,512,512]{2,1,0:T(8,128)(2,1)S(1)}, u32[]{:S(2)}, u32[]{:S(2)}) collective-permute-start(bf16[3,512,512]{2,1,0:T(8,128)(2,1)S(1)} %pad_maximum_fusion.4), channel_id=1, source_target_pairs={{0,1},{1,0},{2,3},{3,2},{4,5},{5,4},{6,7},{7,6},{8,9},{9,8},{10,11... | collective-permute-start | bytes 4718600 | tf_op jit(solution)/shard_map/ppermute | solution.py:438
  81.4 35.4 %collective-permute-start.29 = (bf16[208,2048]{1,0:T(8,128)(2,1)}, bf16[208,2048]{1,0:T(8,128)(2,1)}, u32[]{:S(2)}, u32[]{:S(2)}) collective-permute-start(bf16[208,2048]{1,0:T(8,128)(2,1)} %maximum_select_fusion.2), channel_id=1, source_target_pairs={{0,4},{4,0},{8,12},{12,8},{16,20},{20,16},{24,28},{28,24},{1,5},{5... | collective-permute-start | bytes 2555912 | tf_op jit(solution)/shard_map/ppermute | solution.py:441
  120.1 36.5 %collective-permute-start.23 = (bf16[3,2,256,512]{3,2,0,1:T(8,128)(2,1)S(1)}, bf16[3,2,256,512]{3,2,0,1:T(8,128)(2,1)}, u32[]{:S(2)}, u32[]{:S(2)}) collective-permute-start(bf16[3,2,256,512]{3,2,0,1:T(8,128)(2,1)S(1)} %copy-done.90), channel_id=1, source_target_pairs={{0,4},{4,0},{8,12},{12,8},{16,20},{20,16},{24,28},{28,24},{1,5},{5... | collective-permute-start | bytes 4718600 | tf_op jit(solution)/shard_map/ppermute | solution.py:441
  122.5 36.0 %collective-permute-start.26 = (bf16[3,256,512]{2,1,0:T(8,128)(2,1)}, bf16[3,256,512]{2,1,0:T(8,128)(2,1)S(1)}, u32[]{:S(2)}, u32[]{:S(2)}) collective-permute-start(bf16[3,256,512]{2,1,0:T(8,128)(2,1)} %slice_bitcast_fusion.2), channel_id=1, source_target_pairs={{0,1},{1,0},{2,3},{3,2},{4,5},{5,4},{6,7},{7,6},{8,9},{9,8},{10,11... | collective-permute-start | bytes 2359304 | tf_op jit(solution)/shard_map/ppermute | solution.py:438
  129.7 33.4 %collective-permute-start.25 = (bf16[3,512,512]{2,1,0:T(8,128)(2,1)}, bf16[3,512,512]{2,1,0:T(8,128)(2,1)S(1)}, u32[]{:S(2)}, u32[]{:S(2)}) collective-permute-start(bf16[3,512,512]{2,1,0:T(8,128)(2,1)} %pad_maximum_fusion.5), channel_id=1, source_target_pairs={{0,1},{1,0},{2,3},{3,2},{4,5},{5,4},{6,7},{7,6},{8,9},{9,8},{10,11... | collective-permute-start | bytes 4718600 | tf_op jit(solution)/shard_map/ppermute | solution.py:438
  146.4 29.9 %collective-permute-start.32 = (bf16[256,2048]{1,0:T(8,128)(2,1)S(1)}, bf16[256,2048]{1,0:T(8,128)(2,1)S(1)}, u32[]{:S(2)}, u32[]{:S(2)}) collective-permute-start(bf16[256,2048]{1,0:T(8,128)(2,1)S(1)} %convolution_convert_fusion.3.refs_0_), channel_id=1, source_target_pairs={{0,2},{1,3},{2,0},{3,1},{4,6},{5,7},{6,4},{7,5},{8,10},{9,11},{10,... | collective-permute-start | bytes 3145736 | tf_op jit(solution)/shard_map/ppermute | solution.py:438
  394.5 48.4 %collective-permute-start.76 = (bf16[4,1024,256]{2,1,0:T(8,128)(2,1)}, bf16[4,1024,256]{2,1,0:T(8,128)(2,1)}, u32[]{:S(2)}, u32[]{:S(2)}) collective-permute-start(bf16[4,1024,256]{2,1,0:T(8,128)(2,1)} %shard_map.315), channel_id=1, source_target_pairs={{0,4},{4,0},{8,12},{12,8},{16,20},{20,16},{24,28},{28,24},{1,5},{5... | collective-permute-start | bytes 6291464 | tf_op jit(solution)/shard_map/ppermute | solution.py:542
  408.5 37.7 %collective-permute-start.69 = (bf16[512,1536]{1,0:T(8,128)(2,1)}, bf16[512,1536]{1,0:T(8,128)(2,1)}, u32[]{:S(2)}, u32[]{:S(2)}) collective-permute-start(bf16[512,1536]{1,0:T(8,128)(2,1)} %constant_dynamic-update-slice_fusion.18), channel_id=1, source_target_pairs={{0,2},{1,3},{2,0},{3,1},{4,6},{5,7},{6,4},{7,5},{8,10},{9,11},{10,... | collective-permute-start | bytes 4718600 | tf_op jit(solution)/shard_map/ppermute | solution.py:438
  409.6 61.7 %collective-permute-start.68 = (bf16[512,1536]{1,0:T(8,128)(2,1)}, bf16[512,1536]{1,0:T(8,128)(2,1)}, u32[]{:S(2)}, u32[]{:S(2)}) collective-permute-start(bf16[512,1536]{1,0:T(8,128)(2,1)} %constant_dynamic-update-slice_fusion.18), channel_id=1, source_target_pairs={{0,1},{1,0},{2,3},{3,2},{4,5},{5,4},{6,7},{7,6},{8,9},{9,8},{10,11... | collective-permute-start | bytes 4718600 | tf_op jit(solution)/shard_map/ppermute | solution.py:438
  420.7 48.5 %collective-permute-start.80 = (bf16[2,128,2048]{2,1,0:T(8,128)(2,1)}, bf16[2,128,2048]{2,1,0:T(8,128)(2,1)}, u32[]{:S(2)}, u32[]{:S(2)}) collective-permute-start(bf16[2,128,2048]{2,1,0:T(8,128)(2,1)} %slice.454), channel_id=1, source_target_pairs={{0,1},{1,0},{2,3},{3,2},{4,5},{5,4},{6,7},{7,6},{8,9},{9,8},{10,11... | collective-permute-start | bytes 3145736 | tf_op jit(solution)/shard_map/ppermute | solution.py:438
  445.4 56.6 %collective-permute-start.77 = (bf16[2,1024,256]{2,1,0:T(8,128)(2,1)}, bf16[2,1024,256]{2,1,0:T(8,128)(2,1)}, u32[]{:S(2)}, u32[]{:S(2)}) collective-permute-start(bf16[2,1024,256]{2,1,0:T(8,128)(2,1)} %add_convert_fusion.3), channel_id=1, source_target_pairs={{0,8},{4,12},{8,0},{12,4},{16,24},{20,28},{24,16},{28,20},{1,9},{5... | collective-permute-start | bytes 3145736 | tf_op jit(solution)/shard_map/ppermute | solution.py:542
  460.2 29.6 %collective-permute-start.71 = (bf16[2,256,2048]{2,1,0:T(8,128)(2,1)}, bf16[2,256,2048]{2,1,0:T(8,128)(2,1)S(1)}, u32[]{:S(2)}, u32[]{:S(2)}) collective-permute-start(bf16[2,256,2048]{2,1,0:T(8,128)(2,1)} %slice.439), channel_id=1, source_target_pairs={{0,1},{1,0},{2,3},{3,2},{4,5},{5,4},{6,7},{7,6},{8,9},{9,8},{10,11... | collective-permute-start | bytes 6291464 | tf_op jit(solution)/shard_map/ppermute | solution.py:438
  469.1 75.3 %collective-permute-start.75 = (bf16[4,1536,256]{2,1,0:T(8,128)(2,1)}, bf16[4,1536,256]{2,1,0:T(8,128)(2,1)}, u32[]{:S(2)}, u32[]{:S(2)}) collective-permute-start(bf16[4,1536,256]{2,1,0:T(8,128)(2,1)} %shard_map.325), channel_id=1, source_target_pairs={{0,4},{4,0},{8,12},{12,8},{16,20},{20,16},{24,28},{28,24},{1,5},{5... | collective-permute-start | bytes 9437192 | tf_op jit(solution)/shard_map/ppermute | solution.py:542
  471.3 46.3 %collective-permute-start.81 = (bf16[128,2048]{1,0:T(8,128)(2,1)S(1)}, bf16[128,2048]{1,0:T(8,128)(2,1)}, u32[]{:S(2)}, u32[]{:S(2)}) collective-permute-start(bf16[128,2048]{1,0:T(8,128)(2,1)S(1)} %fusion.23), channel_id=1, source_target_pairs={{0,2},{1,3},{2,0},{3,1},{4,6},{5,7},{6,4},{7,5},{8,10},{9,11},{10,... | collective-permute-start | bytes 1572872 | tf_op jit(solution)/shard_map/ppermute | solution.py:438
  483.6 55.6 %collective-permute-start.79 = (bf16[4,512,256]{2,1,0:T(8,128)(2,1)}, bf16[4,512,256]{2,1,0:T(8,128)(2,1)}, u32[]{:S(2)}, u32[]{:S(2)}) collective-permute-start(bf16[4,512,256]{2,1,0:T(8,128)(2,1)} %shard_map.321), channel_id=1, source_target_pairs={{0,8},{4,12},{8,0},{12,4},{16,24},{20,28},{24,16},{28,20},{1,9},{5... | collective-permute-start | bytes 3145736 | tf_op jit(solution)/shard_map/ppermute | solution.py:542
  504.2 37.5 %collective-permute-start.78 = (bf16[1024,256]{1,0:T(8,128)(2,1)}, bf16[1024,256]{1,0:T(8,128)(2,1)}, u32[]{:S(2)}, u32[]{:S(2)}) collective-permute-start(bf16[1024,256]{1,0:T(8,128)(2,1)} %fusion.41), channel_id=1, source_target_pairs={{0,16},{4,20},{8,24},{12,28},{16,0},{20,4},{24,8},{28,12},{1,17},{... | collective-permute-start | bytes 1572872 | tf_op jit(solution)/shard_map/ppermute | solution.py:542
  548.0 48.8 %collective-permute-start.86 = (bf16[4,1024,256]{2,1,0:T(8,128)(2,1)}, bf16[4,1024,256]{2,1,0:T(8,128)(2,1)}, u32[]{:S(2)}, u32[]{:S(2)}) collective-permute-start(bf16[4,1024,256]{2,1,0:T(8,128)(2,1)} %shard_map.320), channel_id=1, source_target_pairs={{0,4},{4,0},{8,12},{12,8},{16,20},{20,16},{24,28},{28,24},{1,5},{5... | collective-permute-start | bytes 6291464 | tf_op jit(solution)/shard_map/ppermute | solution.py:542
  549.1 37.6 %collective-permute-start.87 = (bf16[2,1536,256]{2,1,0:T(8,128)(2,1)}, bf16[2,1536,256]{2,1,0:T(8,128)(2,1)}, u32[]{:S(2)}, u32[]{:S(2)}) collective-permute-start(bf16[2,1536,256]{2,1,0:T(8,128)(2,1)} %add_convert_fusion.1), channel_id=1, source_target_pairs={{0,8},{4,12},{8,0},{12,4},{16,24},{20,28},{24,16},{28,20},{1,9},{5... | collective-permute-start | bytes 4718600 | tf_op jit(solution)/shard_map/ppermute | solution.py:542
  564.6 56.2 %collective-permute-start.85 = (bf16[4,128,2048]{2,1,0:T(8,128)(2,1)}, bf16[4,128,2048]{2,1,0:T(8,128)(2,1)}, u32[]{:S(2)}, u32[]{:S(2)}) collective-permute-start(bf16[4,128,2048]{2,1,0:T(8,128)(2,1)} %slice.461), channel_id=1, source_target_pairs={{0,1},{1,0},{2,3},{3,2},{4,5},{5,4},{6,7},{7,6},{8,9},{9,8},{10,11... | collective-permute-start | bytes 6291464 | tf_op jit(solution)/shard_map/ppermute | solution.py:438
  564.7 61.6 %collective-permute-start.93 = (bf16[2,512,256]{2,1,0:T(8,128)(2,1)}, bf16[2,512,256]{2,1,0:T(8,128)(2,1)S(1)}, u32[]{:S(2)}, u32[]{:S(2)}) collective-permute-start(bf16[2,512,256]{2,1,0:T(8,128)(2,1)} %add_convert_fusion.6), channel_id=1, source_target_pairs={{0,4},{4,0},{8,12},{12,8},{16,20},{20,16},{24,28},{28,24},{1,5},{5... | collective-permute-start | bytes 1572872 | tf_op jit(solution)/shard_map/ppermute | solution.py:542
  565.6 55.2 %collective-permute-start.91 = (bf16[4,416,256]{2,1,0:T(8,128)(2,1)S(1)}, bf16[4,416,256]{2,1,0:T(8,128)(2,1)S(1)}, u32[]{:S(2)}, u32[]{:S(2)}) collective-permute-start(bf16[4,416,256]{2,1,0:T(8,128)(2,1)S(1)} %shard_map.329), channel_id=1, source_target_pairs={{0,8},{4,12},{8,0},{12,4},{16,24},{20,28},{24,16},{28,20},{1,9},{5... | collective-permute-start | bytes 2555912 | tf_op jit(solution)/shard_map/ppermute | solution.py:542
  588.6 63.1 %collective-permute-start.100 = (bf16[1536,256]{1,0:T(8,128)(2,1)S(1)}, bf16[1536,256]{1,0:T(8,128)(2,1)S(1)}, u32[]{:S(2)}, u32[]{:S(2)}) collective-permute-start(bf16[1536,256]{1,0:T(8,128)(2,1)S(1)} %fusion.37), channel_id=1, source_target_pairs={{0,16},{4,20},{8,24},{12,28},{16,0},{20,4},{24,8},{28,12},{1,17},{... | collective-permute-start | bytes 2359304 | tf_op jit(solution)/shard_map/ppermute | solution.py:542
  598.3 49.5 %collective-permute-start.90 = (bf16[2,1024,256]{2,1,0:T(8,128)(2,1)S(1)}, bf16[2,1024,256]{2,1,0:T(8,128)(2,1)S(1)}, u32[]{:S(2)}, u32[]{:S(2)}) collective-permute-start(bf16[2,1024,256]{2,1,0:T(8,128)(2,1)S(1)} %add_convert_fusion.2), channel_id=1, source_target_pairs={{0,8},{4,12},{8,0},{12,4},{16,24},{20,28},{24,16},{28,20},{1,9},{5... | collective-permute-start | bytes 3145736 | tf_op jit(solution)/shard_map/ppermute | solution.py:542
  645.3 84.5 %collective-permute-start.102 = (bf16[128,2048]{1,0:T(8,128)(2,1)S(1)}, bf16[128,2048]{1,0:T(8,128)(2,1)S(1)}, u32[]{:S(2)}, u32[]{:S(2)}) collective-permute-start(bf16[128,2048]{1,0:T(8,128)(2,1)S(1)} %pad_maximum_fusion.14), channel_id=1, source_target_pairs={{0,4},{4,0},{8,12},{12,8},{16,20},{20,16},{24,28},{28,24},{1,5},{5... | collective-permute-start | bytes 1572872 | tf_op jit(solution)/shard_map/ppermute | solution.py:441
  646.6 42.0 %collective-permute-start.89 = (bf16[128,2048]{1,0:T(8,128)(2,1)S(1)}, bf16[128,2048]{1,0:T(8,128)(2,1)S(1)}, u32[]{:S(2)}, u32[]{:S(2)}) collective-permute-start(bf16[128,2048]{1,0:T(8,128)(2,1)S(1)} %pad_maximum_fusion.13), channel_id=1, source_target_pairs={{0,2},{1,3},{2,0},{3,1},{4,6},{5,7},{6,4},{7,5},{8,10},{9,11},{10,... | collective-permute-start | bytes 1572872 | tf_op jit(solution)/shard_map/ppermute | solution.py:438
  649.0 38.2 %collective-permute-start.98 = (bf16[1024,256]{1,0:T(8,128)(2,1)S(1)}, bf16[1024,256]{1,0:T(8,128)(2,1)S(1)}, u32[]{:S(2)}, u32[]{:S(2)}) collective-permute-start(bf16[1024,256]{1,0:T(8,128)(2,1)S(1)} %fusion.42), channel_id=1, source_target_pairs={{0,16},{4,20},{8,24},{12,28},{16,0},{20,4},{24,8},{28,12},{1,17},{... | collective-permute-start | bytes 1572872 | tf_op jit(solution)/shard_map/ppermute | solution.py:542
  651.9 28.5 %collective-permute-start.101 = (bf16[1920,256]{1,0:T(8,128)(2,1)S(1)}, bf16[1920,256]{1,0:T(8,128)(2,1)S(1)}, u32[]{:S(2)}, u32[]{:S(2)}) collective-permute-start(bf16[1920,256]{1,0:T(8,128)(2,1)S(1)} %get-tuple-element.271), channel_id=1, source_target_pairs={{0,4},{4,0},{8,12},{12,8},{16,20},{20,16},{24,28},{28,24},{1,5},{5... | collective-permute-start | bytes 2949128 | tf_op jit(solution)/shard_map/ppermute | solution.py:441
  680.3 44.6 %collective-permute-start.103 = (bf16[3,512,256]{2,1,0:T(8,128)(2,1)S(1)}, bf16[3,512,256]{2,1,0:T(8,128)(2,1)S(1)}, u32[]{:S(2)}, u32[]{:S(2)}) collective-permute-start(bf16[3,512,256]{2,1,0:T(8,128)(2,1)S(1)} %pad_maximum_fusion.8), channel_id=1, source_target_pairs={{0,0},{1,8},{2,16},{3,24},{4,4},{5,12},{6,20},{7,28},{8,1},{9,9},{... | collective-permute-start | bytes 2359304 | tf_op jit(solution)/shard_map/ppermute | solution.py:592
  (216 other events, 2695.4 us)
Sparse Core Ops, SparseCore 0:
  322.9 143.4 reduce-scatter.1

commit v3 on v2

--- a/solution.py
+++ b/solution.py
@@ -648,8 +648,6 @@
         cross_own = (c_key, c_value, c_query)
         cross_ready = after(cross_own, patch_part, value_near)
         cross_part = swap(sent_parts(cross_ready, f, 2 * x + z, 4), 2)
-        cross_near = pick(z, cross_part, hop(cross_part, 1), 2)
-        cross_far = across(cross_near)
         self_mate = mate_parts((w_query, w_key, w_value), f)
         first_blocks = gather_blocks(first, after(first_chip, pair_far))
         info = jnp.concatenate([info, swap(info, 1), chip_info, swap(chip_info, 1)], axis=0)
@@ -658,8 +656,11 @@
         queries = to_heads(place, first_blocks, query_w)
         keys_all = to_heads(place, first_blocks, key_w)
         values_all = to_heads(place, first_blocks, value_w)
+        cross_part = after(cross_part, values_all)
+        cross_near = pick(z, cross_part, hop(cross_part, 1), 2)
+        cross_far = across(cross_near)
         mixed = attend(info, queries, keys_all, values_all, slot, slot, width, True)
-        own, other = core_sum(low(nn(after(mixed, cross_near, patch_half), w_out)))
+        own, other = core_sum(low(nn(mixed, w_out)))
         cross_mate = mate_parts(after(cross_own, other), f)
         sent_out = other
         other = swap(other, 2)
@@ -768,26 +769,26 @@
         self_part = from_heads(place, (grad_q, grad_k, grad_v), (query_w, key_w, value_w))
         own, other = core_sum(self_part)
         other = swap(other, 2)
-        cross_one = sum_cross.add(1, self_part)
+        context_part = from_heads(
+            place, (after(grad_ck, self_part), grad_cv), (cross_key_w, cross_value_w)
+        )
+        context_own, context_other = core_sum(context_part)
+        context_other = swap(context_other, 2)
+        cross_one = sum_cross.add(1, context_part)
         sum_context = Sum(
             place,
             (
                 ("columns", context_turned, grad_ck),
                 ("columns", context_turned, grad_cv),
-                ("rows", mixed_turned, grad_self_all),
+                ("rows", after(mixed_turned, heads_chip), grad_self_all),
             ),
             (0, 1, 2),
         )
-        context_part = from_heads(
-            place, (after(grad_ck, heads_chip), grad_cv), (cross_key_w, cross_value_w)
-        )
         grad_first = own + after(
-            other, sum_context.send(), context_part, hidden_grads, heads_chip
+            other, sum_context.send(), cross_one, hidden_grads
         ).astype(F32)
         grad_norm, gain_first = norm_back(inputs, norm_gains[0], grad_first)
         tokens_grad = (grad_after_self + grad_norm)[None]
-        context_own, context_other = core_sum(context_part)
-        context_other = swap(context_other, 2)
         gains = jnp.stack([gain_first, gain_second, gain_third])
         heads_all = jnp.stack([heads, swap(heads, 1), heads_chip, swap(heads_chip, 1)])
         sum_self = Sum(

time: 747 us -> 766 us (1.025)
  waiting for transfers between devices: 290 us -> 309 us
    ppermute x71, waiting for transfers between devices: 133 us -> 143 us  [swap(): return lax.ppermute(values, 'fsdp', [(i, i ^ r) for i in range(fsdp)])]
    ppermute x13, waiting for transfers between devices: 39.3 us -> 47.5 us  [across(): return lax.ppermute(values, 'dp', [(i, i ^ 1) for i in range(dp)])]
    unnamed x300 -> x314, local copies, waits for them, and re-layouts: 31.8 us -> 35.8 us
  transfers between devices with their start and end apart: 106 -> 106, of which waited for: 42 -> 43; matrix products, arithmetic and copies ran while one was open for 24% -> 23% of each run, Pallas kernels for 19% -> 19%
where the time goes in v3:
time: 766 us; the launch traced here: 758 us
  waiting for transfers between devices  309 us (40%)
  Pallas kernels  142 us (19%)
  starting transfers between devices  85.4 us (11%)
  other arithmetic  79.9 us (10%)
  local copies, waits for them, and re-layouts  75.8 us (10%)
  matrix products  47.7 us (6%)
  between operations  18.4 us (2%)
    ppermute x71, waiting for transfers between devices, swap(): return lax.ppermute(values, 'fsdp', [(i, i ^ r) for i in range(fsdp)])  143 us
    ppermute x20, waiting for transfers between devices, hop(): return lax.ppermute(values, 'dp', [(i, i ^ 1 << bit) for i in range(dp)])  84.9 us
    pallas_call x10, Pallas kernels, half_grads(): pl.pallas_call(half_kernel, out_shape=jax.ShapeDtypeStruct((4, rows, wide...  48.8 us
    dot_general x12, matrix products, dot(): lax.dot_general(left, right, (((left_dim,), (right_dim,)), ((), ())), pre...  47.7 us
    ppermute x13, waiting for transfers between devices, across(): return lax.ppermute(values, 'dp', [(i, i ^ 1) for i in range(dp)])  47.5 us
    ppermute x71, starting transfers between devices, swap(): return lax.ppermute(values, 'fsdp', [(i, i ^ r) for i in range(fsdp)])  40.7 us
    unnamed x314, local copies, waits for them, and re-layouts  35.8 us
    ppermute x1, waiting for transfers between devices, place_columns(): return lax.ppermute(values, ('dp', 'fsdp'), pairs)  33.3 us
  transfers between devices with their start and end apart: 106, of which 43 were waited for; matrix products, arithmetic and copies ran while one was open for 23% of the time, Pallas kernels for 19%

profile of v3, /device:TPU:4, one launch (start us, length us, event | category | flops | bytes accessed | tf_op | source)
XLA Modules:
  0.0 757.8 jit_solution(9917720264341278429)
XLA Ops:
  22.7 18.4 %collective-permute-done.5 = bf16[2,2,256,512]{3,2,0,1:T(8,128)(2,1)S(1)} collective-permute-done((bf16[2,2,256,512]{3,2,0,1:T(8,128)(2,1)S(1)}, bf16[2,2,256,512]{3,2,0,1:T(8,128)(2,1)S(1)}, u32[]{:S(2)}, u32[]{:S(2)}) %collective-permute-start.5) | collective-permute-done | bytes 1048608 | tf_op jit(solution)/shard_map/ppermute | solution.py:438
  43.5 20.1 %collective-permute-done.11.refs_6_.refs_17_ = bf16[1,2,256,512]{3,2,1,0:T(8,128)(2,1)S(1)} collective-permute-done((bf16[1,2,256,512]{3,2,1,0:T(8,128)(2,1)S(1)}, bf16[1,2,256,512]{3,2,1,0:T(8,128)(2,1)S(1)}, u32[]{:S(2)}, u32[]{:S(2)}) %collective-permute-start.11) | collective-permute-done | bytes 524320 | tf_op jit(solution)/shard_map/ppermute | solution.py:438
  76.5 10.1 %collective-permute-done.6 = bf16[2,2,256,512]{3,2,0,1:T(8,128)(2,1)S(1)} collective-permute-done((bf16[2,2,256,512]{3,2,0,1:T(8,128)(2,1)S(1)}, bf16[2,2,256,512]{3,2,0,1:T(8,128)(2,1)S(1)}, u32[]{:S(2)}, u32[]{:S(2)}) %collective-permute-start.6) | collective-permute-done | bytes 1048608 | tf_op jit(solution)/shard_map/ppermute | solution.py:441
  90.2 10.7 %collective-permute-done.12.refs_7_.refs_18_ = bf16[1,2,256,512]{3,2,1,0:T(8,128)(2,1)S(1)} collective-permute-done((bf16[1,2,256,512]{3,2,1,0:T(8,128)(2,1)S(1)}, bf16[1,2,256,512]{3,2,1,0:T(8,128)(2,1)S(1)}, u32[]{:S(2)}, u32[]{:S(2)}) %collective-permute-start.12) | collective-permute-done | bytes 524320 | tf_op jit(solution)/shard_map/ppermute | solution.py:441
  122.1 6.4 shard_map.300.refs_0_
  153.9 7.9 %collective-permute-done.16 = bf16[128,2048]{1,0:T(8,128)(2,1)S(1)} collective-permute-done((bf16[128,2048]{1,0:T(8,128)(2,1)S(1)}, bf16[128,2048]{1,0:T(8,128)(2,1)S(1)}, u32[]{:S(2)}, u32[]{:S(2)}) %collective-permute-start.16) | collective-permute-done | bytes 524320 | tf_op jit(solution)/shard_map/ppermute | solution.py:438
  169.5 8.8 %collective-permute-done.18.refs_2_ = bf16[128,2048]{1,0:T(8,128)(2,1)S(1)} collective-permute-done((bf16[128,2048]{1,0:T(8,128)(2,1)S(1)}, bf16[128,2048]{1,0:T(8,128)(2,1)S(1)}, u32[]{:S(2)}, u32[]{:S(2)}) %collective-permute-start.18) | collective-permute-done | bytes 524320 | tf_op jit(solution)/shard_map/ppermute | solution.py:438
  190.0 10.4 %collective-permute-done.32.refs_2_ = bf16[256,2048]{1,0:T(8,128)(2,1)S(1)} collective-permute-done((bf16[256,2048]{1,0:T(8,128)(2,1)S(1)}, bf16[256,2048]{1,0:T(8,128)(2,1)S(1)}, u32[]{:S(2)}, u32[]{:S(2)}) %collective-permute-start.32) | collective-permute-done | bytes 1048608 | tf_op jit(solution)/shard_map/ppermute | solution.py:438
  237.8 10.6 %collective-permute-done.37 = bf16[128,2048]{1,0:T(8,128)(2,1)S(1)} collective-permute-done((bf16[128,2048]{1,0:T(8,128)(2,1)S(1)}, bf16[128,2048]{1,0:T(8,128)(2,1)S(1)}, u32[]{:S(2)}, u32[]{:S(2)}) %collective-permute-start.37) | collective-permute-done | bytes 524320 | tf_op jit(solution)/shard_map/ppermute | solution.py:438
  255.0 10.9 %collective-permute-done.47 = bf16[128,2048]{1,0:T(8,128)(2,1)} collective-permute-done((bf16[128,2048]{1,0:T(8,128)(2,1)}, bf16[128,2048]{1,0:T(8,128)(2,1)}, u32[]{:S(2)}, u32[]{:S(2)}) %collective-permute-start.47) | collective-permute-done | bytes 524320 | tf_op jit(solution)/shard_map/ppermute | solution.py:441
  285.1 8.1 %fusion.15 = f32[1024,640]{1,0:T(8,128)} fusion(bf16[1024,2048]{1,0:T(8,128)(2,1)} %constant_dynamic-update-slice_fusion.9.refs_1_.refs_3_, bf16[1280,2048]{1,0:T(8,128)(2,1)} %param.34, s32[]{:T(128)S(6)} %select_n.149), kind=kOutput, calls=%fused_computation.29 | convolution fusion | flops 2684354560 | bytes 9437188 | tf_op jit(solution)/shard_map/dot_general | solution.py:29
  298.2 8.1 %multiply_convert_fusion = (bf16[1024,640]{1,0:T(8,128)(2,1)S(1)}, bf16[1024,640]{1,0:T(8,128)(2,1)S(1)}, bf16[1024,640]{1,0:T(8,128)(2,1)S(1)}) fusion(f32[1024,640]{1,0:T(8,128)} %fusion.18, f32[1024,640]{1,0:T(8,128)} %fusion.15, bf16[1024,2048]{1,0:T(8,128)(2,1)S(1)} %copy-done.138, bf16[1280,2048]{1,0:T(8,128)(2,1)} %param.35, s32[]{:T(128)S(6)} %select_n.149), kind=kOutput, calls=%fused_computation.20 | convolution fusion | flops 2700738560 | bytes 15990788 | tf_op jit(solution)/shard_map/dot_general | solution.py:29
  324.5 5.8 collective-permute-done.58
  333.9 13.1 %shard_map.309 = bf16[4,1920,512]{2,1,0:T(8,128)(2,1)} custom-call(s32[2]{0:T(128)S(1)} %broadcast_6_place.2.place, bf16[640,1024]{1,0:T(8,128)(2,1)S(1)} %shard_map.306.refs_0_, bf16[1024,2048]{1,0:T(8,128)(2,1)} %constant_dynamic-update-slice_fusion.9.refs_1_.refs_3_, bf16[640,1024]{1,0:T(8,128)(2,1)S(1)} %shard_map.307.refs_2_, ...), custom_call_target="tpu_custom_call" | custom-call | flops 14400000000 | bytes 36000000 | tf_op jit(solution)/shard_map/pallas_call | solution.py:407
  354.7 9.7 %collective-permute-done.61 = bf16[128,2048]{1,0:T(8,128)(2,1)S(1)} collective-permute-done((bf16[128,2048]{1,0:T(8,128)(2,1)S(1)}, bf16[128,2048]{1,0:T(8,128)(2,1)S(1)}, u32[]{:S(2)}, u32[]{:S(2)}) %collective-permute-start.61) | collective-permute-done | bytes 524320 | tf_op jit(solution)/shard_map/ppermute | solution.py:438
  367.7 8.1 %shard_map.312 = (bf16[512,512]{1,0:T(8,128)(2,1)S(1)}, bf16[1024,512]{1,0:T(8,128)(2,1)S(1)}, bf16[1024,512]{1,0:T(8,128)(2,1)S(1)}) custom-call(s32[4,2]{1,0:T(4,128)S(1)} %pad_add_fusion.info, bf16[512,512]{1,0:T(8,128)(2,1)S(1)} %copy-done.34, bf16[1024,512]{1,0:T(8,128)(2,1)S(1)} %copy-done.70, bf16[1024,512]{1,0:T(8,128)(2,1)S(1)} %copy-done.68, ...), custom_call_target="tpu_custom_call" | custom-call | flops 6400000000 | bytes 16000000 | tf_op jit(solution)/shard_map/pallas_call | solution.py:129
  422.1 7.8 %shard_map.319 = (bf16[512,512]{1,0:T(8,128)(2,1)S(1)}, bf16[512,512]{1,0:T(8,128)(2,1)S(1)}, bf16[512,512]{1,0:T(8,128)(2,1)S(1)}) custom-call(s32[4,2]{1,0:T(4,128)S(1)} %pad_add_fusion.info, bf16[512,512]{1,0:T(8,128)(2,1)S(1)} %copy-done.26, bf16[512,512]{1,0:T(8,128)(2,1)S(1)} %copy-done.24, bf16[512,512]{1,0:T(8,128)(2,1)S(1)} %copy-done.64, ...), custom_call_target="tpu_custom_call" | custom-call | flops 6400000000 | bytes 16000000 | tf_op jit(solution)/shard_map/pallas_call | solution.py:129
  432.2 8.8 %shard_map.324 = bf16[512,2048]{1,0:T(8,128)(2,1)} custom-call(s32[2]{0:T(128)} %copy-done.44, bf16[512,512]{1,0:T(8,128)(2,1)} %copy-done.39, bf16[512,512]{1,0:T(8,128)(2,1)} %copy-done.37, bf16[512,512]{1,0:T(8,128)(2,1)} %copy-done.35, bf16[512,2048]{1,0:T(8,128)(2,1)} %refs_3_, bf16[3,512,512]{2,1,0:T(8,128)(2,1)} %copy-done.6, ...), custom_call_target="tpu_custom_call" | custom-call | flops 7742608896 | bytes 19356520 | tf_op jit(solution)/shard_map/pallas_call | solution.py:247
  445.2 10.5 %shard_map.325 = bf16[1024,2048]{1,0:T(8,128)(2,1)} custom-call(s32[2]{0:T(128)} %copy-done.44, bf16[1024,512]{1,0:T(8,128)(2,1)} %copy-done.76, bf16[1024,512]{1,0:T(8,128)(2,1)} %copy-done.78, bf16[512,2048]{1,0:T(8,128)(2,1)} %refs_2_.1, bf16[3,512,512]{2,1,0:T(8,128)(2,1)} %copy-done.20, bf16[3,2,256,512]{3,2,1,0:T(8,128)(2,1)} %copy.38.refs_6_.refs_3_.refs_4_.refs_10_, ...), custom_call_target="tpu_custom_call" | custom-call | flops 9523478528 | bytes 23808696 | tf_op jit(solution)/shard_map/pallas_call | solution.py:247
  459.9 7.2 collective-permute-done.76
  471.3 9.1 %collective-permute-done.69 = bf16[512,1536]{1,0:T(8,128)(2,1)} collective-permute-done((bf16[512,1536]{1,0:T(8,128)(2,1)}, bf16[512,1536]{1,0:T(8,128)(2,1)}, u32[]{:S(2)}, u32[]{:S(2)}) %collective-permute-start.69) | collective-permute-done | bytes 1572896 | tf_op jit(solution)/shard_map/ppermute | solution.py:438
  483.4 8.4 %shard_map.326 = bf16[4,1536,256]{2,1,0:T(8,128)(2,1)} custom-call(s32[2]{0:T(128)S(1)} %copy-done.46, bf16[2048,1024]{1,0:T(8,128)(2,1)} %copy-done.65, bf16[1024,512]{1,0:T(8,128)(2,1)S(1)} %copy-done.77, bf16[2048,1024]{1,0:T(8,128)(2,1)} %copy-done.65, bf16[1024,512]{1,0:T(8,128)(2,1)S(1)} %copy-done.79, bf16[512,512]{1,0:T(8,128)(2,1)S(1)} %copy-done.85, ...), custom_call_target="tpu_custom_call" | custom-call | flops 5851428352 | bytes 14628571 | tf_op jit(solution)/shard_map/pallas_call | solution.py:313
  494.3 6.5 pad_maximum_fusion.refs_1_.refs_3_
  512.0 8.4 %shard_map.322 = bf16[4,1536,256]{2,1,0:T(8,128)(2,1)} custom-call(s32[2]{0:T(128)S(1)} %copy-done.46, bf16[2048,1024]{1,0:T(8,128)(2,1)} %copy-done.65, bf16[1024,512]{1,0:T(8,128)(2,1)S(1)} %copy-done.77, bf16[2048,1024]{1,0:T(8,128)(2,1)} %copy-done.65, bf16[1024,512]{1,0:T(8,128)(2,1)S(1)} %copy-done.79, bf16[512,512]{1,0:T(8,128)(2,1)S(1)} %copy-done.85, ...), custom_call_target="tpu_custom_call" | custom-call | flops 5851428352 | bytes 14628571 | tf_op jit(solution)/shard_map/pallas_call | solution.py:313
  545.6 16.5 %collective-permute-done.78 = bf16[1024,256]{1,0:T(8,128)(2,1)S(1)} collective-permute-done((bf16[1024,256]{1,0:T(8,128)(2,1)S(1)}, bf16[1024,256]{1,0:T(8,128)(2,1)S(1)}, u32[]{:S(2)}, u32[]{:S(2)}) %collective-permute-start.78) | collective-permute-done | bytes 524320 | tf_op jit(solution)/shard_map/ppermute | solution.py:542
  587.3 6.6 convolution_bitcast_fusion
  593.9 12.3 %collective-permute-done.87 = bf16[2,1536,256]{2,1,0:T(8,128)(2,1)} collective-permute-done((bf16[2,1536,256]{2,1,0:T(8,128)(2,1)}, bf16[2,1536,256]{2,1,0:T(8,128)(2,1)}, u32[]{:S(2)}, u32[]{:S(2)}) %collective-permute-start.87) | collective-permute-done | bytes 1572896 | tf_op jit(solution)/shard_map/ppermute | solution.py:542
  609.1 7.2 collective-permute-done.86
  617.9 20.6 %collective-permute-done.91 = bf16[4,416,256]{2,1,0:T(8,128)(2,1)S(1)} collective-permute-done((bf16[4,416,256]{2,1,0:T(8,128)(2,1)S(1)}, bf16[4,416,256]{2,1,0:T(8,128)(2,1)S(1)}, u32[]{:S(2)}, u32[]{:S(2)}) %collective-permute-start.91) | collective-permute-done | bytes 852000 | tf_op jit(solution)/shard_map/ppermute | solution.py:542
  674.4 14.4 %collective-permute-done.99 = bf16[512,256]{1,0:T(8,128)(2,1)S(1)} collective-permute-done((bf16[512,256]{1,0:T(8,128)(2,1)S(1)}, bf16[512,256]{1,0:T(8,128)(2,1)S(1)}, u32[]{:S(2)}, u32[]{:S(2)}) %collective-permute-start.99) | collective-permute-done | bytes 262176 | tf_op jit(solution)/shard_map/ppermute | solution.py:542
  688.8 9.9 %collective-permute-done.101 = bf16[1920,256]{1,0:T(8,128)(2,1)S(1)} collective-permute-done((bf16[1920,256]{1,0:T(8,128)(2,1)S(1)}, bf16[1920,256]{1,0:T(8,128)(2,1)S(1)}, u32[]{:S(2)}, u32[]{:S(2)}) %collective-permute-start.101) | collective-permute-done | bytes 983072 | tf_op jit(solution)/shard_map/ppermute | solution.py:441
  710.0 33.3 %collective-permute-done.103 = bf16[3,512,256]{2,1,0:T(8,128)(2,1)S(1)} collective-permute-done((bf16[3,512,256]{2,1,0:T(8,128)(2,1)S(1)}, bf16[3,512,256]{2,1,0:T(8,128)(2,1)S(1)}, u32[]{:S(2)}, u32[]{:S(2)}) %collective-permute-start.103) | collective-permute-done | bytes 786464 | tf_op jit(solution)/shard_map/ppermute | solution.py:592
  (683 shorter events, 384.7 us)
Async XLA Ops:
  7.2 518.2 %reduce-scatter.2.cloned.1.call-start = ((), (), s32[]{:S(2)}) async-start(), calls=%async_computation.1 | async-start | bytes 9830400 | tf_op jit(solution)/shard_map/reduce_scatter | solution.py:723
  16.6 70.0 %collective-permute-start.4 = (bf16[128,2048]{1,0:T(8,128)(2,1)S(1)}, bf16[128,2048]{1,0:T(8,128)(2,1)S(1)}, u32[]{:S(2)}, u32[]{:S(2)}) collective-permute-start(bf16[128,2048]{1,0:T(8,128)(2,1)S(1)} %multiply_convert_fusion.5.refs_0_), channel_id=1, source_target_pairs={{0,2},{1,3},{2,0},{3,1},{4,6},{5,7},{6,4},{7,5},{8,10},{9,11},{10,... | collective-permute-start | bytes 1572872 | tf_op jit(solution)/shard_map/ppermute | solution.py:438
  17.6 70.7 %collective-permute-start.3 = (bf16[128,2048]{1,0:T(8,128)(2,1)S(1)}, bf16[128,2048]{1,0:T(8,128)(2,1)S(1)}, u32[]{:S(2)}, u32[]{:S(2)}) collective-permute-start(bf16[128,2048]{1,0:T(8,128)(2,1)S(1)} %multiply_convert_fusion.5.refs_0_), channel_id=1, source_target_pairs={{0,1},{1,0},{2,3},{3,2},{4,5},{5,4},{6,7},{7,6},{8,9},{9,8},{10,11... | collective-permute-start | bytes 1572872 | tf_op jit(solution)/shard_map/ppermute | solution.py:438
  17.7 45.9 %collective-permute-start.11 = (bf16[1,2,256,512]{3,2,1,0:T(8,128)(2,1)S(1)}, bf16[1,2,256,512]{3,2,1,0:T(8,128)(2,1)S(1)}, u32[]{:S(2)}, u32[]{:S(2)}) collective-permute-start(bf16[1,2,256,512]{3,2,1,0:T(8,128)(2,1)S(1)} %maximum_bitcast_fusion.2), channel_id=1, source_target_pairs={{0,2},{1,3},{2,0},{3,1},{4,6},{5,7},{6,4},{7,5},{8,10},{9,11},{10,... | collective-permute-start | bytes 1572872 | tf_op jit(solution)/shard_map/ppermute | solution.py:438
  22.4 80.6 %collective-permute-start.8 = (bf16[3,512,512]{2,1,0:T(8,128)(2,1)S(1)}, bf16[3,512,512]{2,1,0:T(8,128)(2,1)S(1)}, u32[]{:S(2)}, u32[]{:S(2)}) collective-permute-start(bf16[3,512,512]{2,1,0:T(8,128)(2,1)S(1)} %pad_maximum_fusion.4), channel_id=1, source_target_pairs={{0,1},{1,0},{2,3},{3,2},{4,5},{5,4},{6,7},{7,6},{8,9},{9,8},{10,11... | collective-permute-start | bytes 4718600 | tf_op jit(solution)/shard_map/ppermute | solution.py:438
  103.0 29.7 %collective-permute-start.29 = (bf16[208,2048]{1,0:T(8,128)(2,1)}, bf16[208,2048]{1,0:T(8,128)(2,1)}, u32[]{:S(2)}, u32[]{:S(2)}) collective-permute-start(bf16[208,2048]{1,0:T(8,128)(2,1)} %maximum_select_fusion.2), channel_id=1, source_target_pairs={{0,4},{4,0},{8,12},{12,8},{16,20},{20,16},{24,28},{28,24},{1,5},{5... | collective-permute-start | bytes 2555912 | tf_op jit(solution)/shard_map/ppermute | solution.py:441
  132.2 31.3 %collective-permute-start.27 = (bf16[416,2048]{1,0:T(8,128)(2,1)}, bf16[416,2048]{1,0:T(8,128)(2,1)S(1)}, u32[]{:S(2)}, u32[]{:S(2)}) collective-permute-start(bf16[416,2048]{1,0:T(8,128)(2,1)} %refs_0_), channel_id=1, source_target_pairs={{0,1},{1,0},{2,3},{3,2},{4,5},{5,4},{6,7},{7,6},{8,9},{9,8},{10,11... | collective-permute-start | bytes 5111816 | tf_op jit(solution)/shard_map/ppermute | solution.py:438
  135.5 29.8 %collective-permute-start.30 = (bf16[416,2048]{1,0:T(8,128)(2,1)S(1)}, bf16[416,2048]{1,0:T(8,128)(2,1)S(1)}, u32[]{:S(2)}, u32[]{:S(2)}) collective-permute-start(bf16[416,2048]{1,0:T(8,128)(2,1)S(1)} %maximum_select_fusion.refs_2_), channel_id=1, source_target_pairs={{0,1},{1,0},{2,3},{3,2},{4,5},{5,4},{6,7},{7,6},{8,9},{9,8},{10,11... | collective-permute-start | bytes 5111816 | tf_op jit(solution)/shard_map/ppermute | solution.py:438
  142.8 35.5 %collective-permute-start.22 = (bf16[3,2,256,512]{3,2,0,1:T(8,128)(2,1)}, bf16[3,2,256,512]{3,2,0,1:T(8,128)(2,1)}, u32[]{:S(2)}, u32[]{:S(2)}) collective-permute-start(bf16[3,2,256,512]{3,2,0,1:T(8,128)(2,1)} %maximum_select_fusion.1), channel_id=1, source_target_pairs={{0,4},{4,0},{8,12},{12,8},{16,20},{20,16},{24,28},{28,24},{1,5},{5... | collective-permute-start | bytes 4718600 | tf_op jit(solution)/shard_map/ppermute | solution.py:441
  146.2 34.0 %collective-permute-start.25 = (bf16[3,256,512]{2,1,0:T(8,128)(2,1)}, bf16[3,256,512]{2,1,0:T(8,128)(2,1)S(1)}, u32[]{:S(2)}, u32[]{:S(2)}) collective-permute-start(bf16[3,256,512]{2,1,0:T(8,128)(2,1)} %slice_bitcast_fusion.2), channel_id=1, source_target_pairs={{0,1},{1,0},{2,3},{3,2},{4,5},{5,4},{6,7},{7,6},{8,9},{9,8},{10,11... | collective-permute-start | bytes 2359304 | tf_op jit(solution)/shard_map/ppermute | solution.py:438
  169.2 31.2 %collective-permute-start.32 = (bf16[256,2048]{1,0:T(8,128)(2,1)S(1)}, bf16[256,2048]{1,0:T(8,128)(2,1)S(1)}, u32[]{:S(2)}, u32[]{:S(2)}) collective-permute-start(bf16[256,2048]{1,0:T(8,128)(2,1)S(1)} %convolution_convert_fusion.3.refs_0_), channel_id=1, source_target_pairs={{0,2},{1,3},{2,0},{3,1},{4,6},{5,7},{6,4},{7,5},{8,10},{9,11},{10,... | collective-permute-start | bytes 3145736 | tf_op jit(solution)/shard_map/ppermute | solution.py:438
  418.8 48.4 %collective-permute-start.76 = (bf16[4,1024,256]{2,1,0:T(8,128)(2,1)}, bf16[4,1024,256]{2,1,0:T(8,128)(2,1)}, u32[]{:S(2)}, u32[]{:S(2)}) collective-permute-start(bf16[4,1024,256]{2,1,0:T(8,128)(2,1)} %shard_map.315), channel_id=1, source_target_pairs={{0,4},{4,0},{8,12},{12,8},{16,20},{20,16},{24,28},{28,24},{1,5},{5... | collective-permute-start | bytes 6291464 | tf_op jit(solution)/shard_map/ppermute | solution.py:542
  443.6 36.8 %collective-permute-start.69 = (bf16[512,1536]{1,0:T(8,128)(2,1)}, bf16[512,1536]{1,0:T(8,128)(2,1)}, u32[]{:S(2)}, u32[]{:S(2)}) collective-permute-start(bf16[512,1536]{1,0:T(8,128)(2,1)} %constant_dynamic-update-slice_fusion.18), channel_id=1, source_target_pairs={{0,2},{1,3},{2,0},{3,1},{4,6},{5,7},{6,4},{7,5},{8,10},{9,11},{10,... | collective-permute-start | bytes 4718600 | tf_op jit(solution)/shard_map/ppermute | solution.py:438
  459.1 32.7 %collective-permute-start.71 = (bf16[2,256,2048]{2,1,0:T(8,128)(2,1)}, bf16[2,256,2048]{2,1,0:T(8,128)(2,1)S(1)}, u32[]{:S(2)}, u32[]{:S(2)}) collective-permute-start(bf16[2,256,2048]{2,1,0:T(8,128)(2,1)} %slice.439), channel_id=1, source_target_pairs={{0,1},{1,0},{2,3},{3,2},{4,5},{5,4},{6,7},{7,6},{8,9},{9,8},{10,11... | collective-permute-start | bytes 6291464 | tf_op jit(solution)/shard_map/ppermute | solution.py:438
  459.8 33.7 %collective-permute-start.68 = (bf16[512,1536]{1,0:T(8,128)(2,1)}, bf16[512,1536]{1,0:T(8,128)(2,1)}, u32[]{:S(2)}, u32[]{:S(2)}) collective-permute-start(bf16[512,1536]{1,0:T(8,128)(2,1)} %constant_dynamic-update-slice_fusion.18), channel_id=1, source_target_pairs={{0,1},{1,0},{2,3},{3,2},{4,5},{5,4},{6,7},{7,6},{8,9},{9,8},{10,11... | collective-permute-start | bytes 4718600 | tf_op jit(solution)/shard_map/ppermute | solution.py:438
  469.6 55.8 %collective-permute-start.77 = (bf16[2,1024,256]{2,1,0:T(8,128)(2,1)}, bf16[2,1024,256]{2,1,0:T(8,128)(2,1)}, u32[]{:S(2)}, u32[]{:S(2)}) collective-permute-start(bf16[2,1024,256]{2,1,0:T(8,128)(2,1)} %add_convert_fusion.3), channel_id=1, source_target_pairs={{0,8},{4,12},{8,0},{12,4},{16,24},{20,28},{24,16},{28,20},{1,9},{5... | collective-permute-start | bytes 3145736 | tf_op jit(solution)/shard_map/ppermute | solution.py:542
  481.8 43.7 %collective-permute-start.81 = (bf16[128,2048]{1,0:T(8,128)(2,1)}, bf16[128,2048]{1,0:T(8,128)(2,1)}, u32[]{:S(2)}, u32[]{:S(2)}) collective-permute-start(bf16[128,2048]{1,0:T(8,128)(2,1)} %fusion.23), channel_id=1, source_target_pairs={{0,2},{1,3},{2,0},{3,1},{4,6},{5,7},{6,4},{7,5},{8,10},{9,11},{10,... | collective-permute-start | bytes 1572872 | tf_op jit(solution)/shard_map/ppermute | solution.py:438
  491.8 72.7 %collective-permute-start.75 = (bf16[4,1536,256]{2,1,0:T(8,128)(2,1)}, bf16[4,1536,256]{2,1,0:T(8,128)(2,1)}, u32[]{:S(2)}, u32[]{:S(2)}) collective-permute-start(bf16[4,1536,256]{2,1,0:T(8,128)(2,1)} %shard_map.326), channel_id=1, source_target_pairs={{0,4},{4,0},{8,12},{12,8},{16,20},{20,16},{24,28},{28,24},{1,5},{5... | collective-permute-start | bytes 9437192 | tf_op jit(solution)/shard_map/ppermute | solution.py:542
  505.3 37.7 %collective-permute-start.79 = (bf16[4,512,256]{2,1,0:T(8,128)(2,1)}, bf16[4,512,256]{2,1,0:T(8,128)(2,1)}, u32[]{:S(2)}, u32[]{:S(2)}) collective-permute-start(bf16[4,512,256]{2,1,0:T(8,128)(2,1)} %shard_map.321), channel_id=1, source_target_pairs={{0,8},{4,12},{8,0},{12,4},{16,24},{20,28},{24,16},{28,20},{1,9},{5... | collective-permute-start | bytes 3145736 | tf_op jit(solution)/shard_map/ppermute | solution.py:542
  524.0 43.5 %collective-permute-start.74 = (bf16[256,2048]{1,0:T(8,128)(2,1)}, bf16[256,2048]{1,0:T(8,128)(2,1)}, u32[]{:S(2)}, u32[]{:S(2)}) collective-permute-start(bf16[256,2048]{1,0:T(8,128)(2,1)} %fusion.22), channel_id=1, source_target_pairs={{0,2},{1,3},{2,0},{3,1},{4,6},{5,7},{6,4},{7,5},{8,10},{9,11},{10,... | collective-permute-start | bytes 3145736 | tf_op jit(solution)/shard_map/ppermute | solution.py:438
  525.4 43.2 %collective-permute-start.73 = (bf16[256,2048]{1,0:T(8,128)(2,1)}, bf16[256,2048]{1,0:T(8,128)(2,1)}, u32[]{:S(2)}, u32[]{:S(2)}) collective-permute-start(bf16[256,2048]{1,0:T(8,128)(2,1)} %fusion.22), channel_id=1, source_target_pairs={{0,1},{1,0},{2,3},{3,2},{4,5},{5,4},{6,7},{7,6},{8,9},{9,8},{10,11... | collective-permute-start | bytes 3145736 | tf_op jit(solution)/shard_map/ppermute | solution.py:438
  567.5 48.8 %collective-permute-start.86 = (bf16[4,1024,256]{2,1,0:T(8,128)(2,1)}, bf16[4,1024,256]{2,1,0:T(8,128)(2,1)}, u32[]{:S(2)}, u32[]{:S(2)}) collective-permute-start(bf16[4,1024,256]{2,1,0:T(8,128)(2,1)} %shard_map.320), channel_id=1, source_target_pairs={{0,4},{4,0},{8,12},{12,8},{16,20},{20,16},{24,28},{28,24},{1,5},{5... | collective-permute-start | bytes 6291464 | tf_op jit(solution)/shard_map/ppermute | solution.py:542
  568.6 37.6 %collective-permute-start.87 = (bf16[2,1536,256]{2,1,0:T(8,128)(2,1)}, bf16[2,1536,256]{2,1,0:T(8,128)(2,1)}, u32[]{:S(2)}, u32[]{:S(2)}) collective-permute-start(bf16[2,1536,256]{2,1,0:T(8,128)(2,1)} %add_convert_fusion.1), channel_id=1, source_target_pairs={{0,8},{4,12},{8,0},{12,4},{16,24},{20,28},{24,16},{28,20},{1,9},{5... | collective-permute-start | bytes 4718600 | tf_op jit(solution)/shard_map/ppermute | solution.py:542
  586.0 52.6 %collective-permute-start.85 = (bf16[4,128,2048]{2,1,0:T(8,128)(2,1)}, bf16[4,128,2048]{2,1,0:T(8,128)(2,1)}, u32[]{:S(2)}, u32[]{:S(2)}) collective-permute-start(bf16[4,128,2048]{2,1,0:T(8,128)(2,1)} %slice.461), channel_id=1, source_target_pairs={{0,1},{1,0},{2,3},{3,2},{4,5},{5,4},{6,7},{7,6},{8,9},{9,8},{10,11... | collective-permute-start | bytes 6291464 | tf_op jit(solution)/shard_map/ppermute | solution.py:438
  586.1 57.8 %collective-permute-start.93 = (bf16[2,512,256]{2,1,0:T(8,128)(2,1)}, bf16[2,512,256]{2,1,0:T(8,128)(2,1)S(1)}, u32[]{:S(2)}, u32[]{:S(2)}) collective-permute-start(bf16[2,512,256]{2,1,0:T(8,128)(2,1)} %add_convert_fusion.6), channel_id=1, source_target_pairs={{0,4},{4,0},{8,12},{12,8},{16,20},{20,16},{24,28},{28,24},{1,5},{5... | collective-permute-start | bytes 1572872 | tf_op jit(solution)/shard_map/ppermute | solution.py:542
  587.2 51.4 %collective-permute-start.91 = (bf16[4,416,256]{2,1,0:T(8,128)(2,1)S(1)}, bf16[4,416,256]{2,1,0:T(8,128)(2,1)S(1)}, u32[]{:S(2)}, u32[]{:S(2)}) collective-permute-start(bf16[4,416,256]{2,1,0:T(8,128)(2,1)S(1)} %shard_map.329), channel_id=1, source_target_pairs={{0,8},{4,12},{8,0},{12,4},{16,24},{20,28},{24,16},{28,20},{1,9},{5... | collective-permute-start | bytes 2555912 | tf_op jit(solution)/shard_map/ppermute | solution.py:542
  608.0 62.3 %collective-permute-start.100 = (bf16[1536,256]{1,0:T(8,128)(2,1)S(1)}, bf16[1536,256]{1,0:T(8,128)(2,1)S(1)}, u32[]{:S(2)}, u32[]{:S(2)}) collective-permute-start(bf16[1536,256]{1,0:T(8,128)(2,1)S(1)} %fusion.37), channel_id=1, source_target_pairs={{0,16},{4,20},{8,24},{12,28},{16,0},{20,4},{24,8},{28,12},{1,17},{... | collective-permute-start | bytes 2359304 | tf_op jit(solution)/shard_map/ppermute | solution.py:542
  617.9 48.5 %collective-permute-start.90 = (bf16[2,1024,256]{2,1,0:T(8,128)(2,1)S(1)}, bf16[2,1024,256]{2,1,0:T(8,128)(2,1)S(1)}, u32[]{:S(2)}, u32[]{:S(2)}) collective-permute-start(bf16[2,1024,256]{2,1,0:T(8,128)(2,1)S(1)} %add_convert_fusion.2), channel_id=1, source_target_pairs={{0,8},{4,12},{8,0},{12,4},{16,24},{20,28},{24,16},{28,20},{1,9},{5... | collective-permute-start | bytes 3145736 | tf_op jit(solution)/shard_map/ppermute | solution.py:542
  663.6 84.5 %collective-permute-start.102 = (bf16[128,2048]{1,0:T(8,128)(2,1)S(1)}, bf16[128,2048]{1,0:T(8,128)(2,1)S(1)}, u32[]{:S(2)}, u32[]{:S(2)}) collective-permute-start(bf16[128,2048]{1,0:T(8,128)(2,1)S(1)} %pad_maximum_fusion.14), channel_id=1, source_target_pairs={{0,4},{4,0},{8,12},{12,8},{16,20},{20,16},{24,28},{28,24},{1,5},{5... | collective-permute-start | bytes 1572872 | tf_op jit(solution)/shard_map/ppermute | solution.py:441
  665.5 41.5 %collective-permute-start.89 = (bf16[128,2048]{1,0:T(8,128)(2,1)S(1)}, bf16[128,2048]{1,0:T(8,128)(2,1)S(1)}, u32[]{:S(2)}, u32[]{:S(2)}) collective-permute-start(bf16[128,2048]{1,0:T(8,128)(2,1)S(1)} %pad_maximum_fusion.13), channel_id=1, source_target_pairs={{0,2},{1,3},{2,0},{3,1},{4,6},{5,7},{6,4},{7,5},{8,10},{9,11},{10,... | collective-permute-start | bytes 1572872 | tf_op jit(solution)/shard_map/ppermute | solution.py:438
  667.7 38.0 %collective-permute-start.98 = (bf16[1024,256]{1,0:T(8,128)(2,1)S(1)}, bf16[1024,256]{1,0:T(8,128)(2,1)S(1)}, u32[]{:S(2)}, u32[]{:S(2)}) collective-permute-start(bf16[1024,256]{1,0:T(8,128)(2,1)S(1)} %fusion.42), channel_id=1, source_target_pairs={{0,16},{4,20},{8,24},{12,28},{16,0},{20,4},{24,8},{28,12},{1,17},{... | collective-permute-start | bytes 1572872 | tf_op jit(solution)/shard_map/ppermute | solution.py:542
  698.7 44.6 %collective-permute-start.103 = (bf16[3,512,256]{2,1,0:T(8,128)(2,1)S(1)}, bf16[3,512,256]{2,1,0:T(8,128)(2,1)S(1)}, u32[]{:S(2)}, u32[]{:S(2)}) collective-permute-start(bf16[3,512,256]{2,1,0:T(8,128)(2,1)S(1)} %pad_maximum_fusion.8), channel_id=1, source_target_pairs={{0,0},{1,8},{2,16},{3,24},{4,4},{5,12},{6,20},{7,28},{8,1},{9,9},{... | collective-permute-start | bytes 2359304 | tf_op jit(solution)/shard_map/ppermute | solution.py:592
  (223 other events, 2757.9 us)
Sparse Core Ops, SparseCore 0:
  347.1 145.6 reduce-scatter.1

commit v4 on v3

--- a/solution.py
+++ b/solution.py
@@ -648,6 +648,8 @@
         cross_own = (c_key, c_value, c_query)
         cross_ready = after(cross_own, patch_part, value_near)
         cross_part = swap(sent_parts(cross_ready, f, 2 * x + z, 4), 2)
+        cross_near = pick(z, cross_part, hop(cross_part, 1), 2)
+        cross_far = across(cross_near)
         self_mate = mate_parts((w_query, w_key, w_value), f)
         first_blocks = gather_blocks(first, after(first_chip, pair_far))
         info = jnp.concatenate([info, swap(info, 1), chip_info, swap(chip_info, 1)], axis=0)
@@ -656,11 +658,8 @@
         queries = to_heads(place, first_blocks, query_w)
         keys_all = to_heads(place, first_blocks, key_w)
         values_all = to_heads(place, first_blocks, value_w)
-        cross_part = after(cross_part, values_all)
-        cross_near = pick(z, cross_part, hop(cross_part, 1), 2)
-        cross_far = across(cross_near)
         mixed = attend(info, queries, keys_all, values_all, slot, slot, width, True)
-        own, other = core_sum(low(nn(mixed, w_out)))
+        own, other = core_sum(low(nn(after(mixed, cross_near, patch_half), w_out)))
         cross_mate = mate_parts(after(cross_own, other), f)
         sent_out = other
         other = swap(other, 2)
@@ -807,9 +806,7 @@
         gains = gains + after(hop(gains, 1), grad_context)
         kept = sum_self.keep(grad_context, gains), sum_value.keep(grad_context)
         value_one = sum_value.add(1, *kept)
-        cross_all = sum_cross.add(3, value_one)
-        context_one = sum_context.add(1, cross_all)
-        context_chip = after(context_chip, context_one)
+        context_chip = after(context_chip, value_one, step)
         grad_context_all = gather_rows(grad_context, context_chip)
         sum_patch = Sum(place, (("rows", patch_turned, grad_context_all),), (1, 0, 2))
         sum_patch.send()
@@ -817,10 +814,12 @@
         out_part = low(nn(after(hidden, kept), down_half))
         sums = plane_core(out_part)
         patches_grad = nt(after(grad_context, kept), patch_mat)[None]
-        step = sum_context.add(2, kept, out_part, patches_grad)
+        context_one = sum_context.add(1, kept, out_part, patches_grad)
+        patch_one = sum_patch.add(1, context_one)
+        step = sum_context.add(2, patch_one)
         step = sum_self.add(1, step)
         own, chip, side = plane_far(after(tuple(sums), step))
-        step = sum_patch.add(1, step)
+        step = sum_cross.add(3, step)
         step = sum_value.add(2, step)
         gains = gains + after(hop(after(gains, step), 0), chip, side)
         gains = gains + after(swap(gains, 2), chip)

time: 766 us -> 758 us (0.990)
    unnamed x314 -> x310, local copies, waits for them, and re-layouts: 35.8 us -> 37.4 us
  transfers between devices with their start and end apart: 106 -> 106, of which waited for: 43 -> 42; matrix products, arithmetic and copies ran while one was open for 23% -> 23% of each run, Pallas kernels for 19% -> 19%
where the time goes in v4:
time: 758 us; the launch traced here: 750 us
  waiting for transfers between devices  302 us (40%)
  Pallas kernels  142 us (19%)
  other arithmetic  82.5 us (11%)
  starting transfers between devices  81.4 us (11%)
  local copies, waits for them, and re-layouts  74.7 us (10%)
  matrix products  49.7 us (7%)
  between operations  18.5 us (2%)
    ppermute x71, waiting for transfers between devices, swap(): return lax.ppermute(values, 'fsdp', [(i, i ^ r) for i in range(fsdp)])  137 us
    ppermute x20, waiting for transfers between devices, hop(): return lax.ppermute(values, 'dp', [(i, i ^ 1 << bit) for i in range(dp)])  89.6 us
    dot_general x12, matrix products, dot(): lax.dot_general(left, right, (((left_dim,), (right_dim,)), ((), ())), pre...  49.7 us
    pallas_call x10, Pallas kernels, half_grads(): pl.pallas_call(half_kernel, out_shape=jax.ShapeDtypeStruct((4, rows, wide...  48.8 us
    ppermute x13, waiting for transfers between devices, across(): return lax.ppermute(values, 'dp', [(i, i ^ 1) for i in range(dp)])  43 us
    unnamed x310, local copies, waits for them, and re-layouts  37.4 us
    ppermute x71, starting transfers between devices, swap(): return lax.ppermute(values, 'fsdp', [(i, i ^ r) for i in range(fsdp)])  35.6 us
    ppermute x1, waiting for transfers between devices, place_columns(): return lax.ppermute(values, ('dp', 'fsdp'), pairs)  32.3 us
  transfers between devices with their start and end apart: 106, of which 42 were waited for; matrix products, arithmetic and copies ran while one was open for 23% of the time, Pallas kernels for 19%

profile of v4, /device:TPU:4, one launch (start us, length us, event | category | flops | bytes accessed | tf_op | source)
XLA Modules:
  0.0 750.0 jit_solution(12360400217634443287)
XLA Ops:
  20.8 21.1 %collective-permute-done.5 = bf16[2,2,256,512]{3,2,0,1:T(8,128)(2,1)S(1)} collective-permute-done((bf16[2,2,256,512]{3,2,0,1:T(8,128)(2,1)S(1)}, bf16[2,2,256,512]{3,2,0,1:T(8,128)(2,1)S(1)}, u32[]{:S(2)}, u32[]{:S(2)}) %collective-permute-start.5) | collective-permute-done | bytes 1048608 | tf_op jit(solution)/shard_map/ppermute | solution.py:438
  47.0 6.2 collective-permute-done.11.refs_6_.refs_17_
  53.2 9.1 %collective-permute-done.15 = bf16[104,2048]{1,0:T(8,128)(2,1)S(1)} collective-permute-done((bf16[104,2048]{1,0:T(8,128)(2,1)S(1)}, bf16[104,2048]{1,0:T(8,128)(2,1)S(1)}, u32[]{:S(2)}, u32[]{:S(2)}) %collective-permute-start.15) | collective-permute-done | bytes 426016 | tf_op jit(solution)/shard_map/ppermute | solution.py:438
  82.8 9.5 %collective-permute-done.16 = bf16[3,2,128,512]{3,2,0,1:T(8,128)(2,1)S(1)} collective-permute-done((bf16[3,2,128,512]{3,2,0,1:T(8,128)(2,1)S(1)}, bf16[3,2,128,512]{3,2,0,1:T(8,128)(2,1)S(1)}, u32[]{:S(2)}, u32[]{:S(2)}) %collective-permute-start.16) | collective-permute-done | bytes 786464 | tf_op jit(solution)/shard_map/ppermute | solution.py:438
  104.0 6.4 shard_map.300.refs_0_
  147.5 9.2 %collective-permute-done.23 = bf16[3,2,256,512]{3,2,0,1:T(8,128)(2,1)} collective-permute-done((bf16[3,2,256,512]{3,2,0,1:T(8,128)(2,1)S(1)}, bf16[3,2,256,512]{3,2,0,1:T(8,128)(2,1)}, u32[]{:S(2)}, u32[]{:S(2)}) %collective-permute-start.23) | collective-permute-done | bytes 1572896 | tf_op jit(solution)/shard_map/ppermute | solution.py:441
  166.8 9.6 %collective-permute-done.32.refs_2_ = bf16[256,2048]{1,0:T(8,128)(2,1)S(1)} collective-permute-done((bf16[256,2048]{1,0:T(8,128)(2,1)S(1)}, bf16[256,2048]{1,0:T(8,128)(2,1)S(1)}, u32[]{:S(2)}, u32[]{:S(2)}) %collective-permute-start.32) | collective-permute-done | bytes 1048608 | tf_op jit(solution)/shard_map/ppermute | solution.py:438
  213.2 11.0 %collective-permute-done.37 = bf16[128,2048]{1,0:T(8,128)(2,1)S(1)} collective-permute-done((bf16[128,2048]{1,0:T(8,128)(2,1)S(1)}, bf16[128,2048]{1,0:T(8,128)(2,1)S(1)}, u32[]{:S(2)}, u32[]{:S(2)}) %collective-permute-start.37) | collective-permute-done | bytes 524320 | tf_op jit(solution)/shard_map/ppermute | solution.py:438
  230.4 11.3 %collective-permute-done.47 = bf16[128,2048]{1,0:T(8,128)(2,1)} collective-permute-done((bf16[128,2048]{1,0:T(8,128)(2,1)}, bf16[128,2048]{1,0:T(8,128)(2,1)}, u32[]{:S(2)}, u32[]{:S(2)}) %collective-permute-start.47) | collective-permute-done | bytes 524320 | tf_op jit(solution)/shard_map/ppermute | solution.py:441
  260.5 8.1 %fusion.15 = f32[1024,640]{1,0:T(8,128)} fusion(bf16[1024,2048]{1,0:T(8,128)(2,1)} %constant_dynamic-update-slice_fusion.9.refs_1_.refs_3_, bf16[1280,2048]{1,0:T(8,128)(2,1)} %param.34, s32[]{:T(128)S(6)} %select_n.149), kind=kOutput, calls=%fused_computation.29 | convolution fusion | flops 2684354560 | bytes 9437188 | tf_op jit(solution)/shard_map/dot_general | solution.py:29
  273.7 8.1 %multiply_convert_fusion = (bf16[1024,640]{1,0:T(8,128)(2,1)S(1)}, bf16[1024,640]{1,0:T(8,128)(2,1)S(1)}, bf16[1024,640]{1,0:T(8,128)(2,1)S(1)}) fusion(f32[1024,640]{1,0:T(8,128)} %fusion.18, f32[1024,640]{1,0:T(8,128)} %fusion.15, bf16[1024,2048]{1,0:T(8,128)(2,1)S(1)} %copy-done.134, bf16[1280,2048]{1,0:T(8,128)(2,1)} %param.35, s32[]{:T(128)S(6)} %select_n.149), kind=kOutput, calls=%fused_computation.20 | convolution fusion | flops 2700738560 | bytes 15990788 | tf_op jit(solution)/shard_map/dot_general | solution.py:29
  309.9 13.1 %shard_map.309 = bf16[4,1920,512]{2,1,0:T(8,128)(2,1)} custom-call(s32[2]{0:T(128)S(1)} %broadcast_6_place.2.place, bf16[640,1024]{1,0:T(8,128)(2,1)S(1)} %shard_map.306.refs_0_, bf16[1024,2048]{1,0:T(8,128)(2,1)} %constant_dynamic-update-slice_fusion.9.refs_1_.refs_3_, bf16[640,1024]{1,0:T(8,128)(2,1)S(1)} %shard_map.307.refs_2_, ...), custom_call_target="tpu_custom_call" | custom-call | flops 14400000000 | bytes 36000000 | tf_op jit(solution)/shard_map/pallas_call | solution.py:407
  330.3 10.1 %collective-permute-done.61 = bf16[128,2048]{1,0:T(8,128)(2,1)S(1)} collective-permute-done((bf16[128,2048]{1,0:T(8,128)(2,1)S(1)}, bf16[128,2048]{1,0:T(8,128)(2,1)S(1)}, u32[]{:S(2)}, u32[]{:S(2)}) %collective-permute-start.61) | collective-permute-done | bytes 524320 | tf_op jit(solution)/shard_map/ppermute | solution.py:438
  343.7 8.1 %shard_map.312 = (bf16[512,512]{1,0:T(8,128)(2,1)S(1)}, bf16[1024,512]{1,0:T(8,128)(2,1)S(1)}, bf16[1024,512]{1,0:T(8,128)(2,1)S(1)}) custom-call(s32[4,2]{1,0:T(4,128)S(1)} %pad_add_fusion.info, bf16[512,512]{1,0:T(8,128)(2,1)S(1)} %copy-done.33, bf16[1024,512]{1,0:T(8,128)(2,1)S(1)} %copy-done.69, bf16[1024,512]{1,0:T(8,128)(2,1)S(1)} %copy-done.67, ...), custom_call_target="tpu_custom_call" | custom-call | flops 6400000000 | bytes 16000000 | tf_op jit(solution)/shard_map/pallas_call | solution.py:129
  389.0 5.7 collective-permute-done.66
  398.0 7.8 %shard_map.319 = (bf16[512,512]{1,0:T(8,128)(2,1)S(1)}, bf16[512,512]{1,0:T(8,128)(2,1)S(1)}, bf16[512,512]{1,0:T(8,128)(2,1)S(1)}) custom-call(s32[4,2]{1,0:T(4,128)S(1)} %pad_add_fusion.info, bf16[512,512]{1,0:T(8,128)(2,1)S(1)} %copy-done.25, bf16[512,512]{1,0:T(8,128)(2,1)S(1)} %copy-done.23, bf16[512,512]{1,0:T(8,128)(2,1)S(1)} %copy-done.63, ...), custom_call_target="tpu_custom_call" | custom-call | flops 6400000000 | bytes 16000000 | tf_op jit(solution)/shard_map/pallas_call | solution.py:129
  408.2 8.9 %shard_map.324 = bf16[512,2048]{1,0:T(8,128)(2,1)} custom-call(s32[2]{0:T(128)} %copy-done.43, bf16[512,512]{1,0:T(8,128)(2,1)} %copy-done.38, bf16[512,512]{1,0:T(8,128)(2,1)} %copy-done.36, bf16[512,512]{1,0:T(8,128)(2,1)} %copy-done.34, bf16[512,2048]{1,0:T(8,128)(2,1)} %refs_3_, bf16[3,512,512]{2,1,0:T(8,128)(2,1)} %copy-done.6, ...), custom_call_target="tpu_custom_call" | custom-call | flops 7742608896 | bytes 19356520 | tf_op jit(solution)/shard_map/pallas_call | solution.py:247
  420.7 10.5 %shard_map.325 = bf16[1024,2048]{1,0:T(8,128)(2,1)} custom-call(s32[2]{0:T(128)} %copy-done.43, bf16[1024,512]{1,0:T(8,128)(2,1)} %copy-done.75, bf16[1024,512]{1,0:T(8,128)(2,1)} %copy-done.77, bf16[512,2048]{1,0:T(8,128)(2,1)} %refs_2_.1, bf16[3,512,512]{2,1,0:T(8,128)(2,1)} %copy-done.19, bf16[3,2,256,512]{3,2,1,0:T(8,128)(2,1)} %copy.38.refs_6_.refs_3_.refs_4_.refs_10_, ...), custom_call_target="tpu_custom_call" | custom-call | flops 9523478528 | bytes 23808696 | tf_op jit(solution)/shard_map/pallas_call | solution.py:247
  435.4 7.8 %collective-permute-done.78 = bf16[4,1024,256]{2,1,0:T(8,128)(2,1)} collective-permute-done((bf16[4,1024,256]{2,1,0:T(8,128)(2,1)}, bf16[4,1024,256]{2,1,0:T(8,128)(2,1)}, u32[]{:S(2)}, u32[]{:S(2)}) %collective-permute-start.78) | collective-permute-done | bytes 2097184 | tf_op jit(solution)/shard_map/ppermute | solution.py:542
  446.4 10.0 %collective-permute-done.69 = bf16[512,1536]{1,0:T(8,128)(2,1)} collective-permute-done((bf16[512,1536]{1,0:T(8,128)(2,1)}, bf16[512,1536]{1,0:T(8,128)(2,1)}, u32[]{:S(2)}, u32[]{:S(2)}) %collective-permute-start.69) | collective-permute-done | bytes 1572896 | tf_op jit(solution)/shard_map/ppermute | solution.py:438
  458.9 8.4 %shard_map.327 = bf16[4,1536,256]{2,1,0:T(8,128)(2,1)} custom-call(s32[2]{0:T(128)S(1)} %copy-done.45, bf16[2048,1024]{1,0:T(8,128)(2,1)} %copy-done.64, bf16[1024,512]{1,0:T(8,128)(2,1)S(1)} %copy-done.76, bf16[2048,1024]{1,0:T(8,128)(2,1)} %copy-done.64, bf16[1024,512]{1,0:T(8,128)(2,1)S(1)} %copy-done.78, bf16[512,512]{1,0:T(8,128)(2,1)S(1)} %copy-done.84, ...), custom_call_target="tpu_custom_call" | custom-call | flops 5851428352 | bytes 14628571 | tf_op jit(solution)/shard_map/pallas_call | solution.py:313
  470.2 6.5 pad_maximum_fusion.refs_1_.refs_3_
  487.0 8.4 %shard_map.322 = bf16[4,1536,256]{2,1,0:T(8,128)(2,1)} custom-call(s32[2]{0:T(128)S(1)} %copy-done.45, bf16[2048,1024]{1,0:T(8,128)(2,1)} %copy-done.64, bf16[1024,512]{1,0:T(8,128)(2,1)S(1)} %copy-done.76, bf16[2048,1024]{1,0:T(8,128)(2,1)} %copy-done.64, bf16[1024,512]{1,0:T(8,128)(2,1)S(1)} %copy-done.78, bf16[512,512]{1,0:T(8,128)(2,1)S(1)} %copy-done.84, ...), custom_call_target="tpu_custom_call" | custom-call | flops 5851428352 | bytes 14628571 | tf_op jit(solution)/shard_map/pallas_call | solution.py:313
  534.1 5.9 convolution_convert_fusion
  540.0 5.5 convolution_bitcast_fusion
  555.2 59.5 %collective-permute-done.87 = bf16[4,416,256]{2,1,0:T(8,128)(2,1)} collective-permute-done((bf16[4,416,256]{2,1,0:T(8,128)(2,1)S(1)}, bf16[4,416,256]{2,1,0:T(8,128)(2,1)}, u32[]{:S(2)}, u32[]{:S(2)}) %collective-permute-start.87) | collective-permute-done | bytes 852000 | tf_op jit(solution)/shard_map/ppermute | solution.py:542
  633.4 9.7 %collective-permute-done.88 = bf16[64,2048]{1,0:T(8,128)(2,1)S(1)} collective-permute-done((bf16[64,2048]{1,0:T(8,128)(2,1)S(1)}, bf16[64,2048]{1,0:T(8,128)(2,1)S(1)}, u32[]{:S(2)}, u32[]{:S(2)}) %collective-permute-start.88) | collective-permute-done | bytes 262176 | tf_op jit(solution)/shard_map/ppermute | solution.py:441
  644.2 5.3 collective-permute-done.94
  659.1 7.9 %collective-permute-done.90 = bf16[2,1024,256]{2,1,0:T(8,128)(2,1)S(1)} collective-permute-done((bf16[2,1024,256]{2,1,0:T(8,128)(2,1)S(1)}, bf16[2,1024,256]{2,1,0:T(8,128)(2,1)S(1)}, u32[]{:S(2)}, u32[]{:S(2)}) %collective-permute-start.90) | collective-permute-done | bytes 1048608 | tf_op jit(solution)/shard_map/ppermute | solution.py:542
  672.5 9.0 %collective-permute-done.99 = bf16[512,256]{1,0:T(8,128)(2,1)S(1)} collective-permute-done((bf16[512,256]{1,0:T(8,128)(2,1)S(1)}, bf16[512,256]{1,0:T(8,128)(2,1)S(1)}, u32[]{:S(2)}, u32[]{:S(2)}) %collective-permute-start.99) | collective-permute-done | bytes 262176 | tf_op jit(solution)/shard_map/ppermute | solution.py:542
  681.5 9.3 %collective-permute-done.101 = bf16[1920,256]{1,0:T(8,128)(2,1)S(1)} collective-permute-done((bf16[1920,256]{1,0:T(8,128)(2,1)S(1)}, bf16[1920,256]{1,0:T(8,128)(2,1)S(1)}, u32[]{:S(2)}, u32[]{:S(2)}) %collective-permute-start.101) | collective-permute-done | bytes 983072 | tf_op jit(solution)/shard_map/ppermute | solution.py:441
  703.3 32.3 %collective-permute-done.103 = bf16[3,512,256]{2,1,0:T(8,128)(2,1)S(1)} collective-permute-done((bf16[3,512,256]{2,1,0:T(8,128)(2,1)S(1)}, bf16[3,512,256]{2,1,0:T(8,128)(2,1)S(1)}, u32[]{:S(2)}, u32[]{:S(2)}) %collective-permute-start.103) | collective-permute-done | bytes 786464 | tf_op jit(solution)/shard_map/ppermute | solution.py:592
  (680 shorter events, 372.2 us)
Async XLA Ops:
  7.2 492.7 %reduce-scatter.2.cloned.1.call-start = ((), (), s32[]{:S(2)}) async-start(), calls=%async_computation.1 | async-start | bytes 9830400 | tf_op jit(solution)/shard_map/reduce_scatter | solution.py:722
  8.7 37.4 %collective-permute-start.1 = (s32[1,2]{1,0:T(1,128)S(1)}, s32[1,2]{1,0:T(1,128)S(1)}, u32[]{:S(2)}, u32[]{:S(2)}) collective-permute-start(s32[1,2]{1,0:T(1,128)S(1)} %pad_add_fusion.1), channel_id=1, source_target_pairs={{0,1},{1,0},{2,3},{3,2},{4,5},{5,4},{6,7},{7,6},{8,9},{9,8},{10,11... | collective-permute-start | bytes 32 | tf_op jit(solution)/shard_map/ppermute | solution.py:438
  12.4 34.5 %collective-permute-start.2 = (s32[1,2]{1,0:T(1,128)S(1)}, s32[1,2]{1,0:T(1,128)S(1)}, u32[]{:S(2)}, u32[]{:S(2)}) collective-permute-start(s32[1,2]{1,0:T(1,128)S(1)} %collective-permute-done), channel_id=1, source_target_pairs={{0,1},{1,0},{2,3},{3,2},{4,5},{5,4},{6,7},{7,6},{8,9},{9,8},{10,11... | collective-permute-start | bytes 32 | tf_op jit(solution)/shard_map/ppermute | solution.py:438
  17.4 35.8 %collective-permute-start.11 = (bf16[1,2,256,512]{3,2,1,0:T(8,128)(2,1)S(1)}, bf16[1,2,256,512]{3,2,1,0:T(8,128)(2,1)S(1)}, u32[]{:S(2)}, u32[]{:S(2)}) collective-permute-start(bf16[1,2,256,512]{3,2,1,0:T(8,128)(2,1)S(1)} %maximum_bitcast_fusion.2), channel_id=1, source_target_pairs={{0,2},{1,3},{2,0},{3,1},{4,6},{5,7},{6,4},{7,5},{8,10},{9,11},{10,... | collective-permute-start | bytes 1572872 | tf_op jit(solution)/shard_map/ppermute | solution.py:438
  46.1 27.0 %collective-permute-start.4 = (bf16[128,2048]{1,0:T(8,128)(2,1)S(1)}, bf16[128,2048]{1,0:T(8,128)(2,1)S(1)}, u32[]{:S(2)}, u32[]{:S(2)}) collective-permute-start(bf16[128,2048]{1,0:T(8,128)(2,1)S(1)} %multiply_convert_fusion.5.refs_0_), channel_id=1, source_target_pairs={{0,2},{1,3},{2,0},{3,1},{4,6},{5,7},{6,4},{7,5},{8,10},{9,11},{10,... | collective-permute-start | bytes 1572872 | tf_op jit(solution)/shard_map/ppermute | solution.py:438
  46.9 27.5 %collective-permute-start.3 = (bf16[128,2048]{1,0:T(8,128)(2,1)S(1)}, bf16[128,2048]{1,0:T(8,128)(2,1)S(1)}, u32[]{:S(2)}, u32[]{:S(2)}) collective-permute-start(bf16[128,2048]{1,0:T(8,128)(2,1)S(1)} %multiply_convert_fusion.5.refs_0_), channel_id=1, source_target_pairs={{0,1},{1,0},{2,3},{3,2},{4,5},{5,4},{6,7},{7,6},{8,9},{9,8},{10,11... | collective-permute-start | bytes 1572872 | tf_op jit(solution)/shard_map/ppermute | solution.py:438
  53.2 28.2 %collective-permute-start.8 = (bf16[3,512,512]{2,1,0:T(8,128)(2,1)S(1)}, bf16[3,512,512]{2,1,0:T(8,128)(2,1)S(1)}, u32[]{:S(2)}, u32[]{:S(2)}) collective-permute-start(bf16[3,512,512]{2,1,0:T(8,128)(2,1)S(1)} %pad_maximum_fusion.4), channel_id=1, source_target_pairs={{0,1},{1,0},{2,3},{3,2},{4,5},{5,4},{6,7},{7,6},{8,9},{9,8},{10,11... | collective-permute-start | bytes 4718600 | tf_op jit(solution)/shard_map/ppermute | solution.py:438
  81.4 35.5 %collective-permute-start.29 = (bf16[208,2048]{1,0:T(8,128)(2,1)}, bf16[208,2048]{1,0:T(8,128)(2,1)}, u32[]{:S(2)}, u32[]{:S(2)}) collective-permute-start(bf16[208,2048]{1,0:T(8,128)(2,1)} %maximum_select_fusion.2), channel_id=1, source_target_pairs={{0,4},{4,0},{8,12},{12,8},{16,20},{20,16},{24,28},{28,24},{1,5},{5... | collective-permute-start | bytes 2555912 | tf_op jit(solution)/shard_map/ppermute | solution.py:441
  120.2 36.5 %collective-permute-start.23 = (bf16[3,2,256,512]{3,2,0,1:T(8,128)(2,1)S(1)}, bf16[3,2,256,512]{3,2,0,1:T(8,128)(2,1)}, u32[]{:S(2)}, u32[]{:S(2)}) collective-permute-start(bf16[3,2,256,512]{3,2,0,1:T(8,128)(2,1)S(1)} %copy-done.93), channel_id=1, source_target_pairs={{0,4},{4,0},{8,12},{12,8},{16,20},{20,16},{24,28},{28,24},{1,5},{5... | collective-permute-start | bytes 4718600 | tf_op jit(solution)/shard_map/ppermute | solution.py:441
  122.6 36.0 %collective-permute-start.26 = (bf16[3,256,512]{2,1,0:T(8,128)(2,1)}, bf16[3,256,512]{2,1,0:T(8,128)(2,1)S(1)}, u32[]{:S(2)}, u32[]{:S(2)}) collective-permute-start(bf16[3,256,512]{2,1,0:T(8,128)(2,1)} %slice_bitcast_fusion.2), channel_id=1, source_target_pairs={{0,1},{1,0},{2,3},{3,2},{4,5},{5,4},{6,7},{7,6},{8,9},{9,8},{10,11... | collective-permute-start | bytes 2359304 | tf_op jit(solution)/shard_map/ppermute | solution.py:438
  129.8 33.4 %collective-permute-start.25 = (bf16[3,512,512]{2,1,0:T(8,128)(2,1)}, bf16[3,512,512]{2,1,0:T(8,128)(2,1)S(1)}, u32[]{:S(2)}, u32[]{:S(2)}) collective-permute-start(bf16[3,512,512]{2,1,0:T(8,128)(2,1)} %pad_maximum_fusion.5), channel_id=1, source_target_pairs={{0,1},{1,0},{2,3},{3,2},{4,5},{5,4},{6,7},{7,6},{8,9},{9,8},{10,11... | collective-permute-start | bytes 4718600 | tf_op jit(solution)/shard_map/ppermute | solution.py:438
  146.5 29.9 %collective-permute-start.32 = (bf16[256,2048]{1,0:T(8,128)(2,1)S(1)}, bf16[256,2048]{1,0:T(8,128)(2,1)S(1)}, u32[]{:S(2)}, u32[]{:S(2)}) collective-permute-start(bf16[256,2048]{1,0:T(8,128)(2,1)S(1)} %convolution_convert_fusion.3.refs_0_), channel_id=1, source_target_pairs={{0,2},{1,3},{2,0},{3,1},{4,6},{5,7},{6,4},{7,5},{8,10},{9,11},{10,... | collective-permute-start | bytes 3145736 | tf_op jit(solution)/shard_map/ppermute | solution.py:438
  394.8 48.4 %collective-permute-start.78 = (bf16[4,1024,256]{2,1,0:T(8,128)(2,1)}, bf16[4,1024,256]{2,1,0:T(8,128)(2,1)}, u32[]{:S(2)}, u32[]{:S(2)}) collective-permute-start(bf16[4,1024,256]{2,1,0:T(8,128)(2,1)} %shard_map.315), channel_id=1, source_target_pairs={{0,4},{4,0},{8,12},{12,8},{16,20},{20,16},{24,28},{28,24},{1,5},{5... | collective-permute-start | bytes 6291464 | tf_op jit(solution)/shard_map/ppermute | solution.py:542
  419.6 36.8 %collective-permute-start.69 = (bf16[512,1536]{1,0:T(8,128)(2,1)}, bf16[512,1536]{1,0:T(8,128)(2,1)}, u32[]{:S(2)}, u32[]{:S(2)}) collective-permute-start(bf16[512,1536]{1,0:T(8,128)(2,1)} %constant_dynamic-update-slice_fusion.18), channel_id=1, source_target_pairs={{0,2},{1,3},{2,0},{3,1},{4,6},{5,7},{6,4},{7,5},{8,10},{9,11},{10,... | collective-permute-start | bytes 4718600 | tf_op jit(solution)/shard_map/ppermute | solution.py:438
  434.6 32.7 %collective-permute-start.71 = (bf16[2,256,2048]{2,1,0:T(8,128)(2,1)}, bf16[2,256,2048]{2,1,0:T(8,128)(2,1)S(1)}, u32[]{:S(2)}, u32[]{:S(2)}) collective-permute-start(bf16[2,256,2048]{2,1,0:T(8,128)(2,1)} %slice.439), channel_id=1, source_target_pairs={{0,1},{1,0},{2,3},{3,2},{4,5},{5,4},{6,7},{7,6},{8,9},{9,8},{10,11... | collective-permute-start | bytes 6291464 | tf_op jit(solution)/shard_map/ppermute | solution.py:438
  435.3 33.8 %collective-permute-start.68 = (bf16[512,1536]{1,0:T(8,128)(2,1)}, bf16[512,1536]{1,0:T(8,128)(2,1)}, u32[]{:S(2)}, u32[]{:S(2)}) collective-permute-start(bf16[512,1536]{1,0:T(8,128)(2,1)} %constant_dynamic-update-slice_fusion.18), channel_id=1, source_target_pairs={{0,1},{1,0},{2,3},{3,2},{4,5},{5,4},{6,7},{7,6},{8,9},{9,8},{10,11... | collective-permute-start | bytes 4718600 | tf_op jit(solution)/shard_map/ppermute | solution.py:438
  445.6 54.3 %collective-permute-start.81 = (bf16[2,1024,256]{2,1,0:T(8,128)(2,1)}, bf16[2,1024,256]{2,1,0:T(8,128)(2,1)}, u32[]{:S(2)}, u32[]{:S(2)}) collective-permute-start(bf16[2,1024,256]{2,1,0:T(8,128)(2,1)} %add_convert_fusion.3), channel_id=1, source_target_pairs={{0,8},{4,12},{8,0},{12,4},{16,24},{20,28},{24,16},{28,20},{1,9},{5... | collective-permute-start | bytes 3145736 | tf_op jit(solution)/shard_map/ppermute | solution.py:542
  457.8 42.1 %collective-permute-start.77 = (bf16[128,2048]{1,0:T(8,128)(2,1)}, bf16[128,2048]{1,0:T(8,128)(2,1)}, u32[]{:S(2)}, u32[]{:S(2)}) collective-permute-start(bf16[128,2048]{1,0:T(8,128)(2,1)} %fusion.23), channel_id=1, source_target_pairs={{0,2},{1,3},{2,0},{3,1},{4,6},{5,7},{6,4},{7,5},{8,10},{9,11},{10,... | collective-permute-start | bytes 1572872 | tf_op jit(solution)/shard_map/ppermute | solution.py:438
  467.3 78.2 %collective-permute-start.85 = (bf16[4,1536,256]{2,1,0:T(8,128)(2,1)}, bf16[4,1536,256]{2,1,0:T(8,128)(2,1)}, u32[]{:S(2)}, u32[]{:S(2)}) collective-permute-start(bf16[4,1536,256]{2,1,0:T(8,128)(2,1)} %shard_map.327), channel_id=1, source_target_pairs={{0,4},{4,0},{8,12},{12,8},{16,20},{20,16},{24,28},{28,24},{1,5},{5... | collective-permute-start | bytes 9437192 | tf_op jit(solution)/shard_map/ppermute | solution.py:542
  481.3 37.4 %collective-permute-start.75 = (bf16[4,512,256]{2,1,0:T(8,128)(2,1)}, bf16[4,512,256]{2,1,0:T(8,128)(2,1)}, u32[]{:S(2)}, u32[]{:S(2)}) collective-permute-start(bf16[4,512,256]{2,1,0:T(8,128)(2,1)} %shard_map.321), channel_id=1, source_target_pairs={{0,8},{4,12},{8,0},{12,4},{16,24},{20,28},{24,16},{28,20},{1,9},{5... | collective-permute-start | bytes 3145736 | tf_op jit(solution)/shard_map/ppermute | solution.py:542
  548.5 68.1 %collective-permute-start.86 = (bf16[2,1536,256]{2,1,0:T(8,128)(2,1)}, bf16[2,1536,256]{2,1,0:T(8,128)(2,1)}, u32[]{:S(2)}, u32[]{:S(2)}) collective-permute-start(bf16[2,1536,256]{2,1,0:T(8,128)(2,1)} %add_convert_fusion.1), channel_id=1, source_target_pairs={{0,8},{4,12},{8,0},{12,4},{16,24},{20,28},{24,16},{28,20},{1,9},{5... | collective-permute-start | bytes 4718600 | tf_op jit(solution)/shard_map/ppermute | solution.py:542
  549.9 70.1 %collective-permute-start.84 = (bf16[4,1024,256]{2,1,0:T(8,128)(2,1)}, bf16[4,1024,256]{2,1,0:T(8,128)(2,1)}, u32[]{:S(2)}, u32[]{:S(2)}) collective-permute-start(bf16[4,1024,256]{2,1,0:T(8,128)(2,1)} %shard_map.320), channel_id=1, source_target_pairs={{0,4},{4,0},{8,12},{12,8},{16,20},{20,16},{24,28},{28,24},{1,5},{5... | collective-permute-start | bytes 6291464 | tf_op jit(solution)/shard_map/ppermute | solution.py:542
  552.2 73.1 %collective-permute-start.83 = (bf16[4,128,2048]{2,1,0:T(8,128)(2,1)}, bf16[4,128,2048]{2,1,0:T(8,128)(2,1)}, u32[]{:S(2)}, u32[]{:S(2)}) collective-permute-start(bf16[4,128,2048]{2,1,0:T(8,128)(2,1)} %slice.456), channel_id=1, source_target_pairs={{0,1},{1,0},{2,3},{3,2},{4,5},{5,4},{6,7},{7,6},{8,9},{9,8},{10,11... | collective-permute-start | bytes 6291464 | tf_op jit(solution)/shard_map/ppermute | solution.py:438
  552.2 62.5 %collective-permute-start.87 = (bf16[4,416,256]{2,1,0:T(8,128)(2,1)S(1)}, bf16[4,416,256]{2,1,0:T(8,128)(2,1)}, u32[]{:S(2)}, u32[]{:S(2)}) collective-permute-start(bf16[4,416,256]{2,1,0:T(8,128)(2,1)S(1)} %shard_map.329), channel_id=1, source_target_pairs={{0,8},{4,12},{8,0},{12,4},{16,24},{20,28},{24,16},{28,20},{1,9},{5... | collective-permute-start | bytes 2555912 | tf_op jit(solution)/shard_map/ppermute | solution.py:542
  552.9 69.8 %collective-permute-start.93 = (bf16[1024,256]{1,0:T(8,128)(2,1)}, bf16[1024,256]{1,0:T(8,128)(2,1)S(1)}, u32[]{:S(2)}, u32[]{:S(2)}) collective-permute-start(bf16[1024,256]{1,0:T(8,128)(2,1)} %fusion.41), channel_id=1, source_target_pairs={{0,16},{4,20},{8,24},{12,28},{16,0},{20,4},{24,8},{28,12},{1,17},{... | collective-permute-start | bytes 1572872 | tf_op jit(solution)/shard_map/ppermute | solution.py:542
  616.6 40.6 %collective-permute-start.91 = (bf16[2,416,256]{2,1,0:T(8,128)(2,1)S(1)}, bf16[2,416,256]{2,1,0:T(8,128)(2,1)S(1)}, u32[]{:S(2)}, u32[]{:S(2)}) collective-permute-start(bf16[2,416,256]{2,1,0:T(8,128)(2,1)S(1)} %add_convert_fusion.8), channel_id=1, source_target_pairs={{0,4},{4,0},{8,12},{12,8},{16,20},{20,16},{24,28},{28,24},{1,5},{5... | collective-permute-start | bytes 1277960 | tf_op jit(solution)/shard_map/ppermute | solution.py:542
  620.0 48.4 %collective-permute-start.100 = (bf16[1536,256]{1,0:T(8,128)(2,1)S(1)}, bf16[1536,256]{1,0:T(8,128)(2,1)S(1)}, u32[]{:S(2)}, u32[]{:S(2)}) collective-permute-start(bf16[1536,256]{1,0:T(8,128)(2,1)S(1)} %fusion.37), channel_id=1, source_target_pairs={{0,16},{4,20},{8,24},{12,28},{16,0},{20,4},{24,8},{28,12},{1,17},{... | collective-permute-start | bytes 2359304 | tf_op jit(solution)/shard_map/ppermute | solution.py:542
  622.7 44.3 %collective-permute-start.90 = (bf16[2,1024,256]{2,1,0:T(8,128)(2,1)S(1)}, bf16[2,1024,256]{2,1,0:T(8,128)(2,1)S(1)}, u32[]{:S(2)}, u32[]{:S(2)}) collective-permute-start(bf16[2,1024,256]{2,1,0:T(8,128)(2,1)S(1)} %add_convert_fusion.2), channel_id=1, source_target_pairs={{0,8},{4,12},{8,0},{12,4},{16,24},{20,28},{24,16},{28,20},{1,9},{5... | collective-permute-start | bytes 3145736 | tf_op jit(solution)/shard_map/ppermute | solution.py:542
  655.7 84.7 %collective-permute-start.102 = (bf16[128,2048]{1,0:T(8,128)(2,1)S(1)}, bf16[128,2048]{1,0:T(8,128)(2,1)S(1)}, u32[]{:S(2)}, u32[]{:S(2)}) collective-permute-start(bf16[128,2048]{1,0:T(8,128)(2,1)S(1)} %pad_maximum_fusion.14), channel_id=1, source_target_pairs={{0,4},{4,0},{8,12},{12,8},{16,20},{20,16},{24,28},{28,24},{1,5},{5... | collective-permute-start | bytes 1572872 | tf_op jit(solution)/shard_map/ppermute | solution.py:441
  657.2 41.5 %collective-permute-start.89 = (bf16[128,2048]{1,0:T(8,128)(2,1)S(1)}, bf16[128,2048]{1,0:T(8,128)(2,1)S(1)}, u32[]{:S(2)}, u32[]{:S(2)}) collective-permute-start(bf16[128,2048]{1,0:T(8,128)(2,1)S(1)} %pad_maximum_fusion.13), channel_id=1, source_target_pairs={{0,2},{1,3},{2,0},{3,1},{4,6},{5,7},{6,4},{7,5},{8,10},{9,11},{10,... | collective-permute-start | bytes 1572872 | tf_op jit(solution)/shard_map/ppermute | solution.py:438
  668.3 29.0 %collective-permute-start.98 = (bf16[1024,256]{1,0:T(8,128)(2,1)S(1)}, bf16[1024,256]{1,0:T(8,128)(2,1)S(1)}, u32[]{:S(2)}, u32[]{:S(2)}) collective-permute-start(bf16[1024,256]{1,0:T(8,128)(2,1)S(1)} %fusion.42), channel_id=1, source_target_pairs={{0,16},{4,20},{8,24},{12,28},{16,0},{20,4},{24,8},{28,12},{1,17},{... | collective-permute-start | bytes 1572872 | tf_op jit(solution)/shard_map/ppermute | solution.py:542
  690.8 44.7 %collective-permute-start.103 = (bf16[3,512,256]{2,1,0:T(8,128)(2,1)S(1)}, bf16[3,512,256]{2,1,0:T(8,128)(2,1)S(1)}, u32[]{:S(2)}, u32[]{:S(2)}) collective-permute-start(bf16[3,512,256]{2,1,0:T(8,128)(2,1)S(1)} %pad_maximum_fusion.8), channel_id=1, source_target_pairs={{0,0},{1,8},{2,16},{3,24},{4,4},{5,12},{6,20},{7,28},{8,1},{9,9},{... | collective-permute-start | bytes 2359304 | tf_op jit(solution)/shard_map/ppermute | solution.py:592
  (221 other events, 2652.6 us)
Sparse Core Ops, SparseCore 0:
  323.1 143.3 reduce-scatter.1

commit v5 on v4

--- a/solution.py
+++ b/solution.py
@@ -811,15 +811,15 @@
         sum_patch = Sum(place, (("rows", patch_turned, grad_context_all),), (1, 0, 2))
         sum_patch.send()
         kept = sum_patch.keep(sum_patch.sent)
-        out_part = low(nn(after(hidden, kept), down_half))
+        patch_one = sum_patch.add(1, kept)
+        context_one = sum_context.add(1, patch_one)
+        out_part = low(nn(after(hidden, context_one), down_half))
         sums = plane_core(out_part)
-        patches_grad = nt(after(grad_context, kept), patch_mat)[None]
-        context_one = sum_context.add(1, kept, out_part, patches_grad)
-        patch_one = sum_patch.add(1, context_one)
-        step = sum_context.add(2, patch_one)
+        patches_grad = nt(after(grad_context, context_one), patch_mat)[None]
+        step = sum_cross.add(3, out_part, patches_grad)
+        step = sum_context.add(2, step)
         step = sum_self.add(1, step)
         own, chip, side = plane_far(after(tuple(sums), step))
-        step = sum_cross.add(3, step)
         step = sum_value.add(2, step)
         gains = gains + after(hop(after(gains, step), 0), chip, side)
         gains = gains + after(swap(gains, 2), chip)

time: 758 us -> 736 us (0.971)
  local copies, waits for them, and re-layouts: 74.7 us -> 56.8 us
    ppermute x71, waiting for transfers between devices: 137 us -> 149 us  [swap(): return lax.ppermute(values, 'fsdp', [(i, i ^ r) for i in range(fsdp)])]
    unnamed x310 -> x298, local copies, waits for them, and re-layouts: 37.4 us -> 26.1 us
    ppermute x20, waiting for transfers between devices: 89.6 us -> 78.5 us  [hop(): return lax.ppermute(values, 'dp', [(i, i ^ 1 << bit) for i in range(dp)])]
    ppermute x13, waiting for transfers between devices: 43 us -> 35.4 us  [across(): return lax.ppermute(values, 'dp', [(i, i ^ 1) for i in range(dp)])]
  transfers between devices with their start and end apart: 106 -> 106, of which waited for: 42 -> 46; matrix products, arithmetic and copies ran while one was open for 23% -> 21% of each run, Pallas kernels for 19% -> 20%
where the time goes in v5:
time: 736 us; the launch traced here: 728 us
  waiting for transfers between devices  296 us (40%)
  Pallas kernels  145 us (20%)
  starting transfers between devices  86.5 us (12%)
  other arithmetic  79.4 us (11%)
  local copies, waits for them, and re-layouts  56.8 us (8%)
  matrix products  46 us (6%)
  between operations  18.5 us (3%)
    ppermute x71, waiting for transfers between devices, swap(): return lax.ppermute(values, 'fsdp', [(i, i ^ r) for i in range(fsdp)])  149 us
    ppermute x20, waiting for transfers between devices, hop(): return lax.ppermute(values, 'dp', [(i, i ^ 1 << bit) for i in range(dp)])  78.5 us
    pallas_call x10, Pallas kernels, half_grads(): pl.pallas_call(half_kernel, out_shape=jax.ShapeDtypeStruct((4, rows, wide...  48.9 us
    dot_general x12, matrix products, dot(): lax.dot_general(left, right, (((left_dim,), (right_dim,)), ((), ())), pre...  46 us
    ppermute x13, waiting for transfers between devices, across(): return lax.ppermute(values, 'dp', [(i, i ^ 1) for i in range(dp)])  35.4 us
    ppermute x71, starting transfers between devices, swap(): return lax.ppermute(values, 'fsdp', [(i, i ^ r) for i in range(fsdp)])  35 us
    ppermute x1, waiting for transfers between devices, place_columns(): return lax.ppermute(values, ('dp', 'fsdp'), pairs)  33.3 us
    ppermute x20, starting transfers between devices, hop(): return lax.ppermute(values, 'dp', [(i, i ^ 1 << bit) for i in range(dp)])  30.4 us
  transfers between devices with their start and end apart: 106, of which 46 were waited for; matrix products, arithmetic and copies ran while one was open for 21% of the time, Pallas kernels for 20%

profile of v5, /device:TPU:4, one launch (start us, length us, event | category | flops | bytes accessed | tf_op | source)
XLA Modules:
  0.0 728.5 jit_solution(8255746379099668836)
XLA Ops:
  20.8 21.1 %collective-permute-done.5 = bf16[2,2,256,512]{3,2,0,1:T(8,128)(2,1)S(1)} collective-permute-done((bf16[2,2,256,512]{3,2,0,1:T(8,128)(2,1)S(1)}, bf16[2,2,256,512]{3,2,0,1:T(8,128)(2,1)S(1)}, u32[]{:S(2)}, u32[]{:S(2)}) %collective-permute-start.5) | collective-permute-done | bytes 1048608 | tf_op jit(solution)/shard_map/ppermute | solution.py:438
  47.0 6.2 collective-permute-done.11.refs_6_.refs_17_
  53.2 9.1 %collective-permute-done.15 = bf16[104,2048]{1,0:T(8,128)(2,1)S(1)} collective-permute-done((bf16[104,2048]{1,0:T(8,128)(2,1)S(1)}, bf16[104,2048]{1,0:T(8,128)(2,1)S(1)}, u32[]{:S(2)}, u32[]{:S(2)}) %collective-permute-start.15) | collective-permute-done | bytes 426016 | tf_op jit(solution)/shard_map/ppermute | solution.py:438
  82.8 9.6 %collective-permute-done.16 = bf16[3,2,128,512]{3,2,0,1:T(8,128)(2,1)S(1)} collective-permute-done((bf16[3,2,128,512]{3,2,0,1:T(8,128)(2,1)S(1)}, bf16[3,2,128,512]{3,2,0,1:T(8,128)(2,1)S(1)}, u32[]{:S(2)}, u32[]{:S(2)}) %collective-permute-start.16) | collective-permute-done | bytes 786464 | tf_op jit(solution)/shard_map/ppermute | solution.py:438
  104.0 6.4 shard_map.300.refs_0_
  131.2 7.3 collective-permute-done.20
  141.6 6.1 convolution_convert_fusion.3.refs_0_
  148.6 7.9 %collective-permute-done.23 = bf16[3,2,256,512]{3,2,0,1:T(8,128)(2,1)S(1)} collective-permute-done((bf16[3,2,256,512]{3,2,0,1:T(8,128)(2,1)S(1)}, bf16[3,2,256,512]{3,2,0,1:T(8,128)(2,1)S(1)}, u32[]{:S(2)}, u32[]{:S(2)}) %collective-permute-start.23) | collective-permute-done | bytes 1572896 | tf_op jit(solution)/shard_map/ppermute | solution.py:441
  164.8 11.8 %collective-permute-done.32.refs_2_ = bf16[256,2048]{1,0:T(8,128)(2,1)} collective-permute-done((bf16[256,2048]{1,0:T(8,128)(2,1)}, bf16[256,2048]{1,0:T(8,128)(2,1)}, u32[]{:S(2)}, u32[]{:S(2)}) %collective-permute-start.32) | collective-permute-done | bytes 1048608 | tf_op jit(solution)/shard_map/ppermute | solution.py:438
  191.7 5.5 shard_map.303.k_ref
  213.4 12.8 %collective-permute-done.37 = bf16[128,2048]{1,0:T(8,128)(2,1)S(1)} collective-permute-done((bf16[128,2048]{1,0:T(8,128)(2,1)S(1)}, bf16[128,2048]{1,0:T(8,128)(2,1)S(1)}, u32[]{:S(2)}, u32[]{:S(2)}) %collective-permute-start.37) | collective-permute-done | bytes 524320 | tf_op jit(solution)/shard_map/ppermute | solution.py:438
  235.3 7.5 %collective-permute-done.47 = bf16[128,2048]{1,0:T(8,128)(2,1)S(1)} collective-permute-done((bf16[128,2048]{1,0:T(8,128)(2,1)S(1)}, bf16[128,2048]{1,0:T(8,128)(2,1)S(1)}, u32[]{:S(2)}, u32[]{:S(2)}) %collective-permute-start.47) | collective-permute-done | bytes 524320 | tf_op jit(solution)/shard_map/ppermute | solution.py:441
  260.4 7.1 fusion.9
  295.3 13.1 %shard_map.309 = bf16[4,1920,512]{2,1,0:T(8,128)(2,1)} custom-call(s32[2]{0:T(128)S(1)} %broadcast_6_place.2.place, bf16[640,1024]{1,0:T(8,128)(2,1)S(1)} %shard_map.306.refs_0_, bf16[1024,2048]{1,0:T(8,128)(2,1)} %copy-done.126, bf16[640,1024]{1,0:T(8,128)(2,1)S(1)} %shard_map.307.refs_2_, bf16[1024,2048]{1,0:T(8,128)(2,1)} %copy-done.126, ...), custom_call_target="tpu_custom_call" | custom-call | flops 14400000000 | bytes 36000000 | tf_op jit(solution)/shard_map/pallas_call | solution.py:407
  315.9 10.1 %collective-permute-done.61 = bf16[128,2048]{1,0:T(8,128)(2,1)S(1)} collective-permute-done((bf16[128,2048]{1,0:T(8,128)(2,1)S(1)}, bf16[128,2048]{1,0:T(8,128)(2,1)S(1)}, u32[]{:S(2)}, u32[]{:S(2)}) %collective-permute-start.61) | collective-permute-done | bytes 524320 | tf_op jit(solution)/shard_map/ppermute | solution.py:438
  329.2 8.1 %shard_map.312 = (bf16[512,512]{1,0:T(8,128)(2,1)S(1)}, bf16[1024,512]{1,0:T(8,128)(2,1)S(1)}, bf16[1024,512]{1,0:T(8,128)(2,1)S(1)}) custom-call(s32[4,2]{1,0:T(4,128)S(1)} %pad_add_fusion.info, bf16[512,512]{1,0:T(8,128)(2,1)S(1)} %copy-done.36, bf16[1024,512]{1,0:T(8,128)(2,1)S(1)} %copy-done.64, bf16[1024,512]{1,0:T(8,128)(2,1)S(1)} %copy-done.62, ...), custom_call_target="tpu_custom_call" | custom-call | flops 6400000000 | bytes 16000000 | tf_op jit(solution)/shard_map/pallas_call | solution.py:129
  374.4 5.8 collective-permute-done.66
  383.5 7.8 %shard_map.319 = (bf16[512,512]{1,0:T(8,128)(2,1)S(1)}, bf16[512,512]{1,0:T(8,128)(2,1)S(1)}, bf16[512,512]{1,0:T(8,128)(2,1)S(1)}) custom-call(s32[4,2]{1,0:T(4,128)S(1)} %pad_add_fusion.info, bf16[512,512]{1,0:T(8,128)(2,1)S(1)} %copy-done.27, bf16[512,512]{1,0:T(8,128)(2,1)S(1)} %copy-done.25, bf16[512,512]{1,0:T(8,128)(2,1)S(1)} %copy-done.58, ...), custom_call_target="tpu_custom_call" | custom-call | flops 6400000000 | bytes 16000000 | tf_op jit(solution)/shard_map/pallas_call | solution.py:129
  393.7 8.9 %shard_map.325 = bf16[512,2048]{1,0:T(8,128)(2,1)} custom-call(s32[2]{0:T(128)} %copy-done.46, bf16[512,512]{1,0:T(8,128)(2,1)} %copy-done.41, bf16[512,512]{1,0:T(8,128)(2,1)} %copy-done.39, bf16[512,512]{1,0:T(8,128)(2,1)} %copy-done.37, bf16[512,2048]{1,0:T(8,128)(2,1)} %refs_3_, bf16[3,512,512]{2,1,0:T(8,128)(2,1)} %copy-done.6, ...), custom_call_target="tpu_custom_call" | custom-call | flops 7742608896 | bytes 19356520 | tf_op jit(solution)/shard_map/pallas_call | solution.py:247
  406.1 10.5 %shard_map.326 = bf16[1024,2048]{1,0:T(8,128)(2,1)} custom-call(s32[2]{0:T(128)} %copy-done.46, bf16[1024,512]{1,0:T(8,128)(2,1)} %copy-done.70, bf16[1024,512]{1,0:T(8,128)(2,1)} %copy-done.72, bf16[512,2048]{1,0:T(8,128)(2,1)} %refs_2_.1, bf16[3,512,512]{2,1,0:T(8,128)(2,1)} %copy-done.19, bf16[3,2,256,512]{3,2,1,0:T(8,128)(2,1)} %copy.38.refs_6_.refs_3_.refs_4_.refs_10_, ...), custom_call_target="tpu_custom_call" | custom-call | flops 9523478528 | bytes 23808696 | tf_op jit(solution)/shard_map/pallas_call | solution.py:247
  420.8 7.8 %collective-permute-done.79 = bf16[4,1024,256]{2,1,0:T(8,128)(2,1)} collective-permute-done((bf16[4,1024,256]{2,1,0:T(8,128)(2,1)}, bf16[4,1024,256]{2,1,0:T(8,128)(2,1)}, u32[]{:S(2)}, u32[]{:S(2)}) %collective-permute-start.79) | collective-permute-done | bytes 2097184 | tf_op jit(solution)/shard_map/ppermute | solution.py:542
  431.8 10.0 %collective-permute-done.69 = bf16[512,1536]{1,0:T(8,128)(2,1)} collective-permute-done((bf16[512,1536]{1,0:T(8,128)(2,1)}, bf16[512,1536]{1,0:T(8,128)(2,1)}, u32[]{:S(2)}, u32[]{:S(2)}) %collective-permute-start.69) | collective-permute-done | bytes 1572896 | tf_op jit(solution)/shard_map/ppermute | solution.py:438
  444.2 8.5 %shard_map.323 = bf16[4,1536,256]{2,1,0:T(8,128)(2,1)} custom-call(s32[2]{0:T(128)S(1)} %copy-done.48, bf16[2048,1024]{1,0:T(8,128)(2,1)} %copy-done.59, bf16[1024,512]{1,0:T(8,128)(2,1)S(1)} %copy-done.71, bf16[2048,1024]{1,0:T(8,128)(2,1)} %copy-done.59, bf16[1024,512]{1,0:T(8,128)(2,1)S(1)} %copy-done.73, bf16[512,512]{1,0:T(8,128)(2,1)S(1)} %copy-done.79, ...), custom_call_target="tpu_custom_call" | custom-call | flops 5851428352 | bytes 14628571 | tf_op jit(solution)/shard_map/pallas_call | solution.py:313
  455.6 6.5 pad_maximum_fusion.refs_1_.refs_3_
  472.2 8.5 %shard_map.322 = bf16[4,1536,256]{2,1,0:T(8,128)(2,1)} custom-call(s32[2]{0:T(128)S(1)} %copy-done.48, bf16[2048,1024]{1,0:T(8,128)(2,1)} %copy-done.59, bf16[1024,512]{1,0:T(8,128)(2,1)S(1)} %copy-done.71, bf16[2048,1024]{1,0:T(8,128)(2,1)} %copy-done.59, bf16[1024,512]{1,0:T(8,128)(2,1)S(1)} %copy-done.73, bf16[512,512]{1,0:T(8,128)(2,1)S(1)} %copy-done.79, ...), custom_call_target="tpu_custom_call" | custom-call | flops 5851428352 | bytes 14628571 | tf_op jit(solution)/shard_map/pallas_call | solution.py:313
  521.6 16.3 %collective-permute-done.84 = bf16[4,416,256]{2,1,0:T(8,128)(2,1)S(1)} collective-permute-done((bf16[4,416,256]{2,1,0:T(8,128)(2,1)S(1)}, bf16[4,416,256]{2,1,0:T(8,128)(2,1)S(1)}, u32[]{:S(2)}, u32[]{:S(2)}) %collective-permute-start.84) | collective-permute-done | bytes 852000 | tf_op jit(solution)/shard_map/ppermute | solution.py:542
  543.4 5.7 convolution_convert_fusion
  554.9 6.6 convolution_bitcast_fusion
  561.5 26.6 %collective-permute-done.88 = bf16[1024,256]{1,0:T(8,128)(2,1)S(1)} collective-permute-done((bf16[1024,256]{1,0:T(8,128)(2,1)S(1)}, bf16[1024,256]{1,0:T(8,128)(2,1)S(1)}, u32[]{:S(2)}, u32[]{:S(2)}) %collective-permute-start.88) | collective-permute-done | bytes 524320 | tf_op jit(solution)/shard_map/ppermute | solution.py:542
  624.1 21.9 %collective-permute-done.91 = bf16[2,1024,256]{2,1,0:T(8,128)(2,1)S(1)} collective-permute-done((bf16[2,1024,256]{2,1,0:T(8,128)(2,1)S(1)}, bf16[2,1024,256]{2,1,0:T(8,128)(2,1)S(1)}, u32[]{:S(2)}, u32[]{:S(2)}) %collective-permute-start.91) | collective-permute-done | bytes 1048608 | tf_op jit(solution)/shard_map/ppermute | solution.py:542
  654.1 14.8 %collective-permute-done.101 = bf16[1920,256]{1,0:T(8,128)(2,1)S(1)} collective-permute-done((bf16[1920,256]{1,0:T(8,128)(2,1)S(1)}, bf16[1920,256]{1,0:T(8,128)(2,1)S(1)}, u32[]{:S(2)}, u32[]{:S(2)}) %collective-permute-start.101) | collective-permute-done | bytes 983072 | tf_op jit(solution)/shard_map/ppermute | solution.py:441
  680.7 33.3 %collective-permute-done.103 = bf16[3,512,256]{2,1,0:T(8,128)(2,1)S(1)} collective-permute-done((bf16[3,512,256]{2,1,0:T(8,128)(2,1)S(1)}, bf16[3,512,256]{2,1,0:T(8,128)(2,1)S(1)}, u32[]{:S(2)}, u32[]{:S(2)}) %collective-permute-start.103) | collective-permute-done | bytes 786464 | tf_op jit(solution)/shard_map/ppermute | solution.py:592
  (668 shorter events, 361.2 us)
Async XLA Ops:
  7.2 478.0 %reduce-scatter.2.cloned.1.call-start = ((), (), s32[]{:S(2)}) async-start(), calls=%async_computation.1 | async-start | bytes 9830400 | tf_op jit(solution)/shard_map/reduce_scatter | solution.py:722
  8.7 37.4 %collective-permute-start.1 = (s32[1,2]{1,0:T(1,128)S(1)}, s32[1,2]{1,0:T(1,128)S(1)}, u32[]{:S(2)}, u32[]{:S(2)}) collective-permute-start(s32[1,2]{1,0:T(1,128)S(1)} %pad_add_fusion.1), channel_id=1, source_target_pairs={{0,1},{1,0},{2,3},{3,2},{4,5},{5,4},{6,7},{7,6},{8,9},{9,8},{10,11... | collective-permute-start | bytes 32 | tf_op jit(solution)/shard_map/ppermute | solution.py:438
  12.4 34.5 %collective-permute-start.2 = (s32[1,2]{1,0:T(1,128)S(1)}, s32[1,2]{1,0:T(1,128)S(1)}, u32[]{:S(2)}, u32[]{:S(2)}) collective-permute-start(s32[1,2]{1,0:T(1,128)S(1)} %collective-permute-done), channel_id=1, source_target_pairs={{0,1},{1,0},{2,3},{3,2},{4,5},{5,4},{6,7},{7,6},{8,9},{9,8},{10,11... | collective-permute-start | bytes 32 | tf_op jit(solution)/shard_map/ppermute | solution.py:438
  17.4 35.8 %collective-permute-start.11 = (bf16[1,2,256,512]{3,2,1,0:T(8,128)(2,1)S(1)}, bf16[1,2,256,512]{3,2,1,0:T(8,128)(2,1)S(1)}, u32[]{:S(2)}, u32[]{:S(2)}) collective-permute-start(bf16[1,2,256,512]{3,2,1,0:T(8,128)(2,1)S(1)} %maximum_bitcast_fusion.2), channel_id=1, source_target_pairs={{0,2},{1,3},{2,0},{3,1},{4,6},{5,7},{6,4},{7,5},{8,10},{9,11},{10,... | collective-permute-start | bytes 1572872 | tf_op jit(solution)/shard_map/ppermute | solution.py:438
  46.9 27.5 %collective-permute-start.3 = (bf16[128,2048]{1,0:T(8,128)(2,1)S(1)}, bf16[128,2048]{1,0:T(8,128)(2,1)S(1)}, u32[]{:S(2)}, u32[]{:S(2)}) collective-permute-start(bf16[128,2048]{1,0:T(8,128)(2,1)S(1)} %multiply_convert_fusion.5.refs_0_), channel_id=1, source_target_pairs={{0,1},{1,0},{2,3},{3,2},{4,5},{5,4},{6,7},{7,6},{8,9},{9,8},{10,11... | collective-permute-start | bytes 1572872 | tf_op jit(solution)/shard_map/ppermute | solution.py:438
  53.2 28.2 %collective-permute-start.8 = (bf16[3,512,512]{2,1,0:T(8,128)(2,1)S(1)}, bf16[3,512,512]{2,1,0:T(8,128)(2,1)S(1)}, u32[]{:S(2)}, u32[]{:S(2)}) collective-permute-start(bf16[3,512,512]{2,1,0:T(8,128)(2,1)S(1)} %pad_maximum_fusion.4), channel_id=1, source_target_pairs={{0,1},{1,0},{2,3},{3,2},{4,5},{5,4},{6,7},{7,6},{8,9},{9,8},{10,11... | collective-permute-start | bytes 4718600 | tf_op jit(solution)/shard_map/ppermute | solution.py:438
  81.3 35.5 %collective-permute-start.29 = (bf16[208,2048]{1,0:T(8,128)(2,1)}, bf16[208,2048]{1,0:T(8,128)(2,1)}, u32[]{:S(2)}, u32[]{:S(2)}) collective-permute-start(bf16[208,2048]{1,0:T(8,128)(2,1)} %maximum_select_fusion.2), channel_id=1, source_target_pairs={{0,4},{4,0},{8,12},{12,8},{16,20},{20,16},{24,28},{28,24},{1,5},{5... | collective-permute-start | bytes 2555912 | tf_op jit(solution)/shard_map/ppermute | solution.py:441
  120.1 36.4 %collective-permute-start.23 = (bf16[3,2,256,512]{3,2,0,1:T(8,128)(2,1)S(1)}, bf16[3,2,256,512]{3,2,0,1:T(8,128)(2,1)S(1)}, u32[]{:S(2)}, u32[]{:S(2)}) collective-permute-start(bf16[3,2,256,512]{3,2,0,1:T(8,128)(2,1)S(1)} %copy-done.89), channel_id=1, source_target_pairs={{0,4},{4,0},{8,12},{12,8},{16,20},{20,16},{24,28},{28,24},{1,5},{5... | collective-permute-start | bytes 4718600 | tf_op jit(solution)/shard_map/ppermute | solution.py:441
  122.5 34.6 %collective-permute-start.26 = (bf16[3,256,512]{2,1,0:T(8,128)(2,1)}, bf16[3,256,512]{2,1,0:T(8,128)(2,1)S(1)}, u32[]{:S(2)}, u32[]{:S(2)}) collective-permute-start(bf16[3,256,512]{2,1,0:T(8,128)(2,1)} %slice_bitcast_fusion.2), channel_id=1, source_target_pairs={{0,1},{1,0},{2,3},{3,2},{4,5},{5,4},{6,7},{7,6},{8,9},{9,8},{10,11... | collective-permute-start | bytes 2359304 | tf_op jit(solution)/shard_map/ppermute | solution.py:438
  129.8 30.6 %collective-permute-start.25 = (bf16[3,512,512]{2,1,0:T(8,128)(2,1)}, bf16[3,512,512]{2,1,0:T(8,128)(2,1)S(1)}, u32[]{:S(2)}, u32[]{:S(2)}) collective-permute-start(bf16[3,512,512]{2,1,0:T(8,128)(2,1)} %pad_maximum_fusion.5), channel_id=1, source_target_pairs={{0,1},{1,0},{2,3},{3,2},{4,5},{5,4},{6,7},{7,6},{8,9},{9,8},{10,11... | collective-permute-start | bytes 4718600 | tf_op jit(solution)/shard_map/ppermute | solution.py:438
  147.7 28.9 %collective-permute-start.32 = (bf16[256,2048]{1,0:T(8,128)(2,1)}, bf16[256,2048]{1,0:T(8,128)(2,1)}, u32[]{:S(2)}, u32[]{:S(2)}) collective-permute-start(bf16[256,2048]{1,0:T(8,128)(2,1)} %convolution_convert_fusion.3.refs_0_), channel_id=1, source_target_pairs={{0,2},{1,3},{2,0},{3,1},{4,6},{5,7},{6,4},{7,5},{8,10},{9,11},{10,... | collective-permute-start | bytes 3145736 | tf_op jit(solution)/shard_map/ppermute | solution.py:438
  380.2 48.4 %collective-permute-start.79 = (bf16[4,1024,256]{2,1,0:T(8,128)(2,1)}, bf16[4,1024,256]{2,1,0:T(8,128)(2,1)}, u32[]{:S(2)}, u32[]{:S(2)}) collective-permute-start(bf16[4,1024,256]{2,1,0:T(8,128)(2,1)} %shard_map.315), channel_id=1, source_target_pairs={{0,4},{4,0},{8,12},{12,8},{16,20},{20,16},{24,28},{28,24},{1,5},{5... | collective-permute-start | bytes 6291464 | tf_op jit(solution)/shard_map/ppermute | solution.py:542
  405.0 36.8 %collective-permute-start.69 = (bf16[512,1536]{1,0:T(8,128)(2,1)}, bf16[512,1536]{1,0:T(8,128)(2,1)}, u32[]{:S(2)}, u32[]{:S(2)}) collective-permute-start(bf16[512,1536]{1,0:T(8,128)(2,1)} %constant_dynamic-update-slice_fusion.18), channel_id=1, source_target_pairs={{0,2},{1,3},{2,0},{3,1},{4,6},{5,7},{6,4},{7,5},{8,10},{9,11},{10,... | collective-permute-start | bytes 4718600 | tf_op jit(solution)/shard_map/ppermute | solution.py:438
  420.0 32.7 %collective-permute-start.72 = (bf16[2,256,2048]{2,1,0:T(8,128)(2,1)}, bf16[2,256,2048]{2,1,0:T(8,128)(2,1)S(1)}, u32[]{:S(2)}, u32[]{:S(2)}) collective-permute-start(bf16[2,256,2048]{2,1,0:T(8,128)(2,1)} %slice.440), channel_id=1, source_target_pairs={{0,1},{1,0},{2,3},{3,2},{4,5},{5,4},{6,7},{7,6},{8,9},{9,8},{10,11... | collective-permute-start | bytes 6291464 | tf_op jit(solution)/shard_map/ppermute | solution.py:438
  420.7 33.7 %collective-permute-start.68 = (bf16[512,1536]{1,0:T(8,128)(2,1)}, bf16[512,1536]{1,0:T(8,128)(2,1)}, u32[]{:S(2)}, u32[]{:S(2)}) collective-permute-start(bf16[512,1536]{1,0:T(8,128)(2,1)} %constant_dynamic-update-slice_fusion.18), channel_id=1, source_target_pairs={{0,1},{1,0},{2,3},{3,2},{4,5},{5,4},{6,7},{7,6},{8,9},{9,8},{10,11... | collective-permute-start | bytes 4718600 | tf_op jit(solution)/shard_map/ppermute | solution.py:438
  431.0 54.1 %collective-permute-start.82 = (bf16[2,1024,256]{2,1,0:T(8,128)(2,1)}, bf16[2,1024,256]{2,1,0:T(8,128)(2,1)}, u32[]{:S(2)}, u32[]{:S(2)}) collective-permute-start(bf16[2,1024,256]{2,1,0:T(8,128)(2,1)} %add_convert_fusion.3), channel_id=1, source_target_pairs={{0,8},{4,12},{8,0},{12,4},{16,24},{20,28},{24,16},{28,20},{1,9},{5... | collective-permute-start | bytes 3145736 | tf_op jit(solution)/shard_map/ppermute | solution.py:542
  443.1 42.0 %collective-permute-start.78 = (bf16[128,2048]{1,0:T(8,128)(2,1)}, bf16[128,2048]{1,0:T(8,128)(2,1)}, u32[]{:S(2)}, u32[]{:S(2)}) collective-permute-start(bf16[128,2048]{1,0:T(8,128)(2,1)} %fusion.23), channel_id=1, source_target_pairs={{0,2},{1,3},{2,0},{3,1},{4,6},{5,7},{6,4},{7,5},{8,10},{9,11},{10,... | collective-permute-start | bytes 1572872 | tf_op jit(solution)/shard_map/ppermute | solution.py:438
  452.7 86.2 %collective-permute-start.71 = (bf16[4,1536,256]{2,1,0:T(8,128)(2,1)}, bf16[4,1536,256]{2,1,0:T(8,128)(2,1)}, u32[]{:S(2)}, u32[]{:S(2)}) collective-permute-start(bf16[4,1536,256]{2,1,0:T(8,128)(2,1)} %shard_map.323), channel_id=1, source_target_pairs={{0,4},{4,0},{8,12},{12,8},{16,20},{20,16},{24,28},{28,24},{1,5},{5... | collective-permute-start | bytes 9437192 | tf_op jit(solution)/shard_map/ppermute | solution.py:542
  466.6 37.3 %collective-permute-start.76 = (bf16[4,512,256]{2,1,0:T(8,128)(2,1)}, bf16[4,512,256]{2,1,0:T(8,128)(2,1)}, u32[]{:S(2)}, u32[]{:S(2)}) collective-permute-start(bf16[4,512,256]{2,1,0:T(8,128)(2,1)} %shard_map.321), channel_id=1, source_target_pairs={{0,8},{4,12},{8,0},{12,4},{16,24},{20,28},{24,16},{28,20},{1,9},{5... | collective-permute-start | bytes 3145736 | tf_op jit(solution)/shard_map/ppermute | solution.py:542
  518.3 73.3 %collective-permute-start.86 = (bf16[4,1024,256]{2,1,0:T(8,128)(2,1)}, bf16[4,1024,256]{2,1,0:T(8,128)(2,1)}, u32[]{:S(2)}, u32[]{:S(2)}) collective-permute-start(bf16[4,1024,256]{2,1,0:T(8,128)(2,1)} %shard_map.320), channel_id=1, source_target_pairs={{0,4},{4,0},{8,12},{12,8},{16,20},{20,16},{24,28},{28,24},{1,5},{5... | collective-permute-start | bytes 6291464 | tf_op jit(solution)/shard_map/ppermute | solution.py:542
  542.0 47.7 %collective-permute-start.87 = (bf16[2,1536,256]{2,1,0:T(8,128)(2,1)}, bf16[2,1536,256]{2,1,0:T(8,128)(2,1)}, u32[]{:S(2)}, u32[]{:S(2)}) collective-permute-start(bf16[2,1536,256]{2,1,0:T(8,128)(2,1)} %add_convert_fusion.1), channel_id=1, source_target_pairs={{0,8},{4,12},{8,0},{12,4},{16,24},{20,28},{24,16},{28,20},{1,9},{5... | collective-permute-start | bytes 4718600 | tf_op jit(solution)/shard_map/ppermute | solution.py:542
  551.7 41.9 %collective-permute-start.85 = (bf16[4,128,2048]{2,1,0:T(8,128)(2,1)}, bf16[4,128,2048]{2,1,0:T(8,128)(2,1)}, u32[]{:S(2)}, u32[]{:S(2)}) collective-permute-start(bf16[4,128,2048]{2,1,0:T(8,128)(2,1)} %slice.460), channel_id=1, source_target_pairs={{0,1},{1,0},{2,3},{3,2},{4,5},{5,4},{6,7},{7,6},{8,9},{9,8},{10,11... | collective-permute-start | bytes 6291464 | tf_op jit(solution)/shard_map/ppermute | solution.py:438
  551.7 36.4 %collective-permute-start.88 = (bf16[1024,256]{1,0:T(8,128)(2,1)S(1)}, bf16[1024,256]{1,0:T(8,128)(2,1)S(1)}, u32[]{:S(2)}, u32[]{:S(2)}) collective-permute-start(bf16[1024,256]{1,0:T(8,128)(2,1)S(1)} %copy-done.116), channel_id=1, source_target_pairs={{0,16},{4,20},{8,24},{12,28},{16,0},{20,4},{24,8},{28,12},{1,17},{... | collective-permute-start | bytes 1572872 | tf_op jit(solution)/shard_map/ppermute | solution.py:542
  554.0 48.4 %collective-permute-start.93 = (bf16[2,512,256]{2,1,0:T(8,128)(2,1)S(1)}, bf16[2,512,256]{2,1,0:T(8,128)(2,1)S(1)}, u32[]{:S(2)}, u32[]{:S(2)}) collective-permute-start(bf16[2,512,256]{2,1,0:T(8,128)(2,1)S(1)} %add_convert_fusion.7), channel_id=1, source_target_pairs={{0,4},{4,0},{8,12},{12,8},{16,20},{20,16},{24,28},{28,24},{1,5},{5... | collective-permute-start | bytes 1572872 | tf_op jit(solution)/shard_map/ppermute | solution.py:542
  598.9 49.4 %collective-permute-start.100 = (bf16[1536,256]{1,0:T(8,128)(2,1)S(1)}, bf16[1536,256]{1,0:T(8,128)(2,1)S(1)}, u32[]{:S(2)}, u32[]{:S(2)}) collective-permute-start(bf16[1536,256]{1,0:T(8,128)(2,1)S(1)} %fusion.37), channel_id=1, source_target_pairs={{0,16},{4,20},{8,24},{12,28},{16,0},{20,4},{24,8},{28,12},{1,17},{... | collective-permute-start | bytes 2359304 | tf_op jit(solution)/shard_map/ppermute | solution.py:542
  602.3 43.7 %collective-permute-start.91 = (bf16[2,1024,256]{2,1,0:T(8,128)(2,1)S(1)}, bf16[2,1024,256]{2,1,0:T(8,128)(2,1)S(1)}, u32[]{:S(2)}, u32[]{:S(2)}) collective-permute-start(bf16[2,1024,256]{2,1,0:T(8,128)(2,1)S(1)} %add_convert_fusion.2), channel_id=1, source_target_pairs={{0,8},{4,12},{8,0},{12,4},{16,24},{20,28},{24,16},{28,20},{1,9},{5... | collective-permute-start | bytes 3145736 | tf_op jit(solution)/shard_map/ppermute | solution.py:542
  618.4 33.6 %collective-permute-start.99 = (bf16[512,256]{1,0:T(8,128)(2,1)S(1)}, bf16[512,256]{1,0:T(8,128)(2,1)S(1)}, u32[]{:S(2)}, u32[]{:S(2)}) collective-permute-start(bf16[512,256]{1,0:T(8,128)(2,1)S(1)} %fusion.46), channel_id=1, source_target_pairs={{0,16},{4,20},{8,24},{12,28},{16,0},{20,4},{24,8},{28,12},{1,17},{... | collective-permute-start | bytes 786440 | tf_op jit(solution)/shard_map/ppermute | solution.py:542
  621.7 97.1 %collective-permute-start.102 = (bf16[128,2048]{1,0:T(8,128)(2,1)S(1)}, bf16[128,2048]{1,0:T(8,128)(2,1)S(1)}, u32[]{:S(2)}, u32[]{:S(2)}) collective-permute-start(bf16[128,2048]{1,0:T(8,128)(2,1)S(1)} %pad_maximum_fusion.14), channel_id=1, source_target_pairs={{0,4},{4,0},{8,12},{12,8},{16,20},{20,16},{24,28},{28,24},{1,5},{5... | collective-permute-start | bytes 1572872 | tf_op jit(solution)/shard_map/ppermute | solution.py:441
  623.1 53.9 %collective-permute-start.90 = (bf16[128,2048]{1,0:T(8,128)(2,1)S(1)}, bf16[128,2048]{1,0:T(8,128)(2,1)S(1)}, u32[]{:S(2)}, u32[]{:S(2)}) collective-permute-start(bf16[128,2048]{1,0:T(8,128)(2,1)S(1)} %pad_maximum_fusion.13), channel_id=1, source_target_pairs={{0,2},{1,3},{2,0},{3,1},{4,6},{5,7},{6,4},{7,5},{8,10},{9,11},{10,... | collective-permute-start | bytes 1572872 | tf_op jit(solution)/shard_map/ppermute | solution.py:438
  647.3 28.3 %collective-permute-start.98 = (bf16[1024,256]{1,0:T(8,128)(2,1)S(1)}, bf16[1024,256]{1,0:T(8,128)(2,1)S(1)}, u32[]{:S(2)}, u32[]{:S(2)}) collective-permute-start(bf16[1024,256]{1,0:T(8,128)(2,1)S(1)} %fusion.42), channel_id=1, source_target_pairs={{0,16},{4,20},{8,24},{12,28},{16,0},{20,4},{24,8},{28,12},{1,17},{... | collective-permute-start | bytes 1572872 | tf_op jit(solution)/shard_map/ppermute | solution.py:542
  652.0 27.9 %collective-permute-start.104 = (bf16[416,256]{1,0:T(8,128)(2,1)S(1)}, bf16[416,256]{1,0:T(8,128)(2,1)S(1)}, u32[]{:S(2)}, u32[]{:S(2)}) collective-permute-start(bf16[416,256]{1,0:T(8,128)(2,1)S(1)} %fusion.48), channel_id=1, source_target_pairs={{0,16},{4,20},{8,24},{12,28},{16,0},{20,4},{24,8},{28,12},{1,17},{... | collective-permute-start | bytes 638984 | tf_op jit(solution)/shard_map/ppermute | solution.py:542
  668.9 45.1 %collective-permute-start.103 = (bf16[3,512,256]{2,1,0:T(8,128)(2,1)S(1)}, bf16[3,512,256]{2,1,0:T(8,128)(2,1)S(1)}, u32[]{:S(2)}, u32[]{:S(2)}) collective-permute-start(bf16[3,512,256]{2,1,0:T(8,128)(2,1)S(1)} %pad_maximum_fusion.8), channel_id=1, source_target_pairs={{0,0},{1,8},{2,16},{3,24},{4,4},{5,12},{6,20},{7,28},{8,1},{9,9},{... | collective-permute-start | bytes 2359304 | tf_op jit(solution)/shard_map/ppermute | solution.py:592
  (215 other events, 2476.4 us)
Sparse Core Ops, SparseCore 0:
  308.6 143.4 reduce-scatter.1
